TPU v7x, 256 devices: a whole 4x4x8 slice. The times are simulated.
256 devices in a mesh: dp: 4 (over z_lo), mrow: 16 (over z_hi, y, core), mcol: 4 (over x).
Axes of the slice: x: 4, y: 4, z: 8 (z_hi: 2, z_lo: 4; z = z_hi * 4 + z_lo), core: 2. Of those that a mesh axis runs over, the one named last changes fastest.
Arguments:
- patches: bfloat16 [32, 256, 6144], P('dp', None, ('mcol', 'mrow')), may hold values from -6 to 6
- keep_index: int32 [32, 128], P('dp'), may hold values from 0 to 255, as said below
- counts: int32 [4], replicated, may hold values from 1 to 8, 16 in all
- gain: float32 [6144], P(('mcol', 'mrow')), may hold values from 0.5 to 1.5
- w_qkv: bfloat16 [6144, 3, 4096], P('mcol', None, 'mrow'), may hold values from -0.05103104 to 0.05103104
- w_out: bfloat16 [4096, 6144], P('mrow', 'mcol'), may hold values from -0.375 to 0.375
- cotangent: bfloat16 [4096, 6144], P('dp', ('mcol', 'mrow')), may hold values from -6 to 6
Outputs:
- outputs: bfloat16 [4096, 6144], P('dp', ('mcol', 'mrow'))
- d_patches: bfloat16 [32, 256, 6144], P('dp', None, ('mcol', 'mrow'))
- grad_qkv: float32 [6144, 3, 4096], P(('mcol', 'dp'), None, 'mrow')
- grad_out: float32 [4096, 6144], P('mrow', ('mcol', 'dp'))
- grad_gain: float32 [6144], P(('mcol', 'mrow', 'dp'))
Inputs may be any that keep to these rules, and one draw needn't show every extreme that they name: `keep_index`: each row holds 128 distinct patch numbers in increasing order. The counts sum to 16; the largest is exactly 8.
All inputs are finite; a program needn't handle non-finite values.
Results may differ from a plain program's by a relative error of at most 0.02.
Values may be sent and summed in bfloat16 or wider, within the bound.
A program may use at most 128 MiB of HBM per device.

v0:
```python
from functools import partial

import jax
import jax.numpy as jnp
from jax import lax
from jax.sharding import PartitionSpec as P

D = 6144
HD = 128
KEEP = 128


EPSILON = 1e-06


def normalize(values):
    centred = values - jnp.mean(values, axis=-1, keepdims=True)
    return centred * lax.rsqrt(jnp.mean(centred * centred, axis=-1, keepdims=True) + EPSILON)


def attend(qkv_rows, length):
    total_rows = qkv_rows.shape[0]
    head_count = qkv_rows.shape[2]
    head_size = qkv_rows.shape[3]
    blocks = qkv_rows.reshape(total_rows // length, length, 3, head_count, head_size)
    query_rows = normalize(blocks[:, :, 0])
    key_rows = normalize(blocks[:, :, 1])
    value_rows = blocks[:, :, 2]
    scores = jnp.einsum(
        "bqhd,bkhd->bhqk", query_rows, key_rows, precision=lax.Precision.HIGHEST
    ) * head_size ** (-0.5)
    weights = jnp.exp(scores)
    weights = weights / jnp.sum(weights, axis=-1, keepdims=True)
    head_mixed = jnp.einsum("bhqk,bkhd->bqhd", weights, value_rows, precision=lax.Precision.HIGHEST)
    return head_mixed.reshape(total_rows, head_count * head_size)


def row_gather(values):
    return lax.all_gather(values, "mrow", axis=1, tiled=True)


def column_gather(values):
    return lax.all_gather(values, "mcol", axis=0, tiled=True)


def column_sum(term_maker, shard_rows):
    return lax.psum_scatter(
        term_maker(jnp.int32(0), lax.axis_size("mcol") * shard_rows),
        "mcol",
        scatter_dimension=0,
        tiled=True,
    )


def row_sum(term_maker, shard_rows):
    return lax.psum_scatter(
        term_maker(jnp.int32(0), shard_rows * lax.axis_size("mrow")).astype(jnp.bfloat16),
        "mrow",
        scatter_dimension=0,
        tiled=True,
    ).astype(jnp.float32)


def feature_sums(sum_first, second):
    return lax.psum((sum_first, second), ("mrow", "mcol"))


def layer_pass(inputs, cotan_rows, live_rows, gain, w_qkv, w_out):
    rows_total = inputs.shape[0]
    feature_width = inputs.shape[1]
    local_rows = rows_total // lax.axis_size("mcol")
    stacked = w_qkv.reshape(w_qkv.shape[0], -1)
    inputs_f = inputs.astype(jnp.float32)
    sum_first, second = feature_sums(
        jnp.sum(inputs_f, axis=1), jnp.sum(inputs_f * inputs_f, axis=1)
    )
    mean_row = (sum_first / D)[:, None]
    inv_scale = lax.rsqrt((second / D)[:, None] - mean_row * mean_row + EPSILON)
    centred_rows = (inputs_f - mean_row) * inv_scale
    normed = (centred_rows * gain).astype(jnp.bfloat16)
    gathered = row_gather(normed)

    def project(row_start, row_count):
        return jnp.dot(gathered, stacked, preferred_element_type=jnp.float32)

    qkv_rows = column_sum(project, local_rows).reshape(local_rows, 3, -1, HD)
    head_mixed, pullback = jax.vjp(partial(attend, length=KEEP), qkv_rows)
    heads_out = head_mixed.astype(jnp.bfloat16)
    heads_all = column_gather(heads_out)

    def output_rows(row_start, row_count):
        return lax.dot_general(
            w_out, heads_all, (((0,), (1,)), ((), ())), preferred_element_type=jnp.float32
        )

    attn_out = row_sum(output_rows, feature_width).T
    outputs = ((inputs_f + attn_out) * live_rows).astype(jnp.bfloat16)
    upstream = (cotan_rows.astype(jnp.float32) * live_rows).astype(jnp.bfloat16)
    upstream_all = row_gather(upstream)

    def back_heads(row_start, row_count):
        return lax.dot_general(
            upstream_all, w_out, (((1,), (1,)), ((), ())), preferred_element_type=jnp.float32
        )

    d_mixed = column_sum(back_heads, local_rows)
    d_qkv = pullback(d_mixed)[0].astype(jnp.bfloat16).reshape(local_rows, -1)
    d_all = column_gather(d_qkv)

    def back_features(row_start, row_count):
        return lax.dot_general(
            stacked, d_all, (((1,), (1,)), ((), ())), preferred_element_type=jnp.float32
        )

    d_normed = row_sum(back_features, feature_width).T
    grad_out = lax.dot_general(
        heads_all, upstream_all, (((0,), (0,)), ((), ())), preferred_element_type=jnp.float32
    )
    grad_qkv = lax.dot_general(
        gathered, d_all, (((0,), (0,)), ((), ())), preferred_element_type=jnp.float32
    )
    grad_qkv = grad_qkv.reshape(w_qkv.shape)
    grad_gain = jnp.sum(d_normed * centred_rows, axis=0)
    d_hat = d_normed * gain
    sum_hat, sum_cross = feature_sums(jnp.sum(d_hat, axis=1), jnp.sum(d_hat * centred_rows, axis=1))
    d_inputs = upstream.astype(jnp.float32) + inv_scale * (
        d_hat - (sum_hat / D)[:, None] - centred_rows * (sum_cross / D)[:, None]
    )
    return (outputs, d_inputs.astype(jnp.bfloat16), grad_qkv, grad_out, grad_gain)


def shards(patches, keep_index, counts, gain, w_qkv, w_out, cotangent):
    images, patch_count, width = patches.shape
    keep_len = keep_index.shape[1]
    kept_rows = jnp.take_along_axis(patches, keep_index[:, :, None], axis=1)
    cotan_rows = cotangent.reshape(images, keep_len, width)
    group_index = lax.axis_index("dp")
    groups = counts.shape[0]
    group_ids = jnp.arange(groups, dtype=jnp.int32)
    own_count = jnp.sum(jnp.where(group_ids == group_index, counts, 0))
    slot_ids = jnp.arange(images, dtype=jnp.int32)
    live_image = (slot_ids < own_count).astype(jnp.float32)
    held_images = kept_rows.shape[0]
    live_rows = jnp.broadcast_to(live_image[:, None], (held_images, keep_len)).reshape(
        held_images * keep_len, 1
    )
    outputs, d_inputs, grad_qkv, grad_out, grad_gain = layer_pass(
        kept_rows.reshape(-1, width), cotan_rows.reshape(-1, width), live_rows, gain, w_qkv, w_out
    )
    out_image = outputs.reshape(held_images, keep_len, width)
    d_image = d_inputs.reshape(held_images, keep_len, width)
    d_patches = (
        jnp.zeros((images, patch_count, width), jnp.bfloat16)
        .at[slot_ids[:, None], keep_index]
        .set(d_image)
    )
    grad_qkv, grad_out, grad_gain = (
        lax.psum_scatter(grad_qkv, "dp", scatter_dimension=0, tiled=True),
        lax.psum_scatter(grad_out, "dp", scatter_dimension=1, tiled=True),
        lax.psum_scatter(grad_gain, "dp", scatter_dimension=0, tiled=True),
    )
    return (out_image.reshape(images * keep_len, width), d_patches, grad_qkv, grad_out, grad_gain)


def solution(mesh):
    placed = (
        P("dp", None, ("mcol", "mrow")),
        P("dp", None),
        P(),
        P(("mcol", "mrow")),
        P("mcol", None, "mrow"),
        P("mrow", "mcol"),
        P("dp", ("mcol", "mrow")),
    )
    return jax.shard_map(
        shards,
        mesh=mesh,
        in_specs=placed,
        out_specs=(
            P("dp", ("mcol", "mrow")),
            P("dp", None, ("mcol", "mrow")),
            P(("mcol", "dp"), None, "mrow"),
            P("mrow", ("mcol", "dp")),
            P(("mcol", "mrow", "dp")),
        ),
        check_vma=False,
    )
```

profile of v0, /device:TPU:0, one launch (start us, length us, event | category | flops | bytes accessed | tf_op | source)
XLA Modules:
  0.0 852.5 jit_solution(13378158664047668434)
XLA Ops:
  7.3 1.4 fusion.51
  8.6 0.6 compare_convert_fusion
  9.3 1.1 copy.76
  10.4 0.2 multiply_convert_fusion
  10.6 0.8 copy.77
  11.5 1.3 copy.66
  12.8 0.7 or_bitcast_fusion
  13.5 5.8 gather_fusion
  19.4 0.5 convert_reduce_fusion
  19.8 214.0 %all-reduce.5 = (f32[1024]{0:T(1024)S(1)}, f32[1024]{0:T(1024)S(1)}) all-reduce(f32[1024]{0:T(1024)S(1)} %bitcast.137, f32[1024]{0:T(1024)S(1)} %bitcast.136), channel_id=1, replica_groups=mesh['dp'=4,'mrow'=16,'mcol'=4] {'mrow','mcol'}, use_global_device_ids=true, to_apply=%region_3.4 | all-reduce | flops 2048 | bytes 16384 | tf_op jit(solution)/shard_map/psum | solution.py:65
  233.8 0.5 fusion.9
  234.3 0.8 copy.67
  235.3 4.0 fusion.54
  239.4 2.5 copy.68
  241.8 57.9 %all-gather.4.cloned.1.call-done = bf16[1024,1536]{0,1:T(8,128)(2,1)} async-done(((bf16[1024,96]{0,1:T(8,128)(2,1)}), bf16[1024,1536]{0,1:T(8,128)(2,1)}) %all-gather.4.cloned.1.call-update) | async-done | bytes 3145744 | tf_op jit(solution)/shard_map/all_gather | solution.py:39
  299.7 7.0 fusion.53
  306.7 0.2 all-gather.8.cloned.1.call-start
  307.0 17.8 %reduce-scatter.13.cloned.1.call-done = f32[256,256]{1,0:T(8,128)} async-done(((f32[1024,256]{1,0:T(8,128)}), f32[256,256]{1,0:T(8,128)}) %reduce-scatter.13.cloned.1.call-update) | async-done | bytes 262160 | tf_op jit(solution)/shard_map/reduce_scatter | solution.py:47
  324.7 1.1 reshape.130
  325.8 0.1 copy.78
  325.9 41.9 %reduce-scatter.11.cloned.1.call-done = f32[256,768]{1,0:T(8,128)} async-done(((f32[1024,768]{1,0:T(8,128)}), f32[256,768]{1,0:T(8,128)}) %reduce-scatter.11.cloned.1.call-update) | async-done | bytes 786448 | tf_op jit(solution)/shard_map/reduce_scatter | solution.py:47
  367.9 1.5 reshape_reshape.3
  369.4 0.7 slice_reduce_fusion.1
  370.1 0.1 copy.104
  370.1 0.1 copy.105
  370.2 0.1 copy.102
  370.4 0.1 copy.103
  370.5 0.1 copy.101
  370.8 0.6 fusion.52
  371.4 0.7 convolution_bitcast_fusion.2
  372.1 0.6 multiply_reduce_fusion.2
  372.7 0.5 multiply_reduce_fusion
  373.2 0.7 multiply_reduce_fusion.1
  373.9 0.1 fusion.47
  374.1 0.1 fusion.46
  374.3 0.4 copy.83
  374.7 0.9 convert_element_type.76
  375.7 0.4 fusion.3
  376.1 0.1 copy.75
  376.3 13.4 %all_gather.13 = bf16[1024,256]{1,0:T(8,128)(2,1)S(1)} all-gather(bf16[256,256]{1,0:T(8,128)(2,1)S(1)} %bitcast.134), channel_id=1, replica_groups=mesh['dp'=4,'mrow'=16,'mcol'=4] {'mcol'}, dimensions={0}, use_global_device_ids=true | all-gather | bytes 655360 | tf_op jit(solution)/shard_map/all_gather | solution.py:43
  389.7 2.7 fusion.1
  392.3 4.7 copy.97
  397.1 7.5 all-gather.8.cloned.1.call-done
  404.6 6.4 fusion
  411.1 4.7 copy.99
  415.8 4.2 fusion.56
  420.1 0.3 reduce-scatter.15.cloned.1.call-start
  420.4 6.3 fusion.55
  426.7 6.2 copy.85
  433.0 0.6 copy-done.9
  433.6 0.6 dynamic-slice
  434.9 0.1 multiply_reduce_fusion.5
  434.9 0.1 and_reduce_fusion
  435.0 70.0 %reduce-scatter.19.cloned.1.call-done = bf16[96,1024]{1,0:T(8,128)(2,1)} async-done(((bf16[1536,1024]{1,0:T(8,128)(2,1)}), bf16[96,1024]{1,0:T(8,128)(2,1)}) %reduce-scatter.19.cloned.1.call-update) | async-done | bytes 196624
  505.0 1.1 copy.98
  506.1 95.6 %reduce-scatter.21.cloned.1.call-done = bf16[96,1024]{1,0:T(8,128)(2,1)} async-done(((bf16[1536,1024]{1,0:T(8,128)(2,1)}), bf16[96,1024]{1,0:T(8,128)(2,1)}) %reduce-scatter.21.cloned.1.call-update) | async-done | bytes 196624
  601.7 1.1 copy.100
  602.8 1.2 fusion.15
  604.1 210.5 %all-reduce.4 = (f32[1024]{0:T(1024)S(1)}, f32[1024]{0:T(1024)S(1)}) all-reduce(f32[1024]{0:T(1024)S(1)} %get-tuple-element.28, f32[1024]{0:T(1024)S(1)} %get-tuple-element.31), channel_id=1, replica_groups=mesh['dp'=4,'mrow'=16,'mcol'=4] {'mrow','mcol'}, use_global_device_ids=true, to_apply=%region_22.23 | all-reduce | flops 2048 | bytes 16384 | tf_op jit(solution)/shard_map/psum | solution.py:65
  814.6 4.4 scatter_custom_fusion
  818.9 1.0 copy.87
  819.9 0.8 copy.86
  820.7 24.7 %all-reduce.3 = f32[96]{0:T(128)S(1)} all-reduce(f32[96]{0:T(128)S(1)} %get-tuple-element.27), channel_id=8, replica_groups=mesh['dp'=4,'mrow'=16,'mcol'=4] {'dp'}, use_global_device_ids=true, to_apply=%region_27.28.clone | all-reduce | flops 96 | bytes 768
  845.4 0.6 dynamic-slice.1
  (62 shorter events, 1.0 us)
Async XLA Ops:
  7.2 228.1 %copy-start = (bf16[256,1536]{1,0:T(8,128)(2,1)S(1)}, bf16[256,1536]{1,0:T(8,128)(2,1)}, u32[]{:S(2)}) copy-start(bf16[256,1536]{1,0:T(8,128)(2,1)} %param.12) | copy-start | bytes 2359300
  7.2 12.2 %copy-start.4 = (s32[8,128]{1,0:T(8,128)S(1)}, s32[8,128]{1,0:T(8,128)}, u32[]{:S(2)}) copy-start(s32[8,128]{1,0:T(8,128)} %param.8) | copy-start | bytes 12292
  7.2 226.6 %copy-start.5 = (f32[96]{0:T(128)S(1)}, f32[96]{0:T(128)}, u32[]{:S(2)}) copy-start(f32[96]{0:T(128)} %param.10) | copy-start | bytes 1156
  7.2 228.0 %all-gather.6.cloned.1.call-start = ((), (), s32[]{:S(2)}) async-start(), calls=%async_computation.8 | async-start | bytes 3342336 | tf_op jit(solution)/shard_map/all_gather | solution.py:39
  10.4 2.4 copy-start.2
  11.5 288.2 %all-gather.4.cloned.1.call-start = ((), (), s32[]{:S(2)}) async-start(), calls=%async_computation.6 | async-start | bytes 3342336 | tf_op jit(solution)/shard_map/all_gather | solution.py:39
  235.2 4.2 copy-start.1
  235.2 89.5 %reduce-scatter.13.cloned.1.call-start = ((), (), s32[]{:S(2)}) async-start(), calls=%async_computation.9 | async-start | bytes 1310720 | tf_op jit(solution)/shard_map/reduce_scatter | solution.py:47
  239.3 128.6 %reduce-scatter.11.cloned.1.call-start = ((), (), s32[]{:S(2)}) async-start(), calls=%async_computation.7 | async-start | bytes 3932160 | tf_op jit(solution)/shard_map/reduce_scatter | solution.py:47
  306.7 97.9 %all-gather.8.cloned.1.call-start = ((), (), s32[]{:S(2)}) async-start(), calls=%async_computation.10 | async-start | bytes 1966080 | tf_op jit(solution)/shard_map/all_gather | solution.py:43
  375.6 129.4 %reduce-scatter.19.cloned.1.call-start = ((), (), s32[]{:S(2)}) async-start(), calls=%async_computation.13 | async-start | bytes 3342336
  397.0 204.7 %reduce-scatter.21.cloned.1.call-start = ((), (), s32[]{:S(2)}) async-start(), calls=%async_computation.14 | async-start | bytes 3342336
  415.8 4.6 copy-start.8
  415.8 430.2 %reduce-scatter.17.cloned.1.call-start = ((), (), s32[]{:S(2)}) async-start(), calls=%async_computation.12 | async-start | bytes 1966080 | tf_op jit(solution)/shard_map/reduce_scatter | solution.py:159
  420.1 425.9 %reduce-scatter.15.cloned.1.call-start = ((), (), s32[]{:S(2)}) async-start(), calls=%async_computation.11 | async-start | bytes 5898240 | tf_op jit(solution)/shard_map/reduce_scatter | solution.py:158
  432.9 0.7 copy-start.9
  432.9 1.9 copy-start.7
  432.9 2.0 copy-start.6
  432.9 381.6 %copy-start.3 = (bf16[1024,96]{1,0:T(8,128)(2,1)S(1)}, bf16[1024,96]{1,0:T(8,128)(2,1)}, u32[]{:S(2)}) copy-start(bf16[1024,96]{1,0:T(8,128)(2,1)} %copy-done.2) | copy-start | bytes 589828
Sparse Core Ops, SparseCore 0:
  11.6 71.5 all-gather.5
  235.3 64.4 all-gather.3
  302.9 21.8 reduce-scatter.12
  327.3 40.5 reduce-scatter.10
  375.8 28.7 all-gather.7
  409.4 95.6 reduce-scatter.18
  510.0 91.6 reduce-scatter.20
  605.0 37.2 reduce-scatter.16
  645.6 90.9 reduce-scatter.14
where the time goes:
time: 853 us; the launch traced here: 852 us
  blocking collectives  462 us (54%)
  waiting for transfers between devices  291 us (34%)
  local copies, waits for them, and re-layouts  38.5 us (5%)
  matrix products  34.2 us (4%)
  between operations  14.9 us (2%)
  other arithmetic  10.8 us (1%)
    psum x2, blocking collectives, feature_sums(): return lax.psum((sum_first, second), ('mrow', 'mcol'))  424 us
    unnamed x11, waiting for transfers between devices  166 us
    reduce_scatter x2, waiting for transfers between devices, column_sum(): lax.psum_scatter(term_maker(jnp.int32(0), lax.axis_size('mcol') * shard_r...  59.7 us
    all_gather x2, waiting for transfers between devices, row_gather(): return lax.all_gather(values, 'mrow', axis=1, tiled=True)  57.9 us
    unnamed x1, blocking collectives  24.7 us
    unnamed x37, local copies, waits for them, and re-layouts  20.6 us
  transfers between devices with their start and end apart: 9, of which 6 were waited for; matrix products, arithmetic and copies ran while one was open for 8% of the time, Pallas kernels for 0%

commit v1 on v0

v1 whole, which is shorter than its diff:
```python
from functools import partial

import jax
import jax.numpy as jnp
from jax import lax
from jax.experimental import pallas as pl
from jax.experimental.pallas import tpu as pltpu
from jax.sharding import PartitionSpec as P

D = 6144
HD = 128
KEEP = 128
EPSILON = 1e-06

F32 = jnp.float32
BF16 = jnp.bfloat16
MESH = pl.DeviceIdType.MESH
VM = pl.BlockSpec(memory_space=pltpu.VMEM)
SM = pl.BlockSpec(memory_space=pltpu.SMEM)
DMA = pltpu.SemaphoreType.DMA


def dot(a, b, ca, cb):
    return lax.dot_general(a, b, (((ca,), (cb,)), ((), ())), preferred_element_type=F32)


def remote(src, dst, send, recv, where):
    return pltpu.make_async_remote_copy(
        src_ref=src, dst_ref=dst, send_sem=send, recv_sem=recv, device_id=where, device_id_type=MESH
    )


def greet(peers):
    barrier = pltpu.get_barrier_semaphore()
    for peer in peers:
        pl.semaphore_signal(barrier, inc=1, device_id=peer, device_id_type=MESH)
    pl.semaphore_wait(barrier, len(peers))


class Place:
    def __init__(self):
        self.me = lax.axis_index("mrow")
        self.core = lax.rem(self.me, 2)
        self.y = lax.rem(self.me // 2, 4)
        self.zh = self.me // 8
        self.x = lax.axis_index("mcol")
        self.sib = self.at(self.zh, 0, 1 - self.core)
        self.anti = self.at(1 - self.zh, 0, self.core)
        self.ys = [self.at(self.zh, d, self.core) for d in range(4)]
        self.xs = [lax.rem(self.x + d, 4) for d in range(4)]

    def at(self, zh, dy, core):
        return zh * 8 + lax.rem(self.y + dy, 4) * 2 + core

    def peers(self):
        rows = [self.sib, self.anti] + self.ys[1:]
        return [{"mrow": r} for r in rows] + [{"mcol": c} for c in self.xs[1:]]


class SmallSum:
    def __init__(self, place, val, box, send, recv, x_rows):
        self.place, self.val, self.box = place, val, box
        self.send, self.recv, self.x_rows = send, recv, x_rows
        self.live = []
        self.n = 0

    def push(self, peers, rows=None):
        self.live = []
        for where in peers:
            k = self.n
            self.n += 1
            stage = self.val.at[self.stage]
            box = self.box.at[k]
            if rows is not None:
                stage, box = stage.at[:rows], box.at[:rows]
            c = remote(stage, box, self.send.at[k], self.recv.at[k], where)
            c.start()
            self.live.append((k, c))

    def start(self, value):
        self.stage = 0
        self.val[0] = value
        self.push([{"mrow": self.place.sib}])

    def step(self):
        total = self.val[self.stage]
        rows = self.x_rows if self.stage == 3 else total.shape[0]
        total = total[:rows]
        for k, c in self.live:
            c.wait()
            total = total + self.box[k, :rows]
        self.stage += 1
        if self.stage < 4:
            self.val[self.stage] = total
        if self.stage == 1:
            self.push([{"mrow": r} for r in self.place.ys[1:]])
        elif self.stage == 2:
            self.push([{"mrow": self.place.anti}])
        elif self.stage == 3:
            self.push([{"mcol": c} for c in self.place.xs[1:]], self.x_rows)
        return total


def prep_kernel(n, p_ref, k_ref, c_ref, live_ref, x_ref, u_ref, s_ref):
    patch = lax.broadcasted_iota(jnp.int32, (p_ref.shape[1], KEEP), 0)
    eye = (
        lax.broadcasted_iota(jnp.int32, (KEEP, KEEP), 0)
        == lax.broadcasted_iota(jnp.int32, (KEEP, KEEP), 1)
    ).astype(F32).astype(BF16)
    for i in range(n):
        lanes = slice(i * KEEP, (i + 1) * KEEP)
        pick = (patch == k_ref[i : i + 1, :]).astype(F32).astype(BF16)
        rows = dot(p_ref[i], pick, 0, 0)
        x_ref[:, lanes] = rows.astype(BF16)
        s_ref[i : i + 1, :] = jnp.sum(rows, axis=0, keepdims=True)
        s_ref[n + i : n + i + 1, :] = jnp.sum(rows * rows, axis=0, keepdims=True)
        u_ref[:, lanes] = (dot(c_ref[lanes, :], eye, 0, 0) * live_ref[i]).astype(BF16)


def gather_kernel(
    x_ref, u_ref, s_ref, xg, ug, st, box, val, ss, sr, zsend, ysend, fsend, csend, xr, ur
):
    place = Place()
    greet(place.peers())
    me, sib = place.me, {"mrow": place.sib}
    right, left = {"mrow": place.ys[1]}, {"mrow": place.ys[3]}
    arrays = ((x_ref, xg, xr), (u_ref, ug, ur))
    small = SmallSum(place, val, box, ss, sr, st.shape[0] - 16)
    sends = []
    ncore = [0]

    def push(a, src, slot, sem, where):
        _, out, recv = arrays[a]
        c = remote(src, out.at[slot], sem, recv.at[slot], where)
        c.start()
        sends.append(c)

    def got(a, slot):
        src, out, recv = arrays[a]
        remote(src, out.at[slot], zsend.at[0], recv.at[slot], sib).wait_recv()

    def to_sib(slot):
        for a in range(2):
            push(a, arrays[a][1].at[slot], slot, csend.at[a, ncore[0]], sib)
        ncore[0] += 1

    small.start(s_ref[...])
    for a in range(2):
        push(a, arrays[a][0], me, zsend.at[a], {"mrow": place.anti})
    for a in range(2):
        push(a, arrays[a][0], me, ysend.at[a, 0], right)
        push(a, arrays[a][0], me, ysend.at[a, 1], left)
    for a in range(2):
        push(a, arrays[a][0], me, csend.at[a, 0], sib)
    ncore[0] = 1
    xg[me] = x_ref[...]
    ug[me] = u_ref[...]
    small.step()
    anti = place.anti
    for a in range(2):
        got(a, anti)
        push(a, arrays[a][1].at[anti], anti, ysend.at[a, 2], right)
        push(a, arrays[a][1].at[anti], anti, ysend.at[a, 3], left)
    to_sib(anti)
    small.step()
    for half, zh in enumerate((place.zh, 1 - place.zh)):
        before, after = place.at(zh, 3, place.core), place.at(zh, 1, place.core)
        got(0, before)
        push(0, xg.at[before], before, fsend.at[0, half], right)
        got(1, after)
        push(1, ug.at[after], after, fsend.at[1, half], left)
        got(1, before)
        to_sib(before)
        got(0, after)
        to_sib(after)
        if half == 0:
            small.step()
    for zh in (place.zh, 1 - place.zh):
        far = place.at(zh, 2, place.core)
        got(0, far)
        got(1, far)
        to_sib(far)
    st[...] = jnp.concatenate([small.step(), val[3, st.shape[0] - 16 :]], axis=0)
    for zh in range(2):
        for dy in range(4):
            for a in range(2):
                got(a, place.at(zh, dy, 1 - place.core))
    for c in sends:
        c.wait_send()


def attend(q, k, v, do):
    def norm(t):
        c = t - jnp.mean(t, axis=0, keepdims=True)
        i = lax.rsqrt(jnp.mean(c * c, axis=0, keepdims=True) + EPSILON)
        return c * i, i

    def norm_back(d, y, i):
        return i * (
            d - jnp.mean(d, axis=0, keepdims=True) - y * jnp.mean(d * y, axis=0, keepdims=True)
        )

    def mm(a, b, ca, cb):
        return lax.dot_general(
            a, b, (((ca,), (cb,)), ((), ())), preferred_element_type=F32, precision=lax.Precision.HIGHEST
        )

    scale = HD ** (-0.5)
    qn, iq = norm(q)
    kn, ik = norm(k)
    w = jnp.exp(mm(kn, qn, 0, 0) * scale)
    w = w / jnp.sum(w, axis=0, keepdims=True)
    out = mm(v, w, 1, 0)
    dw = mm(v, do, 0, 0)
    ds = w * (dw - jnp.sum(w * dw, axis=0, keepdims=True)) * scale
    dv = mm(do, w, 1, 1)
    dq = norm_back(mm(kn, ds, 1, 0), qn, iq)
    dk = norm_back(mm(qn, ds, 1, 1), kn, ik)
    return out, dq, dk, dv


def middle_kernel(
    q_ref, m_ref, dall, hall, work, own, bq, bm, sq, sm, rq, rm, gs, gr
):
    x = lax.axis_index("mcol")
    xs = [lax.rem(x + d, 4) for d in range(4)]
    greet([{"mcol": c} for c in (xs[1], xs[3])])
    right, left = {"mcol": xs[1]}, {"mcol": xs[3]}
    width = own.shape[1]
    qrows = q_ref.shape[0]
    half = own.shape[0] // 2
    mrows = m_ref.shape[0]
    qminus = qrows - half

    def lanes(block):
        return pl.ds(pl.multiple_of(block * width, width), width)

    sends = []
    def push_plus(src, slot, where):
        c = remote(src, bq.at[slot], sq.at[slot], rq.at[slot], where)
        c.start()
        sends.append(c)

    def push_minus(srcq, srcm, slot, where):
        c = remote(srcq, bq.at[slot, :qminus], sq.at[slot], rq.at[slot], where)
        d = remote(srcm, bm.at[slot], sm.at[slot], rm.at[slot], where)
        c.start()
        d.start()
        sends.extend((c, d))

    def got_plus(slot):
        remote(bq.at[slot], bq.at[slot], sq.at[slot], rq.at[slot], right).wait_recv()

    def got_minus(slot):
        remote(bq.at[slot, :qminus], bq.at[slot, :qminus], sq.at[slot], rq.at[slot], right).wait_recv()
        remote(bm.at[slot], bm.at[slot], sm.at[slot], rm.at[slot], right).wait_recv()

    plus, minus = pl.ds(0, half), pl.ds(half, qminus)
    push_plus(q_ref.at[plus, lanes(xs[2])], 0, right)
    push_minus(q_ref.at[minus, lanes(xs[2])], m_ref.at[:, lanes(xs[2])], 1, left)
    push_plus(q_ref.at[plus, lanes(xs[3])], 2, left)
    push_minus(q_ref.at[minus, lanes(xs[1])], m_ref.at[:, lanes(xs[1])], 3, right)
    got_plus(0)
    work[:half] = (bq[0].astype(F32) + q_ref[plus, lanes(xs[1])].astype(F32)).astype(BF16)
    push_plus(work.at[:half], 4, right)
    got_minus(1)
    work[half:qrows] = (
        bq[1, :qminus].astype(F32) + q_ref[minus, lanes(xs[3])].astype(F32)
    ).astype(BF16)
    work[qrows:] = (bm[1].astype(F32) + m_ref[:, lanes(xs[3])].astype(F32)).astype(BF16)
    push_minus(work.at[half:qrows], work.at[qrows:], 5, left)
    got_plus(2)
    got_minus(3)
    got_plus(4)
    got_minus(5)
    heads = mrows // HD

    def total(r0, c0):
        cols = pl.ds(pl.multiple_of(x * width + c0, HD), HD)
        here = slice(c0, c0 + HD)
        if r0 < half:
            parts = q_ref[r0 : r0 + HD, cols], bq[2, r0 : r0 + HD, here], bq[4, r0 : r0 + HD, here]
        elif r0 < qrows:
            b = slice(r0 - half, r0 - half + HD)
            parts = q_ref[r0 : r0 + HD, cols], bq[3, b, here], bq[5, b, here]
        else:
            b = slice(r0 - qrows, r0 - qrows + HD)
            parts = m_ref[b, cols], bm[3, b, here], bm[5, b, here]
        return parts[0].astype(F32) + parts[1].astype(F32) + parts[2].astype(F32)

    for c0 in range(0, width, HD):
        here = slice(c0, c0 + HD)
        for h in range(heads):
            q, k, v, do = (total((part * heads + h) * HD, c0) for part in range(4))
            out, dq, dk, dv = attend(q, k, v, do)
            for part, value in enumerate((dq, dk, dv, out)):
                r0 = (part * heads + h) * HD
                own[r0 : r0 + HD, here] = value.astype(BF16)

    dst = ((dall, pl.ds(0, half), pl.ds(0, half)),
           (dall, pl.ds(half, qminus), pl.ds(half, qminus)),
           (hall, pl.ds(qrows, mrows), pl.ds(0, mrows)))

    def push_part(p, block, src, k, where):
        out, _, rows = dst[p]
        c = remote(src, out.at[rows, lanes(block)], gs.at[p, k], gr.at[p, block], where)
        c.start()
        sends.append(c)

    def got_part(p, block):
        out, rows_own, rows = dst[p]
        remote(own.at[rows_own], out.at[rows, lanes(block)], gs.at[p, 0], gr.at[p, block], right).wait_recv()

    for p in range(3):
        for k, where in enumerate((right, left)):
            push_part(p, x, own.at[dst[p][1]], k, where)
    dall[:, lanes(x)] = own[:qrows]
    hall[:, lanes(x)] = own[qrows:]
    got_part(0, xs[3])
    push_part(0, xs[3], dall.at[dst[0][2], lanes(xs[3])], 2, right)
    for p in (1, 2):
        got_part(p, xs[1])
        out = dst[p][0]
        push_part(p, xs[1], out.at[dst[p][2], lanes(xs[1])], 2, left)
    got_part(1, xs[3])
    got_part(2, xs[3])
    got_part(0, xs[1])
    for p in range(3):
        got_part(p, xs[2])
    for c in sends:
        c.wait_send()


def reduce_kernel(
    a_ref, n_ref, s_ref, g_ref, o_ref, ra, rn, st, rg, ro,
    box, val, cbox, ybuf, ysum, ztot, zbox, gr_buf, gl_buf, or_buf, ol_buf,
    ss, sr, csend, crecv, ysend, yrecv, zsend, zrecv, dsend, drecv,
):
    place = Place()
    dp = lax.axis_index("dp")
    ndp = lax.axis_size("dp")
    near = [{"dp": lax.rem(dp + 1, ndp)}, {"dp": lax.rem(dp + ndp - 1, ndp)}]
    greet(place.peers() + near)
    right, left = {"mrow": place.ys[1]}, {"mrow": place.ys[3]}
    sib, anti = {"mrow": place.sib}, {"mrow": place.anti}
    core, zh = place.core, place.zh
    ydev = [lax.rem(place.y + d, 4) for d in range(4)]
    arrays = (a_ref, n_ref)
    outs = (ra, rn)
    rows = ra.shape[0]
    sends = []

    small = SmallSum(place, val, box, ss, sr, st.shape[0])
    small.start(s_ref[...])

    gcols = ro.shape[1]
    bufs = ((gr_buf, or_buf), (gl_buf, ol_buf))

    def own_block(t):
        return g_ref.at[t], o_ref.at[:, pl.ds(pl.multiple_of(t * gcols, gcols), gcols)]

    def line_copies(direction, t, own):
        slot = t - 1 if direction == 0 else t
        srcs = own_block(t) if own else tuple(b.at[slot] for b in bufs[direction])
        return [
            remote(
                srcs[i], bufs[direction][i].at[slot],
                dsend.at[direction, slot, i], drecv.at[direction, slot, i], near[direction],
            )
            for i in range(2)
        ]

    def forward(direction, t):
        slot = t - 1 if direction == 0 else t
        for c in line_copies(direction, t, False):
            c.wait_recv()
        gb, ob = bufs[direction][0].at[slot], bufs[direction][1].at[slot]
        add_rows(gb, g_ref.at[t])
        add_rows(ob, o_ref.at[:, pl.ds(pl.multiple_of(t * gcols, gcols), gcols)])
        for c in line_copies(direction, t, False):
            c.start()

    def add_rows(dst, src):
        @pl.loop(0, dst.shape[0] // 16)
        def _(i):
            r = pl.ds(pl.multiple_of(i * 16, 16), 16)
            dst[r] = (dst[r].astype(F32) + src[r].astype(F32)).astype(BF16)

    @pl.when(dp == 0)
    def _():
        for t in (3, 2, 1):
            for c in line_copies(0, t, True):
                c.start()

    @pl.when(dp == 3)
    def _():
        for t in (0, 1, 2):
            for c in line_copies(1, t, True):
                c.start()

    order = (2, 1, 3, 0)
    cores = []
    for d in order:
        for a in range(2):
            c = remote(
                arrays[a].at[:, ydev[d], 1 - core], cbox.at[a, d], csend.at[a, d], crecv.at[a, d], sib
            )
            c.start()
            cores.append(c)

    def core_sum(a, d, extra=None):
        remote(
            arrays[a].at[:, ydev[d], 1 - core], cbox.at[a, d], csend.at[a, d], crecv.at[a, d], sib
        ).wait_recv()
        add_in(cbox.at[a, d], [arrays[a].at[:, ydev[d], core]] + ([extra] if extra is not None else []))

    def add_in(dst, srcs):
        for z in range(2):
            @pl.loop(0, rows // 16)
            def _(i):
                r = pl.ds(pl.multiple_of(i * 16, 16), 16)
                total = dst[z, r].astype(F32)
                for s in srcs:
                    total = total + s[z, r].astype(F32)
                dst[z, r] = total.astype(BF16)

    def ypush(a, src, slot, where):
        c = remote(src, ybuf.at[a, slot], ysend.at[a, slot], yrecv.at[a, slot], where)
        c.start()
        sends.append(c)

    def ygot(a, slot):
        remote(ybuf.at[a, slot], ybuf.at[a, slot], ysend.at[a, slot], yrecv.at[a, slot], right).wait_recv()

    ahead, behind = (right, left), (left, right)
    nxt, prv = (1, 3), (3, 1)
    for a in range(2):
        core_sum(a, 2)
        ypush(a, cbox.at[a, 2], 0, ahead[a])
    small.step()
    for a in range(2):
        core_sum(a, prv[a])
        ypush(a, cbox.at[a, prv[a]], 1, behind[a])
    for a in range(2):
        core_sum(a, nxt[a])
    small.step()
    for a in range(2):
        ygot(a, 0)
        add_in(cbox.at[a, nxt[a]], [ybuf.at[a, 0]])
        ypush(a, cbox.at[a, nxt[a]], 2, ahead[a])
    for a in range(2):
        core_sum(a, 0)
    small.step()

    @pl.when(dp == 1)
    def _():
        forward(0, 3)

    @pl.when(dp == 2)
    def _():
        forward(1, 0)

    zcopies = []
    for a in range(2):
        ygot(a, 1)
        ygot(a, 2)

        @pl.loop(0, rows // 16)
        def _(i):
            r = pl.ds(pl.multiple_of(i * 16, 16), 16)
            for z in range(2):
                ysum[a, z, r] = (
                    cbox[a, 0, z, r].astype(F32)
                    + ybuf[a, 1, z, r].astype(F32)
                    + ybuf[a, 2, z, r].astype(F32)
                )
            ztot[a, r] = ysum[a, 1 - zh, r].astype(BF16)

        c = remote(ztot.at[a], zbox.at[a], zsend.at[a], zrecv.at[a], anti)
        c.start()
        zcopies.append(c)
    st[...] = small.step()

    @pl.when(dp == 1)
    def _():
        forward(0, 2)
        forward(1, 0)

    @pl.when(dp == 2)
    def _():
        forward(1, 1)
        forward(0, 3)

    for a in range(2):
        zcopies[a].wait()

        @pl.loop(0, rows // 16)
        def _(i):
            r = pl.ds(pl.multiple_of(i * 16, 16), 16)
            outs[a][r] = ysum[a, zh, r] + zbox[a, r].astype(F32)

    def finish(direction, into, first):
        slot = dp - 1 if direction == 0 else dp
        for c in line_copies(direction, dp, False):
            c.wait_recv()
        for b, own, out in (
            (bufs[direction][0].at[slot], g_ref.at[dp], rg),
            (bufs[direction][1].at[slot], own_block(dp)[1], ro),
        ):
            @pl.loop(0, out.shape[0] // 16)
            def _(i):
                r = pl.ds(pl.multiple_of(i * 16, 16), 16)
                base = own[r].astype(F32) if first else out[r]
                out[r] = base + b[r].astype(F32)

    @pl.when(dp == 0)
    def _():
        finish(1, None, True)

    @pl.when(dp > 0)
    def _():
        finish(0, None, True)

    @pl.when((dp > 0) & (dp < 3))
    def _():
        finish(1, None, False)

    for c in cores + sends:
        c.wait_send()
    for t in range(1, 4):
        @pl.when(dp < t)
        def _():
            for c in line_copies(0, t, False):
                c.wait_send()
    for t in range(3):
        @pl.when(dp > t)
        def _():
            for c in line_copies(1, t, False):
                c.wait_send()


def gain_kernel(g_ref, out, box, send, recv):
    dp = lax.axis_index("dp")
    others = [lax.rem(dp + d, 4) for d in range(1, 4)]
    greet([{"dp": o} for o in others])
    copies = []
    for k, o in enumerate(others):
        c = remote(g_ref, box.at[k], send.at[k], recv.at[k], {"dp": o})
        c.start()
        copies.append(c)
    total = g_ref[...]
    for k, c in enumerate(copies):
        c.wait()
        total = total + box[k]
    out[...] = total


def post_kernel(n, x_ref, a_ref, d_ref, u_ref, k_ref, live_ref, g_ref, st_ref, bt_ref, out, dp_out, gg):
    patch = lax.broadcasted_iota(jnp.int32, (dp_out.shape[1], KEEP), 0)
    eye = (
        lax.broadcasted_iota(jnp.int32, (KEEP, KEEP), 0)
        == lax.broadcasted_iota(jnp.int32, (KEEP, KEEP), 1)
    ).astype(F32).astype(BF16)
    gain = g_ref[...]
    acc = jnp.zeros(gg.shape, F32)
    for i in range(n):
        lanes = slice(i * KEEP, (i + 1) * KEEP)
        mean = st_ref[i : i + 1, :] * (1.0 / D)
        inv = lax.rsqrt(st_ref[n + i : n + i + 1, :] * (1.0 / D) - mean * mean + EPSILON)
        mean_hat = bt_ref[i : i + 1, :] * (1.0 / D)
        mean_cross = bt_ref[n + i : n + i + 1, :] * (1.0 / D)
        rows = x_ref[:, lanes].astype(F32)
        centred = (rows - mean) * inv
        normed_grad = d_ref[:, lanes]
        acc = acc + normed_grad * centred
        d_in = u_ref[:, lanes].astype(F32) + inv * (
            normed_grad * gain - mean_hat - centred * mean_cross
        )
        pick = (patch == k_ref[i : i + 1, :]).astype(F32).astype(BF16)
        dp_out[i] = dot(pick, d_in.astype(BF16), 1, 1).astype(BF16)
        res = ((rows + a_ref[:, lanes]) * live_ref[i]).astype(BF16)
        out[lanes, :] = dot(eye, res, 1, 1).astype(BF16)
    gg[...] = acc


def call(kernel, outs, scratch=(), cid=None, vmem=48, smem=(), n_in=0):
    params = dict(vmem_limit_bytes=vmem * 1024 * 1024)
    if cid is not None:
        params.update(collective_id=cid, has_side_effects=True)
    return pl.pallas_call(
        kernel,
        out_shape=[jax.ShapeDtypeStruct(*o) for o in outs],
        in_specs=[SM if i in smem else VM for i in range(n_in)],
        out_specs=[VM] * len(outs),
        scratch_shapes=list(scratch),
        compiler_params=pltpu.CompilerParams(**params),
    )


def sharded(patches, keep_index, counts, gain, w_qkv, w_out, cotangent):
    n, patch_count, width = patches.shape
    rows = n * KEEP
    me = lax.axis_index("mrow")
    own_count = counts[lax.axis_index("dp")]
    live = (jnp.arange(n, dtype=jnp.int32) < own_count).astype(F32)
    stacked = w_qkv.reshape(w_qkv.shape[0], -1)
    feats, heads3 = stacked.shape
    heads = w_out.shape[0]
    share = rows // 4

    xt, ut, sums = call(
        partial(prep_kernel, n),
        [((width, rows), BF16), ((width, rows), BF16), ((2 * n, KEEP), F32)],
        smem=(3,), n_in=4,
    )(patches, keep_index, cotangent, live)
    gain_row = jnp.pad(gain, (0, KEEP - width))[None]
    own_gain = jnp.where(jnp.arange(16)[:, None] == me, gain_row, 0.0)
    small = 2 * n + 16
    xg, ug, stats = call(
        gather_kernel,
        [((16, width, rows), BF16), ((16, width, rows), BF16), ((small, KEEP), F32)],
        [
            pltpu.VMEM((8, small, KEEP), F32), pltpu.VMEM((4, small, KEEP), F32),
            DMA((8,)), DMA((8,)), DMA((2,)), DMA((2, 4)), DMA((2, 2)), DMA((2, 8)),
            DMA((16,)), DMA((16,)),
        ],
        cid=1, n_in=3,
    )(xt, ut, jnp.concatenate([sums, own_gain], axis=0))
    x_all = xg.reshape(feats, rows)
    u_all = ug.reshape(feats, rows)
    gain_all = stats[2 * n :, :width].reshape(feats, 1)
    stats = stats[: 2 * n]
    mean = stats[:n].reshape(1, rows) / D
    inv = lax.rsqrt(stats[n:].reshape(1, rows) / D - mean * mean + EPSILON)
    normed_f = (x_all.astype(F32) - mean) * inv * gain_all
    normed = normed_f.astype(BF16)
    qkv_part = dot(stacked, normed, 0, 0).astype(BF16)
    mix_part = dot(w_out, u_all, 1, 0).astype(BF16)
    half = (heads3 + heads) // 2
    d_all, h_all = call(
        middle_kernel,
        [((heads3, rows), BF16), ((heads, rows), BF16)],
        [
            pltpu.VMEM((heads3 + heads, share), BF16), pltpu.VMEM((heads3 + heads, share), BF16),
            pltpu.VMEM((6, half, share), BF16), pltpu.VMEM((6, heads, share), BF16),
            DMA((6,)), DMA((6,)), DMA((6,)), DMA((6,)), DMA((3, 3)), DMA((3, 4)),
        ],
        cid=2, n_in=2,
    )(qkv_part, mix_part)
    attn_part = dot(w_out, h_all, 0, 0).astype(BF16)
    dn_f = dot(stacked, d_all, 1, 0)
    hat = dn_f * gain_all
    cross = dn_f * normed_f
    back = jnp.concatenate(
        [jnp.sum(hat, axis=0).reshape(n, KEEP), jnp.sum(cross, axis=0).reshape(n, KEEP)], axis=0
    )
    dn_part = dn_f.astype(BF16)
    g_qkv = dot(normed, d_all, 1, 1).astype(BF16)
    g_out = dot(h_all, u_all, 1, 1).astype(BF16)
    ndp = 4
    gr, gc = feats // ndp, feats // ndp
    blk = (2, width, rows)
    attn, dn, back, grad_qkv, grad_out = call(
        reduce_kernel,
        [
            ((width, rows), F32), ((width, rows), F32), ((2 * n, KEEP), F32),
            ((gr, heads3), F32), ((heads, gc), F32),
        ],
        [
            pltpu.VMEM((8, 2 * n, KEEP), F32), pltpu.VMEM((4, 2 * n, KEEP), F32),
            pltpu.VMEM((2, 4) + blk, BF16), pltpu.VMEM((2, 3) + blk, BF16),
            pltpu.VMEM((2,) + blk, F32), pltpu.VMEM((2, width, rows), BF16),
            pltpu.VMEM((2, width, rows), BF16),
            pltpu.VMEM((3, gr, heads3), BF16), pltpu.VMEM((3, gr, heads3), BF16),
            pltpu.VMEM((3, heads, gc), BF16), pltpu.VMEM((3, heads, gc), BF16),
            DMA((8,)), DMA((8,)), DMA((2, 4)), DMA((2, 4)), DMA((2, 3)), DMA((2, 3)),
            DMA((2,)), DMA((2,)), DMA((2, 3, 2)), DMA((2, 3, 2)),
        ],
        cid=3, n_in=5, vmem=56,
    )(
        attn_part.reshape(2, 4, 2, width, rows), dn_part.reshape(2, 4, 2, width, rows), back,
        g_qkv.reshape(ndp, gr, heads3), g_out,
    )
    outputs, d_patches, gg = call(
        partial(post_kernel, n),
        [((rows, width), BF16), ((n, patch_count, width), BF16), ((width, KEEP), F32)],
        smem=(5,), n_in=9,
    )(xt, attn, dn, ut, keep_index, live, gain[:, None], stats, back)
    gg = jnp.pad(jnp.sum(gg, axis=1)[None], ((0, 7), (0, KEEP - width)))
    total = call(
        gain_kernel, [((8, KEEP), F32)],
        [pltpu.VMEM((3, 8, KEEP), F32), DMA((3,)), DMA((3,))], cid=4, n_in=1,
    )(gg)[0]
    part = width // ndp
    grad_gain = lax.dynamic_slice(total[0], (lax.axis_index("dp") * part,), (part,))
    return (
        outputs, d_patches, grad_qkv.reshape(gr, 3, heads3 // 3), grad_out, grad_gain
    )


def solution(mesh):
    placed = (
        P("dp", None, ("mcol", "mrow")),
        P("dp", None),
        P(),
        P(("mcol", "mrow")),
        P("mcol", None, "mrow"),
        P("mrow", "mcol"),
        P("dp", ("mcol", "mrow")),
    )
    return jax.shard_map(
        sharded,
        mesh=mesh,
        in_specs=placed,
        out_specs=(
            P("dp", ("mcol", "mrow")),
            P("dp", None, ("mcol", "mrow")),
            P(("mcol", "dp"), None, "mrow"),
            P("mrow", ("mcol", "dp")),
            P(("mcol", "mrow", "dp")),
        ),
        check_vma=False,
    )
```

time: 853 us -> 243 us (0.28)
  blocking collectives: 462 us -> 0 us
  waiting for transfers between devices: 291 us -> 0 us
  Pallas kernels: 0 us -> 177 us
  between operations: 14.9 us -> 0.9 us
  matrix products: 34.2 us -> 24.8 us
    psum x2 -> x0, blocking collectives: 424 us -> none  [feature_sums(): return lax.psum((sum_first, second), ('mrow', 'mcol'))]
    pallas_call x0 -> x6, Pallas kernels: none -> 177 us  [the longest x1 84.6 us: sharded(): call(reduce_kernel, [((width, rows), F32), ((width, rows), F32), ((2 * n,...]
    unnamed x11 -> x0, waiting for transfers between devices: 166 us -> none
    all_gather x3 -> x0, waiting for transfers between devices: 65.5 us -> none  [the longest x2 57.9 us: row_gather(): return lax.all_gather(values, 'mrow', axis=1, tiled=True)]
    reduce_scatter x4 -> x0, waiting for transfers between devices: 59.7 us -> none  [the longest x2 59.7 us: column_sum(): lax.psum_scatter(term_maker(jnp.int32(0), lax.axis_size('mcol') * shard_r...]
    unnamed x1 -> x0, blocking collectives: 24.7 us -> none
    all_gather x1 -> x0, blocking collectives: 13.4 us -> none  [column_gather(): return lax.all_gather(values, 'mcol', axis=0, tiled=True)]
    convert_element_type x5 -> x3, local copies, waits for them, and re-layouts: 3.08 us -> 14.7 us  [the longest x1 5.4 us: sharded(): normed_f = (x_all.astype(F32) - mean) * inv * gain_all]
  transfers between devices with their start and end apart: 9 -> 0, of which waited for: 6 -> 0; matrix products, arithmetic and copies ran while one was open for 8% -> 0% of each run, Pallas kernels for 0% -> 0%
where the time goes in v1:
time: 243 us; the launch traced here: 240 us
  Pallas kernels  177 us (73%)
  local copies, waits for them, and re-layouts  31.4 us (13%)
  matrix products  24.8 us (10%)
  other arithmetic  6.18 us (3%)
    pallas_call x1, Pallas kernels, sharded(): call(reduce_kernel, [((width, rows), F32), ((width, rows), F32), ((2 * n,...  84.6 us
    pallas_call x1, Pallas kernels, sharded(): call(middle_kernel, [((heads3, rows), BF16), ((heads, rows), BF16)], [plt...  43.3 us
    pallas_call x1, Pallas kernels, sharded(): call(gather_kernel, [((16, width, rows), BF16), ((16, width, rows), BF16)...  41 us
    dot_general x6, matrix products, dot(): lax.dot_general(a, b, (((ca,), (cb,)), ((), ())), preferred_element_type=...  24.8 us
    unnamed x29, local copies, waits for them, and re-layouts  12.3 us
    pallas_call x1, Pallas kernels, sharded(): call(gain_kernel, [((8, KEEP), F32)], [pltpu.VMEM((3, 8, KEEP), F32), DMA...  5.64 us
    convert_element_type x1, local copies, waits for them, and re-layouts, sharded(): normed_f = (x_all.astype(F32) - mean) * inv * gain_all  5.4 us

profile of v1, /device:TPU:0, one launch (start us, length us, event | category | flops | bytes accessed | tf_op | source)
XLA Modules:
  0.0 239.8 jit_solution(18084263231027842833)
XLA Ops:
  0.6 0.0 copy-start
  0.7 1.3 dynamic_slice.8
  2.0 0.6 compare_convert_fusion.live_ref
  2.6 1.3 copy.23.p_ref
  3.9 1.1 copy.24.c_ref
  5.0 0.0 copy-start.4
  5.0 0.7 copy-done.4
  5.7 0.9 shard_map.110
  6.6 0.7 pad.8
  7.3 0.1 broadcast_select_fusion
  7.4 41.0 %shard_map.111 = (bf16[16,96,1024]{2,1,0:T(8,128)(2,1)S(1)}, bf16[16,96,1024]{2,1,0:T(8,128)(2,1)}, f32[32,128]{1,0:T(8,128)S(1)}) custom-call(bf16[96,1024]{1,0:T(8,128)(2,1)S(1)} %get-tuple-element.21.x_ref, bf16[96,1024]{1,0:T(8,128)(2,1)S(1)} %get-tuple-element.22.u_ref, f32[32,128]{1,0:T(8,128)S(1)} %pad_maximum_fusion.s_ref), custom_call_target="tpu_custom_call" | custom-call | tf_op jit(solution)/shard_map/pallas_call | solution.py:619
  48.4 0.0 copy-start.1
  48.4 2.6 %multiply_convert_fusion = bf16[16,96,1024]{2,1,0:T(8,128)(2,1)} fusion(f32[16,96]{1,0:T(8,128)S(1)} %slice.19, f32[1024]{0:T(1024)S(1)} %fusion.11, f32[1024]{0:T(1024)S(1)} %multiply_bitcast_fusion, bf16[16,96,1024]{2,1,0:T(8,128)(2,1)S(1)} %get-tuple-element.24), kind=kLoop, calls=%fused_computation.6 | loop fusion | flops 7864320 | bytes 6305792 | tf_op jit(solution)/shard_map/convert_element_type | solution.py:636
  51.1 0.0 copy-done.1
  51.1 4.3 %copy.25 = bf16[1536,3,256]{0,2,1:T(8,128)(2,1)} copy(bf16[1536,3,256]{2,0,1:T(8,128)(2,1)} %param.11) | data formatting | bytes 4718592 | tf_op args[4]
  55.3 0.0 copy-start.10
  55.3 5.3 %fusion.8.q_ref = bf16[768,1024]{1,0:T(8,128)(2,1)S(1)} fusion(bf16[1536,768]{0,1:T(8,128)(2,1)} %bitcast.56, bf16[1536,1024]{1,0:T(8,128)(2,1)} %bitcast.55), kind=kOutput, calls=%fused_computation.16 | convolution fusion | flops 2416705536 | bytes 7077888 | tf_op jit(solution)/shard_map/dot_general | solution.py:24
  60.7 0.0 copy-done
  60.7 0.0 copy-done.10
  60.7 1.0 fusion.9.m_ref
  61.8 43.3 %shard_map.112 = (bf16[768,1024]{1,0:T(8,128)(2,1)S(1)}, bf16[256,1024]{1,0:T(8,128)(2,1)S(1)}) custom-call(bf16[768,1024]{1,0:T(8,128)(2,1)S(1)} %fusion.8.q_ref, bf16[256,1024]{1,0:T(8,128)(2,1)S(1)} %fusion.9.m_ref), custom_call_target="tpu_custom_call" | custom-call | tf_op jit(solution)/shard_map/pallas_call | solution.py:640
  105.1 0.1 mul.53
  105.2 5.4 %copy.30 = f32[1536,1024]{0,1:T(8,128)} copy(bf16[1536,1024]{1,0:T(8,128)(2,1)} %bitcast.51) | data formatting | bytes 9437184 | tf_op jit(solution)/shard_map/convert_element_type | solution.py:635
  110.6 0.0 copy-start.8
  110.6 7.5 %convolution_convert_fusion.1 = bf16[1536,768]{1,0:T(8,128)(2,1)} fusion(bf16[768,1024]{1,0:T(8,128)(2,1)S(1)} %get-tuple-element.28, f32[1536,1024]{0,1:T(8,128)} %copy.30, f32[1024]{0:T(1024)S(1)} %fusion.11, f32[1024]{0:T(1024)S(1)} %multiply_bitcast_fusion, f32[1536]{0:T(1024)S(1)} %mul.53), kind=kOutput, calls=%fused_computation.9 | convolution fusion | flops 2423390208 | bytes 10237952 | tf_op jit(solution)/shard_map/dot_general | solution.py:24
  118.1 0.0 copy-done.8
  118.1 0.0 copy-start.7
  118.1 4.3 %bitcast_convert_fusion = (bf16[1536,1024]{0,1:T(8,128)(2,1)}, f32[1024,1536]{1,0:T(8,128)S(1)}) fusion(bf16[768,1024]{1,0:T(8,128)(2,1)S(1)} %get-tuple-element.28, bf16[1536,768]{0,1:T(8,128)(2,1)S(1)} %bitcast.57), kind=kOutput, calls=%fused_computation.2 | convolution fusion | flops 2417491968 | bytes 13369344 | tf_op jit(solution)/shard_map/dot_general | solution.py:24
  122.4 0.0 copy-done.7
  122.4 2.1 fusion
  124.5 0.6 pad_maximum_fusion.1.s_ref
  125.1 4.6 %copy.29 = bf16[1536,1024]{1,0:T(8,128)(2,1)} copy(bf16[1536,1024]{0,1:T(8,128)(2,1)} %get-tuple-element.49) | data formatting | bytes 6291456 | tf_op jit(solution)/shard_map/convert_element_type | solution.py:657
  129.8 3.8 %convolution_convert_fusion.2.o_ref = bf16[256,1536]{1,0:T(8,128)(2,1)} fusion(bf16[256,1024]{1,0:T(8,128)(2,1)S(1)} %get-tuple-element.27, bf16[1536,1024]{1,0:T(8,128)(2,1)} %bitcast.63), kind=kOutput, calls=%fused_computation.14 | convolution fusion | flops 805699584 | bytes 4456448 | tf_op jit(solution)/shard_map/dot_general | solution.py:24
  133.6 2.7 %fusion.3 = bf16[1536,1024]{0,1:T(8,128)(2,1)} fusion(bf16[256,1024]{1,0:T(8,128)(2,1)S(1)} %get-tuple-element.27, bf16[256,1536]{1,0:T(8,128)(2,1)S(1)} %copy-done), kind=kOutput, calls=%fused_computation.10 | convolution fusion | flops 806879232 | bytes 4456448 | tf_op jit(solution)/shard_map/dot_general | solution.py:24
  136.3 4.6 %copy.28 = bf16[1536,1024]{1,0:T(8,128)(2,1)} copy(bf16[1536,1024]{0,1:T(8,128)(2,1)} %fusion.3) | data formatting | bytes 6291456 | tf_op jit(solution)/shard_map/convert_element_type | solution.py:650
  141.0 84.6 %shard_map.113 = (f32[96,1024]{1,0:T(8,128)}, f32[96,1024]{1,0:T(8,128)}, f32[16,128]{1,0:T(8,128)}, f32[384,768]{1,0:T(8,128)}, f32[256,384]{1,0:T(8,128)}) custom-call(bf16[2,4,2,96,1024]{4,3,2,1,0:T(8,128)(2,1)} %bitcast.53, bf16[2,4,2,96,1024]{4,3,2,1,0:T(8,128)(2,1)} %bitcast.52, f32[16,128]{1,0:T(8,128)} %pad_maximum_fusion.1.s_ref, ...), custom_call_target="tpu_custom_call" | custom-call | tf_op jit(solution)/shard_map/pallas_call | solution.py:663
  225.5 0.0 copy-start.9
  225.5 0.0 copy-start.2
  225.5 0.0 copy-start.3
  225.5 0.0 copy-start.5
  225.6 0.0 copy-start.6
  225.6 1.7 copy.32
  227.3 1.4 copy.35
  228.7 0.0 copy-done.9
  228.7 0.1 copy.31.g_ref
  228.8 0.0 copy-done.2
  228.8 0.0 copy-done.3
  228.8 0.0 copy-done.5
  228.8 0.0 copy-done.6
  228.8 1.1 shard_map.114
  229.9 1.0 copy.34
  230.9 0.8 copy.33
  231.7 0.1 reduce_sum.29
  231.8 5.6 %shard_map.115 = f32[8,128]{1,0:T(8,128)S(1)} custom-call(f32[8,128]{1,0:T(8,128)S(1)} %pad.9.g_ref), custom_call_target="tpu_custom_call" | custom-call | tf_op jit(solution)/shard_map/pallas_call | solution.py:690
  237.5 0.6 dynamic-slice_bitcast_fusion
  238.0 1.8 copy.39
  (8 shorter events, 0.0 us)
Async XLA Ops:
  0.6 60.1 %copy-start = (bf16[256,1536]{1,0:T(8,128)(2,1)S(1)}, bf16[256,1536]{1,0:T(8,128)(2,1)}, u32[]{:S(2)}) copy-start(bf16[256,1536]{1,0:T(8,128)(2,1)} %param.12) | copy-start | bytes 2359300
  5.0 0.7 copy-start.4
  48.4 2.7 %copy-start.1 = (bf16[16,96,1024]{2,1,0:T(8,128)(2,1)}, bf16[16,96,1024]{2,1,0:T(8,128)(2,1)S(1)}, u32[]{:S(2)}) copy-start(bf16[16,96,1024]{2,1,0:T(8,128)(2,1)S(1)} %get-tuple-element.24) | copy-start | bytes 9437188
  55.3 5.4 %copy-start.10 = (bf16[16,96,1024]{2,1,0:T(8,128)(2,1)S(1)}, bf16[16,96,1024]{2,1,0:T(8,128)(2,1)}, u32[]{:S(2)}) copy-start(bf16[16,96,1024]{2,1,0:T(8,128)(2,1)} %get-tuple-element.26) | copy-start | bytes 9437188
  110.6 7.5 %copy-start.8 = (bf16[1536,3,256]{0,2,1:T(8,128)(2,1)S(1)}, bf16[1536,3,256]{0,2,1:T(8,128)(2,1)}, u32[]{:S(2)}) copy-start(bf16[1536,3,256]{0,2,1:T(8,128)(2,1)} %copy.25) | copy-start | bytes 7077892
  118.1 4.3 %copy-start.7 = (f32[1536,1024]{0,1:T(8,128)S(1)}, f32[1536,1024]{0,1:T(8,128)}, u32[]{:S(2)}) copy-start(f32[1536,1024]{0,1:T(8,128)} %copy.30) | copy-start | bytes 18874372
  225.5 3.2 %copy-start.9 = (f32[96]{0:T(128)S(1)}, f32[96]{0:T(128)}, u32[]{:S(2)}) copy-start(f32[96]{0:T(128)} %param.10) | copy-start | bytes 1156
  225.5 3.2 %copy-start.2 = (f32[96,1024]{1,0:T(8,128)S(1)}, f32[96,1024]{1,0:T(8,128)}, u32[]{:S(2)}) copy-start(f32[96,1024]{1,0:T(8,128)} %get-tuple-element.29.a_ref) | copy-start | bytes 1179652
  225.5 3.2 %copy-start.3 = (f32[96,1024]{1,0:T(8,128)S(1)}, f32[96,1024]{1,0:T(8,128)}, u32[]{:S(2)}) copy-start(f32[96,1024]{1,0:T(8,128)} %get-tuple-element.30.d_ref) | copy-start | bytes 1179652
  225.5 3.2 %copy-start.5 = (s32[8,128]{1,0:T(8,128)S(1)}, s32[8,128]{1,0:T(8,128)}, u32[]{:S(2)}) copy-start(s32[8,128]{1,0:T(8,128)} %k_ref.3) | copy-start | bytes 12292
  225.6 3.2 %copy-start.6 = (f32[16,128]{1,0:T(8,128)S(1)}, f32[16,128]{1,0:T(8,128)}, u32[]{:S(2)}) copy-start(f32[16,128]{1,0:T(8,128)} %get-tuple-element.31.bt_ref) | copy-start | bytes 24580

commit v2 on v0

v2 whole, which is shorter than its diff:
```python
from functools import partial

import jax
import jax.numpy as jnp
from jax import lax
from jax.experimental import pallas as pl
from jax.experimental.pallas import tpu as pltpu
from jax.sharding import PartitionSpec as P

D = 6144
HD = 128
KEEP = 128
SLOTS = 4
SPARE = 6
CHUNKS = 3
EPSILON = 1e-06

F32 = jnp.float32
BF16 = jnp.bfloat16
MESH = pl.DeviceIdType.MESH
VM = pl.BlockSpec(memory_space=pltpu.VMEM)
SM = pl.BlockSpec(memory_space=pltpu.SMEM)
DMA = pltpu.SemaphoreType.DMA


def dot(a, b, ca, cb):
    return lax.dot_general(a, b, (((ca,), (cb,)), ((), ())), preferred_element_type=F32)


def remote(src, dst, send, recv, where):
    return pltpu.make_async_remote_copy(
        src_ref=src, dst_ref=dst, send_sem=send, recv_sem=recv, device_id=where, device_id_type=MESH
    )


def clamp(value, top):
    return jnp.minimum(jnp.maximum(value, 0), top)


def greet(peers):
    barrier = pltpu.get_barrier_semaphore()
    for peer in peers:
        pl.semaphore_signal(barrier, inc=1, device_id=peer, device_id_type=MESH)
    pl.semaphore_wait(barrier, len(peers))


def span(start, size, step=None):
    return pl.ds(pl.multiple_of(start, step or size), size)


class Place:
    def __init__(self):
        self.me = lax.axis_index("mrow")
        self.core = lax.rem(self.me, 2)
        self.y = lax.rem(lax.div(self.me, 2), 4)
        self.zh = lax.div(self.me, 8)
        self.x = lax.axis_index("mcol")
        self.dp = lax.axis_index("dp")
        self.sib = self.at(self.zh, 0, 1 - self.core)
        self.anti = self.at(1 - self.zh, 0, self.core)
        self.ys = [self.at(self.zh, d, self.core) for d in range(4)]
        self.xs = [lax.rem(self.x + d, 4) for d in range(4)]
        self.dps = [lax.rem(self.dp + d, 4) for d in range(4)]

    def at(self, zh, dy, core):
        return zh * 8 + lax.rem(self.y + dy, 4) * 2 + core

    def peers(self):
        rows = [self.sib, self.anti] + self.ys[1:]
        return (
            [{"mrow": r} for r in rows]
            + [{"mcol": c} for c in self.xs[1:]]
            + [{"dp": c} for c in self.dps[1:]]
        )


class Share:
    def __init__(self, counts, dp):
        c = [counts[g] for g in range(4)]
        keep = [jnp.minimum(v, SLOTS) for v in c]
        zero = jnp.int32(0)
        self.own = self.extra = self.spare_at = self.free = self.free_at = zero
        spare_at = free_at = zero
        for g in range(4):
            here = dp == g
            spare, free = c[g] - keep[g], SLOTS - keep[g]
            self.own = jnp.where(here, keep[g], self.own)
            self.extra = jnp.where(here, spare, self.extra)
            self.free = jnp.where(here, free, self.free)
            self.spare_at = jnp.where(here, spare_at, self.spare_at)
            self.free_at = jnp.where(here, free_at, self.free_at)
            spare_at, free_at = spare_at + spare, free_at + free

    def sent(self, slot):
        k = slot - self.spare_at
        return (k >= 0) & (k < self.extra), clamp(SLOTS + k, 2 * SLOTS - 1)

    def taken(self, position):
        return position < self.own, clamp(self.free_at + position - self.own, SPARE - 1)


class SmallSum:
    def __init__(self, place, val, box, send, recv, x_rows):
        self.place, self.val, self.box = place, val, box
        self.send, self.recv, self.x_rows = send, recv, x_rows
        self.live = []
        self.n = 0

    def push(self, peers, rows=None):
        self.live = []
        for where in peers:
            k = self.n
            self.n += 1
            stage = self.val.at[self.stage]
            box = self.box.at[k]
            if rows is not None:
                stage, box = stage.at[:rows], box.at[:rows]
            c = remote(stage, box, self.send.at[k], self.recv.at[k], where)
            c.start()
            self.live.append((k, c))

    def start(self, value):
        self.stage = 0
        self.val[0] = value
        self.push([{"mrow": self.place.sib}])

    def step(self):
        total = self.val[self.stage]
        rows = self.x_rows if self.stage == 3 else total.shape[0]
        total = total[:rows]
        for k, c in self.live:
            c.wait()
            total = total + self.box[k, :rows]
        self.stage += 1
        if self.stage < 4:
            self.val[self.stage] = total
        if self.stage == 1:
            self.push([{"mrow": r} for r in self.place.ys[1:]])
        elif self.stage == 2:
            self.push([{"mrow": self.place.anti}])
        elif self.stage == 3:
            self.push([{"mcol": c} for c in self.place.xs[1:]], self.x_rows)
        return total


class Chain:
    def __init__(self, place, own, got, fwd, send, recv):
        self.dp, self.own, self.got, self.fwd, self.send, self.recv = place.dp, own, got, fwd, send, recv
        self.near = [{"dp": place.dps[1]}, {"dp": place.dps[3]}]
        self.width = own.shape[2] // CHUNKS

    def lanes(self, ch):
        return pl.ds(ch * self.width, self.width)

    def copy(self, way, ch, first):
        src = self.own if first else self.fwd.at[way]
        return remote(
            src.at[:, :, self.lanes(ch)], self.got.at[way, :, :, self.lanes(ch)],
            self.send.at[way, ch], self.recv.at[way, ch], self.near[way],
        )

    def forward(self, way, ch):
        self.copy(way, ch, False).wait_recv()
        here = self.lanes(ch)
        self.fwd[way, :, :, here] = (
            self.got[way, :, :, here].astype(F32) + self.own[:, :, here].astype(F32)
        ).astype(BF16)
        self.copy(way, ch, False).start()

    def start(self):
        for dp, way in ((0, 0), (3, 1)):
            @pl.when(self.dp == dp)
            def _():
                for ch in range(CHUNKS):
                    self.copy(way, ch, True).start()
                self.got[way] = jnp.zeros(self.got.shape[1:], BF16)

    def run(self):
        for dp, way in ((1, 0), (2, 1)):
            @pl.when(self.dp == dp)
            def _():
                for w, ch in ((way, 0), (way, 1), (1 - way, 0), (way, 2), (1 - way, 1), (1 - way, 2)):
                    self.forward(w, ch)
        for dp, way in ((0, 1), (3, 0)):
            @pl.when(self.dp == dp)
            def _():
                for ch in range(CHUNKS):
                    self.copy(way, ch, False).wait_recv()
        for way, last in ((0, 3), (1, 0)):
            @pl.when(self.dp != last)
            def _():
                for ch in range(CHUNKS):
                    self.copy(way, ch, False).wait_send()

    def slot(self, a, s):
        here = slice(s * KEEP, (s + 1) * KEEP)
        return (
            self.own[a, :, here].astype(F32)
            + self.got[0, a, :, here].astype(F32)
            + self.got[1, a, :, here].astype(F32)
        )


def attend(q, k, v, do):
    def norm(t):
        c = t - jnp.mean(t, axis=0, keepdims=True)
        i = lax.rsqrt(jnp.mean(c * c, axis=0, keepdims=True) + EPSILON)
        return c * i, i

    def norm_back(d, y, i):
        return i * (
            d - jnp.mean(d, axis=0, keepdims=True) - y * jnp.mean(d * y, axis=0, keepdims=True)
        )

    def mm(a, b, ca, cb):
        return lax.dot_general(
            a, b, (((ca,), (cb,)), ((), ())), preferred_element_type=F32, precision=lax.Precision.HIGHEST
        )

    scale = HD ** (-0.5)
    qn, iq = norm(q)
    kn, ik = norm(k)
    w = jnp.exp(mm(kn, qn, 0, 0) * scale)
    w = w / jnp.sum(w, axis=0, keepdims=True)
    out = mm(v, w, 1, 0)
    dw = mm(v, do, 0, 0)
    ds = w * (dw - jnp.sum(w * dw, axis=0, keepdims=True)) * scale
    dv = mm(do, w, 1, 1)
    dq = norm_back(mm(kn, ds, 1, 0), qn, iq)
    dk = norm_back(mm(qn, ds, 1, 1), kn, ik)
    return out, dq, dk, dv


def gather_rows(place, locs, alls, small, zsend, ysend, fsend, csend, recv, meanwhile):
    width = locs[0].shape[0]
    me, sib, core = place.me, {"mrow": place.sib}, place.core
    right, left = {"mrow": place.ys[1]}, {"mrow": place.ys[3]}
    sends = []
    ncore = [0]

    def there(a, slot):
        return alls[a].at[span(slot * width, width)]

    def push(a, src, slot, sem, where):
        c = remote(src, there(a, slot), sem, recv.at[a, slot], where)
        c.start()
        sends.append(c)

    def got(a, slot):
        remote(locs[a], there(a, slot), zsend.at[0], recv.at[a, slot], sib).wait_recv()

    def to_sib(slot):
        for a in range(2):
            push(a, there(a, slot), slot, csend.at[a, ncore[0]], sib)
        ncore[0] += 1

    for a in range(2):
        push(a, locs[a], me, zsend.at[a], {"mrow": place.anti})
    for a in range(2):
        push(a, locs[a], me, ysend.at[a, 0], right)
        push(a, locs[a], me, ysend.at[a, 1], left)
    for a in range(2):
        push(a, locs[a], me, csend.at[a, 0], sib)
    ncore[0] = 1
    for a in range(2):
        alls[a][span(me * width, width)] = locs[a][...]
    small.step()
    meanwhile()
    anti = place.anti
    for a in range(2):
        got(a, anti)
        push(a, there(a, anti), anti, ysend.at[a, 2], right)
        push(a, there(a, anti), anti, ysend.at[a, 3], left)
    to_sib(anti)
    small.step()
    for half, zh in enumerate((place.zh, 1 - place.zh)):
        before, after = place.at(zh, 3, core), place.at(zh, 1, core)
        got(0, before)
        push(0, there(0, before), before, fsend.at[0, half], right)
        got(1, after)
        push(1, there(1, after), after, fsend.at[1, half], left)
        got(1, before)
        to_sib(before)
        got(0, after)
        to_sib(after)
        if half == 0:
            small.step()
    for zh in (place.zh, 1 - place.zh):
        far = place.at(zh, 2, core)
        got(0, far)
        got(1, far)
        to_sib(far)
    total = small.step()
    for zh in range(2):
        for dy in range(4):
            for a in range(2):
                got(a, place.at(zh, dy, 1 - core))
    for c in sends:
        c.wait_send()
    return total


def middle(place, q_ref, m_ref, dall, hall, work, own, bq, bm, sq, sm, rq, rm, gs, gr):
    x, xs = place.x, place.xs
    right, left = {"mcol": xs[1]}, {"mcol": xs[3]}
    width = own.shape[1]
    qrows = q_ref.shape[0]
    half = own.shape[0] // 2
    mrows = m_ref.shape[0]
    qminus = qrows - half

    def lanes(block):
        return span(block * width, width)

    sends = []

    def push_plus(src, slot, where):
        c = remote(src, bq.at[slot], sq.at[slot], rq.at[slot], where)
        c.start()
        sends.append(c)

    def push_minus(srcq, srcm, slot, where):
        c = remote(srcq, bq.at[slot, :qminus], sq.at[slot], rq.at[slot], where)
        d = remote(srcm, bm.at[slot], sm.at[slot], rm.at[slot], where)
        c.start()
        d.start()
        sends.extend((c, d))

    def got_plus(slot):
        remote(bq.at[slot], bq.at[slot], sq.at[slot], rq.at[slot], right).wait_recv()

    def got_minus(slot):
        remote(bq.at[slot, :qminus], bq.at[slot, :qminus], sq.at[slot], rq.at[slot], right).wait_recv()
        remote(bm.at[slot], bm.at[slot], sm.at[slot], rm.at[slot], right).wait_recv()

    plus, minus = pl.ds(0, half), pl.ds(half, qminus)
    push_plus(q_ref.at[plus, lanes(xs[2])], 0, right)
    push_minus(q_ref.at[minus, lanes(xs[2])], m_ref.at[:, lanes(xs[2])], 1, left)
    push_plus(q_ref.at[plus, lanes(xs[3])], 2, left)
    push_minus(q_ref.at[minus, lanes(xs[1])], m_ref.at[:, lanes(xs[1])], 3, right)
    got_plus(0)
    work[:half] = (bq[0].astype(F32) + q_ref[plus, lanes(xs[1])].astype(F32)).astype(BF16)
    push_plus(work.at[:half], 4, right)
    got_minus(1)
    work[half:qrows] = (
        bq[1, :qminus].astype(F32) + q_ref[minus, lanes(xs[3])].astype(F32)
    ).astype(BF16)
    work[qrows:] = (bm[1].astype(F32) + m_ref[:, lanes(xs[3])].astype(F32)).astype(BF16)
    push_minus(work.at[half:qrows], work.at[qrows:], 5, left)
    got_plus(2)
    got_minus(3)
    got_plus(4)
    got_minus(5)
    heads = mrows // HD

    def total(r0):
        cols = lanes(x)
        if r0 < half:
            parts = q_ref[r0 : r0 + HD, cols], bq[2, r0 : r0 + HD], bq[4, r0 : r0 + HD]
        elif r0 < qrows:
            b = slice(r0 - half, r0 - half + HD)
            parts = q_ref[r0 : r0 + HD, cols], bq[3, b], bq[5, b]
        else:
            b = slice(r0 - qrows, r0 - qrows + HD)
            parts = m_ref[b, cols], bm[3, b], bm[5, b]
        return parts[0].astype(F32) + parts[1].astype(F32) + parts[2].astype(F32)

    for h in range(heads):
        q, k, v, do = (total((part * heads + h) * HD) for part in range(4))
        out, dq, dk, dv = attend(q, k, v, do)
        for part, value in enumerate((dq, dk, dv, out)):
            r0 = (part * heads + h) * HD
            own[r0 : r0 + HD] = value.astype(BF16)

    dst = (
        (dall, pl.ds(0, half), pl.ds(0, half)),
        (dall, pl.ds(half, qminus), pl.ds(half, qminus)),
        (hall, pl.ds(qrows, mrows), pl.ds(0, mrows)),
    )

    def push_part(p, block, src, k, where):
        out, _, rows = dst[p]
        c = remote(src, out.at[rows, lanes(block)], gs.at[p, k], gr.at[p, block], where)
        c.start()
        sends.append(c)

    def got_part(p, block):
        out, rows_own, rows = dst[p]
        remote(
            own.at[rows_own], out.at[rows, lanes(block)], gs.at[p, 0], gr.at[p, block], right
        ).wait_recv()

    for p in range(3):
        for k, where in enumerate((right, left)):
            push_part(p, x, own.at[dst[p][1]], k, where)
    dall[:, lanes(x)] = own[:qrows]
    hall[:, lanes(x)] = own[qrows:]
    got_part(0, xs[3])
    push_part(0, xs[3], dall.at[dst[0][2], lanes(xs[3])], 2, right)
    for p in (1, 2):
        got_part(p, xs[1])
        out = dst[p][0]
        push_part(p, xs[1], out.at[dst[p][2], lanes(xs[1])], 2, left)
    got_part(1, xs[3])
    got_part(2, xs[3])
    got_part(0, xs[1])
    for p in range(3):
        got_part(p, xs[2])
    for c in sends:
        c.wait_send()


class Line:
    def __init__(self, place, owns, bufs, send, recv):
        self.dp, self.owns, self.bufs, self.send, self.recv = place.dp, owns, bufs, send, recv
        self.near = [{"dp": place.dps[1]}, {"dp": place.dps[3]}]

    def copies(self, way, t, own):
        slot = t - 1 if way == 0 else t
        return [
            remote(
                o.at[t] if own else b.at[way, slot], b.at[way, slot],
                self.send.at[way, slot, i], self.recv.at[way, slot, i], self.near[way],
            )
            for i, (o, b) in enumerate(zip(self.owns, self.bufs))
        ]

    def start(self):
        for dp, way, blocks in ((0, 0, (3, 2, 1)), (3, 1, (0, 1, 2))):
            @pl.when(self.dp == dp)
            def _():
                for t in blocks:
                    for c in self.copies(way, t, True):
                        c.start()

    def forward(self, way, t):
        slot = t - 1 if way == 0 else t
        for c in self.copies(way, t, False):
            c.wait_recv()
        for o, b in zip(self.owns, self.bufs):
            add_blocks(b.at[way, slot], o.at[t])
        for c in self.copies(way, t, False):
            c.start()

    def turn(self, n):
        for dp, todo in (
            (1, ([(0, 3)], [(0, 2), (1, 0)])[n]),
            (2, ([(1, 0)], [(1, 1), (0, 3)])[n]),
        ):
            @pl.when(self.dp == dp)
            def _():
                for way, t in todo:
                    self.forward(way, t)

    def finish(self, outs):
        dp = self.dp

        def add(way, first):
            for c in self.copies(way, dp, False):
                c.wait_recv()
            slot = dp - 1 if way == 0 else dp
            for o, b, out in zip(self.owns, self.bufs, outs):
                add_blocks(out, b.at[way, slot], o.at[dp] if first else out)

        @pl.when(dp == 0)
        def _():
            add(1, True)

        @pl.when(dp > 0)
        def _():
            add(0, True)

        @pl.when((dp > 0) & (dp < 3))
        def _():
            add(1, False)

        for t in range(1, 4):
            @pl.when(dp < t)
            def _():
                for c in self.copies(0, t, False):
                    c.wait_send()
        for t in range(3):
            @pl.when(dp > t)
            def _():
                for c in self.copies(1, t, False):
                    c.wait_send()


def add_blocks(out, *srcs):
    if len(srcs) == 1:
        srcs = (out,) + srcs
    for p in range(out.shape[0]):
        @pl.loop(0, out.shape[1] // 16)
        def _(i):
            r = span(i * 16, 16)
            total = srcs[0][p, r].astype(F32)
            for s in srcs[1:]:
                total = total + s[p, r].astype(F32)
            out[p, r] = total.astype(out.dtype)


def prep_kernel(counts, p_ref, k_ref, c_ref, own, spare, sel):
    share = Share(counts, lax.axis_index("dp"))
    patch = lax.broadcasted_iota(jnp.int32, (p_ref.shape[2], KEEP), 0)

    def put(out, place, img, mine):
        flag = jnp.where(mine, 1.0, 0.0)
        here = slice(place * KEEP, (place + 1) * KEEP)
        pick = (patch == k_ref[pl.ds(img, 1), :]).astype(F32).astype(BF16)
        out[0, :, here] = (dot(p_ref[img], pick, 1, 0) * flag).astype(BF16)
        out[1, :, here] = (c_ref[:, span(img * KEEP, KEEP)].astype(F32) * flag).astype(BF16)

    for j in range(SLOTS):
        put(own, j, j, j < share.own)
    for s in range(SPARE):
        mine, img = share.sent(s)
        put(spare, s, img, mine)
    for j in range(SLOTS):
        keep, slot = share.taken(j)
        for s in range(SPARE):
            flag = jnp.where((slot == s) & jnp.logical_not(keep), 1.0, 0.0)
            sel[j * SPARE + s : j * SPARE + s + 1, :] = jnp.zeros((1, KEEP), F32) + flag


def main_kernel(
    first, sp_own, sel, g_ref, w_ref, wo_ref,
    out_own, out_buf, out_got, gq_out, go_out, gain_out,
    x_loc, u_loc, x_all, u_all, normed, wt, wot,
    sp_got, sp_fwd, rt_fwd,
    box1, val1, box2, val2,
    q_part, m_part, d_all, h_all, work, own, bq, bm,
    a_part, n_part, cbox, ybuf, ysum, ztot, zbox,
    gq, go, gq_buf, go_buf, gbox, gval,
    s1s, s1r, s2s, s2r, zs1, ys1, fs1, cs1, r1,
    sps, spr, rts, rtr,
    sq, sm, rq, rm, gs, gr,
    cs2, cr2, ys2, yr2, zs2, zr2, lns, lnr, ggs, ggr,
):
    place = Place()
    greet(place.peers())
    width = x_loc.shape[0]
    core, zh = place.core, place.zh
    chain = Chain(place, sp_own, sp_got, sp_fwd, sps, spr)
    chain.start()
    chain.run()
    spare = [[chain.slot(a, s) for s in range(SPARE)] for a in range(2)]
    sums, squares = [], []
    for j in range(SLOTS):
        here = slice(j * KEEP, (j + 1) * KEEP)
        values = []
        for a, loc in enumerate((x_loc, u_loc)):
            v = first[a, :, here].astype(F32)
            for s in range(SPARE):
                v = v + spare[a][s] * sel[j * SPARE + s : j * SPARE + s + 1, :]
            loc[:, here] = v.astype(BF16)
            values.append(v)
        sums.append(jnp.sum(values[0], axis=0, keepdims=True))
        squares.append(jnp.sum(values[0] * values[0], axis=0, keepdims=True))
    me_row = lax.broadcasted_iota(jnp.int32, (16, KEEP), 0) == place.me
    own_gain = jnp.where(me_row, g_ref[...], 0.0)

    small = SmallSum(place, val1, box1, s1s, s1r, 2 * SLOTS)
    small.start(jnp.concatenate(sums + squares + [own_gain], axis=0))

    def turn_weights():
        for p in range(3):
            wt[p] = jnp.transpose(w_ref[p])
        wot[...] = jnp.transpose(wo_ref[...])

    stats = gather_rows(
        place, (x_loc, u_loc), (x_all, u_all), small, zs1, ys1, fs1, cs1, r1, turn_weights
    )
    gain_cols = jnp.transpose(
        jnp.concatenate([val1[3, 2 * SLOTS :], jnp.zeros((KEEP - 16, KEEP), F32)], axis=0)
    )
    mean = stats[:SLOTS] * (1.0 / D)
    inv = lax.rsqrt(stats[SLOTS:] * (1.0 / D) - mean * mean + EPSILON)
    for b in range(16):
        rb = slice(b * width, (b + 1) * width)
        col = gain_cols[:width, b : b + 1]
        for j in range(SLOTS):
            here = slice(j * KEEP, (j + 1) * KEEP)
            centred = (x_all[rb, here].astype(F32) - mean[j : j + 1]) * inv[j : j + 1]
            normed[rb, here] = (centred * col).astype(BF16)

    part = w_ref.shape[2]
    for p in range(3):
        q_part[p * part : (p + 1) * part] = dot(wt[p], normed[...], 1, 0).astype(BF16)
    m_part[...] = dot(wo_ref[...], u_all[...], 1, 0).astype(BF16)

    middle(place, q_part, m_part, d_all, h_all, work, own, bq, bm, sq, sm, rq, rm, gs, gr)

    hat = [jnp.zeros((8, KEEP), F32) for _ in range(SLOTS)]
    cross = [jnp.zeros((8, KEEP), F32) for _ in range(SLOTS)]
    feats = normed.shape[0]
    block = 2 * width
    for b in range(feats // block):
        rb = slice(b * block, (b + 1) * block)
        a_part[rb] = dot(wot[rb], h_all[...], 1, 0).astype(BF16)
        dn = dot(w_ref[0, rb], d_all[:part], 1, 0)
        for p in (1, 2):
            dn = dn + dot(w_ref[p, rb], d_all[p * part : (p + 1) * part], 1, 0)
        n_part[rb] = dn.astype(BF16)
        for i in range(2):
            col = gain_cols[:width, 2 * b + i : 2 * b + i + 1]
            ri = slice(i * width, (i + 1) * width)
            ra = slice((2 * b + i) * width, (2 * b + i + 1) * width)
            for j in range(SLOTS):
                here = slice(j * KEEP, (j + 1) * KEEP)
                d_hat = dn[ri, here] * col
                centred = (x_all[ra, here].astype(F32) - mean[j : j + 1]) * inv[j : j + 1]
                hat[j] = hat[j] + jnp.sum(d_hat.reshape(-1, 8, KEEP), axis=0)
                cross[j] = cross[j] + jnp.sum((d_hat * centred).reshape(-1, 8, KEEP), axis=0)
    back_part = jnp.concatenate(
        [jnp.sum(t, axis=0, keepdims=True) for t in hat + cross], axis=0
    )
    small = SmallSum(place, val2, box2, s2s, s2r, 2 * SLOTS)
    small.start(back_part)

    arrays = (a_part, n_part)
    sib, anti = {"mrow": place.sib}, {"mrow": place.anti}
    right, left = {"mrow": place.ys[1]}, {"mrow": place.ys[3]}
    sends = []

    def target(a, z, d, c):
        return arrays[a].at[span(place.at(z, d, c) * width, width)]

    def core_copy(a, d, z):
        return remote(
            target(a, z, d, 1 - core), cbox.at[a, d, z], cs2.at[a, d, z], cr2.at[a, d, z], sib
        )

    for d in (2, 1, 3, 0):
        for a in range(2):
            for z in range(2):
                c = core_copy(a, d, z)
                c.start()
                sends.append(c)

    def add_in(dst, srcs):
        for z in range(2):
            @pl.loop(0, width // 16)
            def _(i):
                r = span(i * 16, 16)
                total = dst[z, r].astype(F32)
                for s in srcs:
                    total = total + s[z][r].astype(F32)
                dst[z, r] = total.astype(BF16)

    def core_sum(a, d):
        for z in range(2):
            core_copy(a, d, z).wait_recv()
        add_in(cbox.at[a, d], [[target(a, z, d, core) for z in range(2)]])

    def ypush(a, src, slot, where):
        c = remote(src, ybuf.at[a, slot], ys2.at[a, slot], yr2.at[a, slot], where)
        c.start()
        sends.append(c)

    def ygot(a, slot):
        remote(ybuf.at[a, slot], ybuf.at[a, slot], ys2.at[a, slot], yr2.at[a, slot], right).wait_recv()

    ahead, behind = (right, left), (left, right)
    nxt, prv = (1, 3), (3, 1)
    for a in range(2):
        core_sum(a, 2)
        ypush(a, cbox.at[a, 2], 0, ahead[a])
    small.step()
    for a in range(2):
        core_sum(a, prv[a])
        ypush(a, cbox.at[a, prv[a]], 1, behind[a])
    for a in range(2):
        core_sum(a, nxt[a])
    small.step()

    quarter = feats // 4
    line = Line(place, (gq, go), (gq_buf, go_buf), lns, lnr)
    for t in range(4):
        rt = slice(t * quarter, (t + 1) * quarter)
        for p in range(3):
            gq[t, p] = dot(normed[rt], d_all[p * part : (p + 1) * part], 1, 1).astype(BF16)
        go[t, 0] = dot(h_all[...], u_all[rt], 1, 1).astype(BF16)
    line.start()

    for a in range(2):
        ygot(a, 0)
        add_in(cbox.at[a, nxt[a]], [[ybuf.at[a, 0, z] for z in range(2)]])
        ypush(a, cbox.at[a, nxt[a]], 2, ahead[a])
    for a in range(2):
        core_sum(a, 0)
    small.step()
    zcopies = []
    for a in range(2):
        ygot(a, 1)
        ygot(a, 2)

        @pl.loop(0, width // 16)
        def _(i):
            r = span(i * 16, 16)
            for z in range(2):
                ysum[a, z, r] = (
                    cbox[a, 0, z, r].astype(F32)
                    + ybuf[a, 1, z, r].astype(F32)
                    + ybuf[a, 2, z, r].astype(F32)
                )
            ztot[a, r] = ysum[a, 1 - zh, r].astype(BF16)

        c = remote(ztot.at[a], zbox.at[a], zs2.at[a], zr2.at[a], anti)
        c.start()
        zcopies.append(c)
    back = small.step()
    line.turn(0)
    for c in zcopies:
        c.wait()

    mean_hat = back[:SLOTS] * (1.0 / D)
    mean_cross = back[SLOTS:] * (1.0 / D)
    gain_col = jnp.transpose(jnp.broadcast_to(g_ref[...], (KEEP, KEEP)))[:width, :1]
    acc = jnp.zeros((width, KEEP), F32)
    for j in range(SLOTS):
        here = slice(j * KEEP, (j + 1) * KEEP)
        attn = ysum[0, zh, :, here] + zbox[0, :, here].astype(F32)
        dn = ysum[1, zh, :, here] + zbox[1, :, here].astype(F32)
        xv = x_loc[:, here].astype(F32)
        centred = (xv - mean[j : j + 1]) * inv[j : j + 1]
        acc = acc + dn * centred
        d_in = u_loc[:, here].astype(F32) + inv[j : j + 1] * (
            dn * gain_col - mean_hat[j : j + 1] - centred * mean_cross[j : j + 1]
        )
        out_own[0, :, here] = (xv + attn).astype(BF16)
        out_own[1, :, here] = d_in.astype(BF16)
    for s in range(SPARE):
        for a in range(2):
            value = jnp.zeros((width, KEEP), F32)
            for j in range(SLOTS):
                value = value + out_own[a, :, j * KEEP : (j + 1) * KEEP].astype(F32) * (
                    sel[j * SPARE + s : j * SPARE + s + 1, :]
                )
            out_buf[a, :, s * KEEP : (s + 1) * KEEP] = value.astype(BF16)
    gain_row = jnp.sum(
        jnp.transpose(jnp.concatenate([acc, jnp.zeros((KEEP - width, KEEP), F32)], axis=0)),
        axis=0, keepdims=True,
    )
    gval[...] = jnp.broadcast_to(gain_row, gval.shape)
    back_chain = Chain(place, out_buf, out_got, rt_fwd, rts, rtr)
    back_chain.start()
    gains = []
    for k in range(3):
        c = remote(gval, gbox.at[k], ggs.at[k], ggr.at[k], {"dp": place.dps[k + 1]})
        c.start()
        gains.append(c)
    back_chain.run()
    total = gval[...]
    for k, c in enumerate(gains):
        c.wait()
        total = total + gbox[k]
    gain_out[...] = total
    line.turn(1)
    line.finish((gq_out, go_out))
    for c in sends:
        c.wait_send()


def post_kernel(n, counts, k_ref, own_ref, buf_ref, got_ref, out, dp_out):
    share = Share(counts, lax.axis_index("dp"))
    patch = lax.broadcasted_iota(jnp.int32, (dp_out.shape[2], KEEP), 0)
    for i in range(n):
        lanes = slice(i * KEEP, (i + 1) * KEEP)
        if i < SLOTS:
            flag = jnp.where(i < share.own, 1.0, 0.0)
            res, d_in = (own_ref[a, :, lanes].astype(F32) * flag for a in range(2))
        else:
            slot = clamp(share.spare_at + i - SLOTS, SPARE - 1)
            flag = jnp.where(i - SLOTS < share.extra, 1.0, 0.0)
            here = span(slot * KEEP, KEEP)
            res, d_in = (
                (
                    buf_ref[a, :, here].astype(F32)
                    + got_ref[0, a, :, here].astype(F32)
                    + got_ref[1, a, :, here].astype(F32)
                )
                * flag
                for a in range(2)
            )
        pick = (patch == k_ref[i : i + 1, :]).astype(F32).astype(BF16)
        out[:, lanes] = res.astype(BF16)
        dp_out[i] = dot(d_in.astype(BF16), pick, 1, 1).astype(BF16)


def sharded(patches, keep_index, counts, gain, w_qkv, w_out, cotangent):
    n, patch_count, width = patches.shape
    total_rows = n * KEEP
    rows = SLOTS * KEEP
    feats = w_qkv.shape[0]
    heads = w_out.shape[0]
    heads3 = 3 * heads
    quarter = feats // 4
    half = (heads3 + heads) // 2
    gain_row = jnp.pad(gain, (0, KEEP - width))[None]
    spare = SPARE * KEEP
    small = 2 * SLOTS + 16
    blk = (2, width, rows)

    def v(shape, dtype=BF16):
        return pltpu.VMEM(shape, dtype)

    scratch = [
        v((width, rows)), v((width, rows)), v((feats, rows)), v((feats, rows)), v((feats, rows)),
        v((3, heads, feats)), v((feats, heads)),
        v((2, 2, width, spare)), v((2, 2, width, spare)), v((2, 2, width, spare)),
        v((8, small, KEEP), F32), v((4, small, KEEP), F32),
        v((8, 2 * SLOTS, KEEP), F32), v((4, 2 * SLOTS, KEEP), F32),
        v((heads3, rows)), v((heads, rows)), v((heads3, rows)), v((heads, rows)),
        v((heads3 + heads, KEEP)), v((heads3 + heads, KEEP)),
        v((6, half, KEEP)), v((6, heads, KEEP)),
        v((feats, rows)), v((feats, rows)), v((2, 4) + blk), v((2, 3) + blk),
        v((2,) + blk, F32), v((2, width, rows)), v((2, width, rows)),
        v((4, 3, quarter, heads)), v((4, 1, heads, quarter)),
        v((2, 3, 3, quarter, heads)), v((2, 3, 1, heads, quarter)),
        v((3, 8, KEEP), F32), v((8, KEEP), F32),
        DMA((8,)), DMA((8,)), DMA((8,)), DMA((8,)),
        DMA((2,)), DMA((2, 4)), DMA((2, 2)), DMA((2, 8)), DMA((2, 16)),
        DMA((2, CHUNKS)), DMA((2, CHUNKS)), DMA((2, CHUNKS)), DMA((2, CHUNKS)),
        DMA((6,)), DMA((6,)), DMA((6,)), DMA((6,)), DMA((3, 3)), DMA((3, 4)),
        DMA((2, 4, 2)), DMA((2, 4, 2)), DMA((2, 3)), DMA((2, 3)), DMA((2,)), DMA((2,)),
        DMA((2, 3, 2)), DMA((2, 3, 2)), DMA((3,)), DMA((3,)),
    ]
    shape = jax.ShapeDtypeStruct
    first, spare_own, sel = pl.pallas_call(
        prep_kernel,
        out_shape=[
            shape((2, width, rows), BF16), shape((2, width, spare), BF16),
            shape((SLOTS * SPARE, KEEP), F32),
        ],
        in_specs=[SM] + [VM] * 3,
        out_specs=[VM] * 3,
        compiler_params=pltpu.CompilerParams(vmem_limit_bytes=32 * 1024 * 1024),
    )(counts, jnp.transpose(patches, (0, 2, 1)), keep_index, cotangent.T)
    out_own, out_buf, out_got, gq, go, gg = pl.pallas_call(
        main_kernel,
        out_shape=[
            shape((2, width, rows), BF16), shape((2, width, spare), BF16),
            shape((2, 2, width, spare), BF16),
            shape((3, quarter, heads), F32), shape((1, heads, quarter), F32),
            shape((8, KEEP), F32),
        ],
        in_specs=[VM] * 6,
        out_specs=[VM] * 6,
        scratch_shapes=scratch,
        compiler_params=pltpu.CompilerParams(
            vmem_limit_bytes=58 * 1024 * 1024, collective_id=1, has_side_effects=True
        ),
    )(
        first, spare_own, sel, gain_row, jnp.transpose(w_qkv, (1, 0, 2)), w_out,
    )
    outputs, d_patches = pl.pallas_call(
        partial(post_kernel, n),
        out_shape=[shape((width, total_rows), BF16), shape((n, width, patch_count), BF16)],
        in_specs=[SM] + [VM] * 4,
        out_specs=[VM] * 2,
        compiler_params=pltpu.CompilerParams(vmem_limit_bytes=32 * 1024 * 1024),
    )(counts, keep_index, out_own, out_buf, out_got)
    part = width // 4
    grad_gain = lax.dynamic_slice(gg[0], (lax.axis_index("dp") * part,), (part,))
    return (
        outputs.T, jnp.transpose(d_patches, (0, 2, 1)), jnp.transpose(gq, (1, 0, 2)), go[0], grad_gain
    )


def solution(mesh):
    placed = (
        P("dp", None, ("mcol", "mrow")),
        P("dp", None),
        P(),
        P(("mcol", "mrow")),
        P("mcol", None, "mrow"),
        P("mrow", "mcol"),
        P("dp", ("mcol", "mrow")),
    )
    return jax.shard_map(
        sharded,
        mesh=mesh,
        in_specs=placed,
        out_specs=(
            P("dp", ("mcol", "mrow")),
            P("dp", None, ("mcol", "mrow")),
            P(("mcol", "dp"), None, "mrow"),
            P("mrow", ("mcol", "dp")),
            P(("mcol", "mrow", "dp")),
        ),
        check_vma=False,
    )
```

time: 853 us -> 206 us (0.24)
  blocking collectives: 462 us -> 0 us
  waiting for transfers between devices: 291 us -> 0 us
  Pallas kernels: 0 us -> 189 us
  matrix products: 34.2 us -> 0 us
  local copies, waits for them, and re-layouts: 38.5 us -> 13.8 us
  between operations: 14.9 us -> 0.7 us
  other arithmetic: 10.8 us -> 0 us
    psum x2 -> x0, blocking collectives: 424 us -> none  [feature_sums(): return lax.psum((sum_first, second), ('mrow', 'mcol'))]
    pallas_call x0 -> x3, Pallas kernels: none -> 189 us  [the longest x1 187 us: sharded(): pl.pallas_call(main_kernel, out_shape=[shape((2, width, rows), BF16), sha...]
    unnamed x11 -> x0, waiting for transfers between devices: 166 us -> none
    all_gather x3 -> x0, waiting for transfers between devices: 65.5 us -> none  [the longest x2 57.9 us: row_gather(): return lax.all_gather(values, 'mrow', axis=1, tiled=True)]
    reduce_scatter x4 -> x0, waiting for transfers between devices: 59.7 us -> none  [the longest x2 59.7 us: column_sum(): lax.psum_scatter(term_maker(jnp.int32(0), lax.axis_size('mcol') * shard_r...]
    dot_general x12 -> x0, matrix products: 34.2 us -> none  [the longest x1 6.97 us: project(): return jnp.dot(gathered, stacked, preferred_element_type=jnp.float32)]
    unnamed x1 -> x0, blocking collectives: 24.7 us -> none
    all_gather x1 -> x0, blocking collectives: 13.4 us -> none  [column_gather(): return lax.all_gather(values, 'mcol', axis=0, tiled=True)]
  transfers between devices with their start and end apart: 9 -> 0, of which waited for: 6 -> 0; matrix products, arithmetic and copies ran while one was open for 8% -> 0% of each run, Pallas kernels for 0% -> 0%
where the time goes in v2:
time: 206 us; the launch traced here: 204 us
  Pallas kernels  189 us (92%)
  local copies, waits for them, and re-layouts  13.8 us (7%)
    pallas_call x1, Pallas kernels, sharded(): pl.pallas_call(main_kernel, out_shape=[shape((2, width, rows), BF16), sha...  187 us
    unnamed x28, local copies, waits for them, and re-layouts  11.4 us

profile of v2, /device:TPU:0, one launch (start us, length us, event | category | flops | bytes accessed | tf_op | source)
XLA Modules:
  0.0 203.8 jit_solution(7677433457359759971)
XLA Ops:
  0.6 1.2 pad_bitcast_fusion.g_ref
  1.8 0.0 copy-start.1
  1.8 1.0 copy-done.1
  2.8 0.0 copy-start.5
  2.8 0.9 copy-done.5
  3.7 0.0 copy-start.7
  3.7 0.7 copy-done.7
  4.4 0.0 copy-start.10
  4.4 0.7 copy-done.10
  5.1 0.8 shard_map.110
  5.9 0.0 copy-start.2
  5.9 0.7 copy-done.2
  6.6 0.0 copy-start.4
  6.6 0.7 copy-done.4
  7.3 0.0 copy-start.9
  7.3 0.6 copy-done.9
  7.9 0.0 copy-start.8
  7.9 0.0 copy-start.11
  7.9 186.7 %shard_map.111 = (bf16[2,96,512]{2,1,0:T(8,128)(2,1)}, bf16[2,96,768]{2,1,0:T(8,128)(2,1)}, bf16[2,2,96,768]{3,2,1,0:T(8,128)(2,1)}, f32[3,384,256]{2,1,0:T(8,12...) custom-call(bf16[2,96,512]{2,1,0:T(8,128)(2,1)} %copy-done.4, bf16[2,96,768]{2,1,0:T(8,128)(2,1)} %copy-done.2, ...), custom_call_target="tpu_custom_call" | custom-call | tf_op jit(solution)/shard_map/pallas_call | solution.py:839
  194.7 0.0 copy-done.8
  194.7 0.0 copy-done.11
  194.7 0.0 copy-start
  194.7 1.1 copy-done
  195.8 0.0 copy-start.3
  195.8 1.0 copy-done.3
  196.7 0.0 copy-start.6
  196.7 0.9 copy-done.6
  197.7 1.7 shard_map.112
  199.3 0.7 slice.3
  200.0 0.6 dynamic-slice_bitcast_fusion
  200.6 0.0 copy-start.12
  200.6 2.4 %copy.14 = f32[384,3,256]{2,0,1:T(8,128)} copy(f32[384,3,256]{2,0,1:T(8,128)} %bitcast.14) | data formatting | bytes 2359296
  203.0 0.0 copy-done.12
  203.0 0.7 copy.15
Async XLA Ops:
  1.8 1.0 copy-start.1
  2.8 0.9 copy-start.5
  3.7 0.7 copy-start.7
  4.4 0.7 copy-start.10
  5.9 0.7 copy-start.2
  6.6 0.7 copy-start.4
  7.3 0.6 copy-start.9
  7.9 186.8 %copy-start.8 = (s32[8,128]{1,0:T(8,128)S(1)}, s32[8,128]{1,0:T(8,128)}, u32[]{:S(2)}) copy-start(s32[8,128]{1,0:T(8,128)} %k_ref.3) | copy-start | bytes 12292
  7.9 186.8 %copy-start.11 = (s32[4]{0:T(128)S(1)}, s32[4]{0:T(128)}, u32[]{:S(2)}) copy-start(s32[4]{0:T(128)} %counts.3) | copy-start | bytes 52
  194.7 1.1 copy-start
  195.8 1.0 copy-start.3
  196.7 0.9 copy-start.6
  200.6 2.4 %copy-start.12 = (f32[1,256,384]{2,1,0:T(8,128)S(1)}, f32[1,256,384]{2,1,0:T(8,128)}, u32[]{:S(2)}) copy-start(f32[1,256,384]{2,1,0:T(8,128)} %get-tuple-element.25) | copy-start | bytes 1179652

commit v3 on v2

--- a/solution.py
+++ b/solution.py
@@ -20,6 +20,7 @@
 MESH = pl.DeviceIdType.MESH
 VM = pl.BlockSpec(memory_space=pltpu.VMEM)
 SM = pl.BlockSpec(memory_space=pltpu.SMEM)
+ANY = pl.BlockSpec(memory_space=pl.ANY)
 DMA = pltpu.SemaphoreType.DMA
 
 
@@ -46,6 +47,14 @@
 
 def span(start, size, step=None):
     return pl.ds(pl.multiple_of(start, step or size), size)
+
+
+def load(pairs, sem):
+    copies = [pltpu.make_async_copy(src, dst, sem.at[i]) for i, (src, dst) in enumerate(pairs)]
+    for c in copies:
+        c.start()
+    for c in copies:
+        c.wait()
 
 
 class Place:
@@ -300,15 +309,123 @@
     return total
 
 
-def middle(place, q_ref, m_ref, dall, hall, work, own, bq, bm, sq, sm, rq, rm, gs, gr):
+class RingX:
+    def __init__(self, place, dh, send, recv):
+        self.x, self.xs, self.dh, self.send, self.recv = place.x, place.xs, dh, send, recv
+        self.right, self.left = {"mcol": place.xs[1]}, {"mcol": place.xs[3]}
+        self.half = dh.shape[1] // 2
+        self.width = dh.shape[2] // 4
+        self.sends = []
+
+    def copy(self, slot, p, block, k, where):
+        view = self.dh.at[slot, pl.ds(p * self.half, self.half), span(block * self.width, self.width)]
+        return remote(view, view, self.send.at[slot, p, k], self.recv.at[slot, p, block], where)
+
+    def push(self, slot, p, block, k, where):
+        c = self.copy(slot, p, block, k, where)
+        c.start()
+        self.sends.append(c)
+
+    def got(self, slot, p, block):
+        self.copy(slot, p, block, 0, self.right).wait_recv()
+
+    def start(self, slot):
+        for p in range(2):
+            self.push(slot, p, self.x, 0, self.right)
+            self.push(slot, p, self.x, 1, self.left)
+
+    def forward(self, slot):
+        self.got(slot, 0, self.xs[3])
+        self.push(slot, 0, self.xs[3], 2, self.right)
+        self.got(slot, 1, self.xs[1])
+        self.push(slot, 1, self.xs[1], 2, self.left)
+
+    def finish(self, slot):
+        self.got(slot, 1, self.xs[3])
+        self.got(slot, 0, self.xs[1])
+        self.got(slot, 0, self.xs[2])
+        self.got(slot, 1, self.xs[2])
+
+
+class Quarters:
+    def __init__(self, place, arrays, out, zsend, zrecv, send, recv):
+        self.place, self.arrays, self.out = place, arrays, out
+        self.zsend, self.zrecv, self.send, self.recv = zsend, zrecv, send, recv
+        self.share = out.shape[2] // 8
+        self.sends = []
+        self.n = [0, 0]
+        self.right, self.left = {"mrow": place.ys[1]}, {"mrow": place.ys[3]}
+        self.sib = {"mrow": place.sib}
+
+    def index(self, dy, core):
+        return lax.rem(self.place.y + dy, 4) * 2 + core
+
+    def view(self, a, index):
+        return self.out.at[a, 1:4, span(index * self.share, self.share)]
+
+    def zcopy(self, a, r):
+        dp, mine = self.place.dps[r], self.index(0, self.place.core)
+        src = self.arrays[a].at[span(dp * self.out.shape[2] + mine * self.share, self.share)]
+        dst = self.out.at[a, r, span(mine * self.share, self.share)]
+        return remote(src, dst, self.zsend.at[a, r], self.zrecv.at[a, r], {"dp": dp})
+
+    def push(self, a, index, where):
+        k = self.n[a]
+        self.n[a] += 1
+        c = remote(self.view(a, index), self.view(a, index), self.send.at[a, k], self.recv.at[a, index], where)
+        c.start()
+        self.sends.append(c)
+
+    def got(self, a, index):
+        remote(
+            self.view(a, index), self.view(a, index), self.send.at[a, 0], self.recv.at[a, index], self.sib
+        ).wait_recv()
+
+    def start(self):
+        for a in range(2):
+            for r in (1, 3, 2):
+                self.zcopy(a, r).start()
+
+    def spread(self):
+        mine = self.index(0, self.place.core)
+        for a in range(2):
+            for r in (1, 3, 2):
+                self.zcopy(a, r).wait()
+            for where in (self.right, self.left, self.sib):
+                self.push(a, mine, where)
+
+    def forward(self):
+        before, after = self.index(3, self.place.core), self.index(1, self.place.core)
+        self.got(0, before)
+        self.push(0, before, self.right)
+        self.got(1, after)
+        self.push(1, after, self.left)
+        self.got(1, before)
+        self.got(0, after)
+        for a in range(2):
+            self.push(a, before, self.sib)
+            self.push(a, after, self.sib)
+
+    def far(self):
+        far = self.index(2, self.place.core)
+        for a in range(2):
+            self.got(a, far)
+            self.push(a, far, self.sib)
+
+    def finish(self):
+        for a in range(2):
+            for dy in range(4):
+                self.got(a, self.index(dy, 1 - self.place.core))
+
+
+def middle(place, q_ref, m_ref, own, work, bq, bm, sq, sm, rq, rm, between):
     x, xs = place.x, place.xs
     right, left = {"mcol": xs[1]}, {"mcol": xs[3]}
-    width = own.shape[1]
+    width = work.shape[1]
     qrows = q_ref.shape[0]
-    half = own.shape[0] // 2
+    half = work.shape[0] // 2
     mrows = m_ref.shape[0]
     qminus = qrows - half
-
     def lanes(block):
         return span(block * width, width)
 
@@ -351,6 +468,7 @@
     got_minus(3)
     got_plus(4)
     got_minus(5)
+    between()
     heads = mrows // HD
 
     def total(r0):
@@ -370,136 +488,13 @@
         out, dq, dk, dv = attend(q, k, v, do)
         for part, value in enumerate((dq, dk, dv, out)):
             r0 = (part * heads + h) * HD
-            own[r0 : r0 + HD] = value.astype(BF16)
-
-    dst = (
-        (dall, pl.ds(0, half), pl.ds(0, half)),
-        (dall, pl.ds(half, qminus), pl.ds(half, qminus)),
-        (hall, pl.ds(qrows, mrows), pl.ds(0, mrows)),
-    )
-
-    def push_part(p, block, src, k, where):
-        out, _, rows = dst[p]
-        c = remote(src, out.at[rows, lanes(block)], gs.at[p, k], gr.at[p, block], where)
-        c.start()
-        sends.append(c)
-
-    def got_part(p, block):
-        out, rows_own, rows = dst[p]
-        remote(
-            own.at[rows_own], out.at[rows, lanes(block)], gs.at[p, 0], gr.at[p, block], right
-        ).wait_recv()
-
-    for p in range(3):
-        for k, where in enumerate((right, left)):
-            push_part(p, x, own.at[dst[p][1]], k, where)
-    dall[:, lanes(x)] = own[:qrows]
-    hall[:, lanes(x)] = own[qrows:]
-    got_part(0, xs[3])
-    push_part(0, xs[3], dall.at[dst[0][2], lanes(xs[3])], 2, right)
-    for p in (1, 2):
-        got_part(p, xs[1])
-        out = dst[p][0]
-        push_part(p, xs[1], out.at[dst[p][2], lanes(xs[1])], 2, left)
-    got_part(1, xs[3])
-    got_part(2, xs[3])
-    got_part(0, xs[1])
-    for p in range(3):
-        got_part(p, xs[2])
+            own[r0 : r0 + HD, lanes(x)] = value.astype(BF16)
     for c in sends:
         c.wait_send()
 
 
-class Line:
-    def __init__(self, place, owns, bufs, send, recv):
-        self.dp, self.owns, self.bufs, self.send, self.recv = place.dp, owns, bufs, send, recv
-        self.near = [{"dp": place.dps[1]}, {"dp": place.dps[3]}]
-
-    def copies(self, way, t, own):
-        slot = t - 1 if way == 0 else t
-        return [
-            remote(
-                o.at[t] if own else b.at[way, slot], b.at[way, slot],
-                self.send.at[way, slot, i], self.recv.at[way, slot, i], self.near[way],
-            )
-            for i, (o, b) in enumerate(zip(self.owns, self.bufs))
-        ]
-
-    def start(self):
-        for dp, way, blocks in ((0, 0, (3, 2, 1)), (3, 1, (0, 1, 2))):
-            @pl.when(self.dp == dp)
-            def _():
-                for t in blocks:
-                    for c in self.copies(way, t, True):
-                        c.start()
-
-    def forward(self, way, t):
-        slot = t - 1 if way == 0 else t
-        for c in self.copies(way, t, False):
-            c.wait_recv()
-        for o, b in zip(self.owns, self.bufs):
-            add_blocks(b.at[way, slot], o.at[t])
-        for c in self.copies(way, t, False):
-            c.start()
-
-    def turn(self, n):
-        for dp, todo in (
-            (1, ([(0, 3)], [(0, 2), (1, 0)])[n]),
-            (2, ([(1, 0)], [(1, 1), (0, 3)])[n]),
-        ):
-            @pl.when(self.dp == dp)
-            def _():
-                for way, t in todo:
-                    self.forward(way, t)
-
-    def finish(self, outs):
-        dp = self.dp
-
-        def add(way, first):
-            for c in self.copies(way, dp, False):
-                c.wait_recv()
-            slot = dp - 1 if way == 0 else dp
-            for o, b, out in zip(self.owns, self.bufs, outs):
-                add_blocks(out, b.at[way, slot], o.at[dp] if first else out)
-
-        @pl.when(dp == 0)
-        def _():
-            add(1, True)
-
-        @pl.when(dp > 0)
-        def _():
-            add(0, True)
-
-        @pl.when((dp > 0) & (dp < 3))
-        def _():
-            add(1, False)
-
-        for t in range(1, 4):
-            @pl.when(dp < t)
-            def _():
-                for c in self.copies(0, t, False):
-                    c.wait_send()
-        for t in range(3):
-            @pl.when(dp > t)
-            def _():
-                for c in self.copies(1, t, False):
-                    c.wait_send()
-
-
-def add_blocks(out, *srcs):
-    if len(srcs) == 1:
-        srcs = (out,) + srcs
-    for p in range(out.shape[0]):
-        @pl.loop(0, out.shape[1] // 16)
-        def _(i):
-            r = span(i * 16, 16)
-            total = srcs[0][p, r].astype(F32)
-            for s in srcs[1:]:
-                total = total + s[p, r].astype(F32)
-            out[p, r] = total.astype(out.dtype)
-
-
-def prep_kernel(counts, p_ref, k_ref, c_ref, own, spare, sel):
+def prep_kernel(counts, p_hbm, k_hbm, c_hbm, own, spare, sel, p_ref, k_ref, c_ref, sem):
+    load(((p_hbm, p_ref), (k_hbm, k_ref), (c_hbm, c_ref)), sem)
     share = Share(counts, lax.axis_index("dp"))
     patch = lax.broadcasted_iota(jnp.int32, (p_ref.shape[2], KEEP), 0)
 
@@ -523,19 +518,22 @@
 
 
 def main_kernel(
-    first, sp_own, sel, g_ref, w_ref, wo_ref,
+    first, sp_own, sel, g_ref, w_hbm, wo_hbm,
     out_own, out_buf, out_got, gq_out, go_out, gain_out,
     x_loc, u_loc, x_all, u_all, normed, wt, wot,
     sp_got, sp_fwd, rt_fwd,
     box1, val1, box2, val2,
-    q_part, m_part, d_all, h_all, work, own, bq, bm,
+    q_part, m_part, work, bq, bm,
     a_part, n_part, cbox, ybuf, ysum, ztot, zbox,
-    gq, go, gq_buf, go_buf, gbox, gval,
+    dh, quarters, w_ref, wo_ref, gbox, gval,
     s1s, s1r, s2s, s2r, zs1, ys1, fs1, cs1, r1,
     sps, spr, rts, rtr,
-    sq, sm, rq, rm, gs, gr,
-    cs2, cr2, ys2, yr2, zs2, zr2, lns, lnr, ggs, ggr,
+    sq, sm, rq, rm,
+    cs2, cr2, ys2, yr2, zs2, zr2, dxs, dxr, dzs, dzr, qzs, qzr, qys, qyr, wsem, ggs, ggr,
 ):
+    loads = [pltpu.make_async_copy(w_hbm, w_ref, wsem.at[0]), pltpu.make_async_copy(wo_hbm, wo_ref, wsem.at[1])]
+    for c in loads:
+        c.start()
     place = Place()
     greet(place.peers())
     width = x_loc.shape[0]
@@ -557,12 +555,17 @@
         sums.append(jnp.sum(values[0], axis=0, keepdims=True))
         squares.append(jnp.sum(values[0] * values[0], axis=0, keepdims=True))
     me_row = lax.broadcasted_iota(jnp.int32, (16, KEEP), 0) == place.me
-    own_gain = jnp.where(me_row, g_ref[...], 0.0)
+    gval[...] = jnp.zeros(gval.shape, F32)
+    gval[:1, :width] = g_ref[...]
+    gain_row = gval[:1]
+    own_gain = jnp.where(me_row, gain_row, 0.0)
 
     small = SmallSum(place, val1, box1, s1s, s1r, 2 * SLOTS)
     small.start(jnp.concatenate(sums + squares + [own_gain], axis=0))
 
     def turn_weights():
+        for c in loads:
+            c.wait()
         for p in range(3):
             wt[p] = jnp.transpose(w_ref[p])
         wot[...] = jnp.transpose(wo_ref[...])
@@ -583,12 +586,29 @@
             centred = (x_all[rb, here].astype(F32) - mean[j : j + 1]) * inv[j : j + 1]
             normed[rb, here] = (centred * col).astype(BF16)
 
+    fetch = Quarters(place, (normed, u_all), quarters, qzs, qzr, qys, qyr)
+    fetch.start()
     part = w_ref.shape[2]
     for p in range(3):
         q_part[p * part : (p + 1) * part] = dot(wt[p], normed[...], 1, 0).astype(BF16)
     m_part[...] = dot(wo_ref[...], u_all[...], 1, 0).astype(BF16)
 
-    middle(place, q_part, m_part, d_all, h_all, work, own, bq, bm, sq, sm, rq, rm, gs, gr)
+    mine = dh.at[0]
+    middle(place, q_part, m_part, mine, work, bq, bm, sq, sm, rq, rm, fetch.spread)
+
+    ring = RingX(place, dh, dxs, dxr)
+    ring.start(0)
+    here = span(place.x * KEEP, KEEP)
+    zsends = [
+        remote(dh.at[0, :, here], dh.at[r, :, here], dzs.at[r], dzr.at[r], {"dp": place.dps[r]})
+        for r in range(1, 4)
+    ]
+    for r in (1, 3, 2):
+        zsends[r - 1].start()
+    fetch.forward()
+    ring.forward(0)
+    ring.finish(0)
+    d_all, h_all = dh.at[0, : 3 * part], dh.at[0, 3 * part :]
 
     hat = [jnp.zeros((8, KEEP), F32) for _ in range(SLOTS)]
     cross = [jnp.zeros((8, KEEP), F32) for _ in range(SLOTS)]
@@ -673,15 +693,7 @@
         core_sum(a, nxt[a])
     small.step()
 
-    quarter = feats // 4
-    line = Line(place, (gq, go), (gq_buf, go_buf), lns, lnr)
-    for t in range(4):
-        rt = slice(t * quarter, (t + 1) * quarter)
-        for p in range(3):
-            gq[t, p] = dot(normed[rt], d_all[p * part : (p + 1) * part], 1, 1).astype(BF16)
-        go[t, 0] = dot(h_all[...], u_all[rt], 1, 1).astype(BF16)
-    line.start()
-
+    fetch.far()
     for a in range(2):
         ygot(a, 0)
         add_in(cbox.at[a, nxt[a]], [[ybuf.at[a, 0, z] for z in range(2)]])
@@ -689,6 +701,9 @@
     for a in range(2):
         core_sum(a, 0)
     small.step()
+    for r in (1, 3, 2):
+        zsends[r - 1].wait_recv()
+        ring.start(r)
     zcopies = []
     for a in range(2):
         ygot(a, 1)
@@ -709,13 +724,14 @@
         c.start()
         zcopies.append(c)
     back = small.step()
-    line.turn(0)
+    for r in (1, 3, 2):
+        ring.forward(r)
     for c in zcopies:
         c.wait()
 
     mean_hat = back[:SLOTS] * (1.0 / D)
     mean_cross = back[SLOTS:] * (1.0 / D)
-    gain_col = jnp.transpose(jnp.broadcast_to(g_ref[...], (KEEP, KEEP)))[:width, :1]
+    gain_col = jnp.transpose(jnp.broadcast_to(gain_row, (KEEP, KEEP)))[:width, :1]
     acc = jnp.zeros((width, KEEP), F32)
     for j in range(SLOTS):
         here = slice(j * KEEP, (j + 1) * KEEP)
@@ -749,19 +765,33 @@
         c = remote(gval, gbox.at[k], ggs.at[k], ggr.at[k], {"dp": place.dps[k + 1]})
         c.start()
         gains.append(c)
+    fetch.finish()
+    quarter = quarters.shape[2]
+    for a, arr in enumerate((normed, u_all)):
+        quarters[a, 0] = arr[span(place.dp * quarter, quarter)]
+    for r in (1, 3, 2):
+        ring.finish(r)
+    for p in range(3):
+        total = dot(quarters[0, 0], dh[0, p * part : (p + 1) * part], 1, 1)
+        for r in range(1, 4):
+            total = total + dot(quarters[0, r], dh[r, p * part : (p + 1) * part], 1, 1)
+        gq_out[p] = total
+    total = dot(dh[0, 3 * part :], quarters[1, 0], 1, 1)
+    for r in range(1, 4):
+        total = total + dot(dh[r, 3 * part :], quarters[1, r], 1, 1)
+    go_out[...] = total
     back_chain.run()
     total = gval[...]
     for k, c in enumerate(gains):
         c.wait()
         total = total + gbox[k]
     gain_out[...] = total
-    line.turn(1)
-    line.finish((gq_out, go_out))
-    for c in sends:
+    for c in sends + zsends + ring.sends + fetch.sends:
         c.wait_send()
 
 
-def post_kernel(n, counts, k_ref, own_ref, buf_ref, got_ref, out, dp_out):
+def post_kernel(n, counts, k_hbm, own_hbm, buf_hbm, got_hbm, out, dp_out, k_ref, own_ref, buf_ref, got_ref, sem):
+    load(((k_hbm, k_ref), (own_hbm, own_ref), (buf_hbm, buf_ref), (got_hbm, got_ref)), sem)
     share = Share(counts, lax.axis_index("dp"))
     patch = lax.broadcasted_iota(jnp.int32, (dp_out.shape[2], KEEP), 0)
     for i in range(n):
@@ -796,7 +826,7 @@
     heads3 = 3 * heads
     quarter = feats // 4
     half = (heads3 + heads) // 2
-    gain_row = jnp.pad(gain, (0, KEEP - width))[None]
+    gain_row = gain[None]
     spare = SPARE * KEEP
     small = 2 * SLOTS + 16
     blk = (2, width, rows)
@@ -810,20 +840,20 @@
         v((2, 2, width, spare)), v((2, 2, width, spare)), v((2, 2, width, spare)),
         v((8, small, KEEP), F32), v((4, small, KEEP), F32),
         v((8, 2 * SLOTS, KEEP), F32), v((4, 2 * SLOTS, KEEP), F32),
-        v((heads3, rows)), v((heads, rows)), v((heads3, rows)), v((heads, rows)),
-        v((heads3 + heads, KEEP)), v((heads3 + heads, KEEP)),
+        v((heads3, rows)), v((heads, rows)),
+        v((heads3 + heads, KEEP)),
         v((6, half, KEEP)), v((6, heads, KEEP)),
         v((feats, rows)), v((feats, rows)), v((2, 4) + blk), v((2, 3) + blk),
         v((2,) + blk, F32), v((2, width, rows)), v((2, width, rows)),
-        v((4, 3, quarter, heads)), v((4, 1, heads, quarter)),
-        v((2, 3, 3, quarter, heads)), v((2, 3, 1, heads, quarter)),
+        v((4, heads3 + heads, rows)), v((2, 4, quarter, rows)), v((3, feats, heads)), v((heads, feats)),
         v((3, 8, KEEP), F32), v((8, KEEP), F32),
         DMA((8,)), DMA((8,)), DMA((8,)), DMA((8,)),
         DMA((2,)), DMA((2, 4)), DMA((2, 2)), DMA((2, 8)), DMA((2, 16)),
         DMA((2, CHUNKS)), DMA((2, CHUNKS)), DMA((2, CHUNKS)), DMA((2, CHUNKS)),
-        DMA((6,)), DMA((6,)), DMA((6,)), DMA((6,)), DMA((3, 3)), DMA((3, 4)),
+        DMA((6,)), DMA((6,)), DMA((6,)), DMA((6,)),
         DMA((2, 4, 2)), DMA((2, 4, 2)), DMA((2, 3)), DMA((2, 3)), DMA((2,)), DMA((2,)),
-        DMA((2, 3, 2)), DMA((2, 3, 2)), DMA((3,)), DMA((3,)),
+        DMA((4, 2, 3)), DMA((4, 2, 4)), DMA((4,)), DMA((4,)), DMA((2, 4)), DMA((2, 4)),
+        DMA((2, 8)), DMA((2, 8)), DMA((2,)), DMA((3,)), DMA((3,)),
     ]
     shape = jax.ShapeDtypeStruct
     first, spare_own, sel = pl.pallas_call(
@@ -832,19 +862,22 @@
             shape((2, width, rows), BF16), shape((2, width, spare), BF16),
             shape((SLOTS * SPARE, KEEP), F32),
         ],
-        in_specs=[SM] + [VM] * 3,
+        in_specs=[SM] + [ANY] * 3,
         out_specs=[VM] * 3,
-        compiler_params=pltpu.CompilerParams(vmem_limit_bytes=32 * 1024 * 1024),
+        scratch_shapes=[
+            v((n, width, patch_count)), v((n, KEEP), jnp.int32), v((width, total_rows)), DMA((3,))
+        ],
+        compiler_params=pltpu.CompilerParams(vmem_limit_bytes=58 * 1024 * 1024),
     )(counts, jnp.transpose(patches, (0, 2, 1)), keep_index, cotangent.T)
     out_own, out_buf, out_got, gq, go, gg = pl.pallas_call(
         main_kernel,
         out_shape=[
             shape((2, width, rows), BF16), shape((2, width, spare), BF16),
             shape((2, 2, width, spare), BF16),
-            shape((3, quarter, heads), F32), shape((1, heads, quarter), F32),
+            shape((3, quarter, heads), F32), shape((heads, quarter), F32),
             shape((8, KEEP), F32),
         ],
-        in_specs=[VM] * 6,
+        in_specs=[VM] * 4 + [ANY] * 2,
         out_specs=[VM] * 6,
         scratch_shapes=scratch,
         compiler_params=pltpu.CompilerParams(
@@ -856,14 +889,18 @@
     outputs, d_patches = pl.pallas_call(
         partial(post_kernel, n),
         out_shape=[shape((width, total_rows), BF16), shape((n, width, patch_count), BF16)],
-        in_specs=[SM] + [VM] * 4,
+        in_specs=[SM] + [ANY] * 4,
         out_specs=[VM] * 2,
-        compiler_params=pltpu.CompilerParams(vmem_limit_bytes=32 * 1024 * 1024),
+        scratch_shapes=[
+            v((n, KEEP), jnp.int32), v((2, width, rows)), v((2, width, spare)), v((2, 2, width, spare)),
+            DMA((4,)),
+        ],
+        compiler_params=pltpu.CompilerParams(vmem_limit_bytes=58 * 1024 * 1024),
     )(counts, keep_index, out_own, out_buf, out_got)
     part = width // 4
     grad_gain = lax.dynamic_slice(gg[0], (lax.axis_index("dp") * part,), (part,))
     return (
-        outputs.T, jnp.transpose(d_patches, (0, 2, 1)), jnp.transpose(gq, (1, 0, 2)), go[0], grad_gain
+        outputs.T, jnp.transpose(d_patches, (0, 2, 1)), jnp.transpose(gq, (1, 0, 2)), go, grad_gain
     )
 
 

time: 206 us -> 144 us (0.70)
  Pallas kernels: 189 us -> 137 us
  local copies, waits for them, and re-layouts: 13.8 us -> 4.43 us
    pallas_call x1, Pallas kernels: 187 us -> 131 us  [sharded(): pl.pallas_call(main_kernel, out_shape=[shape((2, width, rows), BF16), sha...]
    unnamed x28 -> x4, local copies, waits for them, and re-layouts: 11.4 us -> 3.16 us
where the time goes in v3:
time: 144 us; the launch traced here: 142 us
  Pallas kernels  137 us (95%)
  local copies, waits for them, and re-layouts  4.43 us (3%)
    pallas_call x1, Pallas kernels, sharded(): pl.pallas_call(main_kernel, out_shape=[shape((2, width, rows), BF16), sha...  131 us
    unnamed x4, local copies, waits for them, and re-layouts  3.16 us
    pallas_call x1, Pallas kernels, sharded(): pl.pallas_call(partial(post_kernel, n), out_shape=[shape((width, total_ro...  3.1 us

profile of v3, /device:TPU:0, one launch (start us, length us, event | category | flops | bytes accessed | tf_op | source)
XLA Modules:
  0.0 142.2 jit_solution(1651264276657768910)
XLA Ops:
  0.6 2.8 %shard_map.110 = (bf16[2,96,512]{2,1,0:T(8,128)(2,1)}, bf16[2,96,768]{2,1,0:T(8,128)(2,1)}, f32[24,128]{1,0:T(8,128)}) custom-call(s32[4]{0:T(128)} %counts.3, bf16[8,96,256]{2,1,0:T(8,128)(2,1)} %bitcast.11, s32[8,128]{1,0:T(8,128)} %k_hbm.3, bf16[96,1024]{1,0:T(8,128)(2,1)} %bitcast.12), custom_call_target="tpu_custom_call" | custom-call | tf_op jit(solution)/shard_map/pallas_call | solution.py:859
  3.5 131.1 %shard_map.111 = (bf16[2,96,512]{2,1,0:T(8,128)(2,1)}, bf16[2,96,768]{2,1,0:T(8,128)(2,1)}, bf16[2,2,96,768]{3,2,1,0:T(8,128)(2,1)}, f32[3,384,256]{2,1,0:T(8,12...) custom-call(bf16[2,96,512]{2,1,0:T(8,128)(2,1)} %get-tuple-element.16.first, bf16[2,96,768]{2,1,0:T(8,128)(2,1)} %get-tuple-element.17.sp_own, ...), custom_call_target="tpu_custom_call" | custom-call | tf_op jit(solution)/shard_map/pallas_call | solution.py:872
  134.6 3.1 %shard_map.112 = (bf16[96,1024]{1,0:T(8,128)(2,1)}, bf16[8,96,256]{2,1,0:T(8,128)(2,1)}) custom-call(s32[4]{0:T(128)} %counts.3, s32[8,128]{1,0:T(8,128)} %k_hbm.3, bf16[2,96,512]{2,1,0:T(8,128)(2,1)} %get-tuple-element.19.own_hbm, bf16[2,96,768]{2,1,0:T(8,128)(2,1)} %get-tuple-element.20.buf_hbm, bf16[2,2,96,768]{3,2,1,0:T(8,128)(2,1)} %get-tuple-element.21.got_hbm), custom_call_target="tpu_custom_call" | custom-call | tf_op jit(solution)/shard_map/pallas_call | solution.py:889
  137.7 0.7 slice.3
  138.4 0.6 dynamic-slice_bitcast_fusion
  139.0 0.0 copy-start
  139.0 2.4 %copy.14 = f32[384,3,256]{2,0,1:T(8,128)} copy(f32[384,3,256]{2,0,1:T(8,128)} %bitcast.10) | data formatting | bytes 2359296
  141.4 0.0 copy-done
  141.4 0.7 copy.15
Async XLA Ops:
  139.0 2.4 %copy-start = (f32[256,384]{1,0:T(8,128)S(1)}, f32[256,384]{1,0:T(8,128)}, u32[]{:S(2)}) copy-start(f32[256,384]{1,0:T(8,128)} %get-tuple-element.35) | copy-start | bytes 1179652

commit v4 on v3

--- a/solution.py
+++ b/solution.py
@@ -100,12 +100,16 @@
             self.free_at = jnp.where(here, free_at, self.free_at)
             spare_at, free_at = spare_at + spare, free_at + free
 
-    def sent(self, slot):
-        k = slot - self.spare_at
-        return (k >= 0) & (k < self.extra), clamp(SLOTS + k, 2 * SLOTS - 1)
-
-    def taken(self, position):
-        return position < self.own, clamp(self.free_at + position - self.own, SPARE - 1)
+    def holds(self, slot, image):
+        k = image - SLOTS
+        return jnp.where((self.spare_at + k == slot) & (k < self.extra), 1.0, 0.0)
+
+    def keeps(self, position):
+        return jnp.where(position < self.own, 1.0, 0.0)
+
+    def works(self, position, slot):
+        k = position - self.own
+        return jnp.where((k >= 0) & (self.free_at + k == slot), 1.0, 0.0)
 
 
 class SmallSum:
@@ -156,7 +160,7 @@
     def __init__(self, place, own, got, fwd, send, recv):
         self.dp, self.own, self.got, self.fwd, self.send, self.recv = place.dp, own, got, fwd, send, recv
         self.near = [{"dp": place.dps[1]}, {"dp": place.dps[3]}]
-        self.width = own.shape[2] // CHUNKS
+        self.width = own.shape[1] // CHUNKS
 
     def lanes(self, ch):
         return pl.ds(ch * self.width, self.width)
@@ -164,15 +168,15 @@
     def copy(self, way, ch, first):
         src = self.own if first else self.fwd.at[way]
         return remote(
-            src.at[:, :, self.lanes(ch)], self.got.at[way, :, :, self.lanes(ch)],
+            src.at[:, self.lanes(ch)], self.got.at[way, :, self.lanes(ch)],
             self.send.at[way, ch], self.recv.at[way, ch], self.near[way],
         )
 
     def forward(self, way, ch):
         self.copy(way, ch, False).wait_recv()
         here = self.lanes(ch)
-        self.fwd[way, :, :, here] = (
-            self.got[way, :, :, here].astype(F32) + self.own[:, :, here].astype(F32)
+        self.fwd[way, :, here] = (
+            self.got[way, :, here].astype(F32) + self.own[:, here].astype(F32)
         ).astype(BF16)
         self.copy(way, ch, False).start()
 
@@ -201,12 +205,12 @@
                 for ch in range(CHUNKS):
                     self.copy(way, ch, False).wait_send()
 
-    def slot(self, a, s):
+    def slot(self, s):
         here = slice(s * KEEP, (s + 1) * KEEP)
         return (
-            self.own[a, :, here].astype(F32)
-            + self.got[0, a, :, here].astype(F32)
-            + self.got[1, a, :, here].astype(F32)
+            self.own[:, here].astype(F32)
+            + self.got[0, :, here].astype(F32)
+            + self.got[1, :, here].astype(F32)
         )
 
 
@@ -240,7 +244,9 @@
     return out, dq, dk, dv
 
 
-def gather_rows(place, locs, alls, small, zsend, ysend, fsend, csend, recv, meanwhile):
+def gather_rows(
+    place, locs, alls, small, zsend, ysend, fsend, csend, recv, choose_second, meanwhile
+):
     width = locs[0].shape[0]
     me, sib, core = place.me, {"mrow": place.sib}, place.core
     right, left = {"mrow": place.ys[1]}, {"mrow": place.ys[3]}
@@ -264,15 +270,14 @@
         ncore[0] += 1
 
     for a in range(2):
+        if a == 1:
+            choose_second()
         push(a, locs[a], me, zsend.at[a], {"mrow": place.anti})
-    for a in range(2):
         push(a, locs[a], me, ysend.at[a, 0], right)
         push(a, locs[a], me, ysend.at[a, 1], left)
-    for a in range(2):
         push(a, locs[a], me, csend.at[a, 0], sib)
+        alls[a][span(me * width, width)] = locs[a][...]
     ncore[0] = 1
-    for a in range(2):
-        alls[a][span(me * width, width)] = locs[a][...]
     small.step()
     meanwhile()
     anti = place.anti
@@ -493,35 +498,11 @@
         c.wait_send()
 
 
-def prep_kernel(counts, p_hbm, k_hbm, c_hbm, own, spare, sel, p_ref, k_ref, c_ref, sem):
-    load(((p_hbm, p_ref), (k_hbm, k_ref), (c_hbm, c_ref)), sem)
-    share = Share(counts, lax.axis_index("dp"))
-    patch = lax.broadcasted_iota(jnp.int32, (p_ref.shape[2], KEEP), 0)
-
-    def put(out, place, img, mine):
-        flag = jnp.where(mine, 1.0, 0.0)
-        here = slice(place * KEEP, (place + 1) * KEEP)
-        pick = (patch == k_ref[pl.ds(img, 1), :]).astype(F32).astype(BF16)
-        out[0, :, here] = (dot(p_ref[img], pick, 1, 0) * flag).astype(BF16)
-        out[1, :, here] = (c_ref[:, span(img * KEEP, KEEP)].astype(F32) * flag).astype(BF16)
-
-    for j in range(SLOTS):
-        put(own, j, j, j < share.own)
-    for s in range(SPARE):
-        mine, img = share.sent(s)
-        put(spare, s, img, mine)
-    for j in range(SLOTS):
-        keep, slot = share.taken(j)
-        for s in range(SPARE):
-            flag = jnp.where((slot == s) & jnp.logical_not(keep), 1.0, 0.0)
-            sel[j * SPARE + s : j * SPARE + s + 1, :] = jnp.zeros((1, KEEP), F32) + flag
-
-
 def main_kernel(
-    first, sp_own, sel, g_ref, w_hbm, wo_hbm,
+    counts, p_hbm, k_hbm, c_hbm, g_hbm, w_hbm, wo_hbm,
     out_own, out_buf, out_got, gq_out, go_out, gain_out,
     x_loc, u_loc, x_all, u_all, normed, wt, wot,
-    sp_got, sp_fwd, rt_fwd,
+    p_ref, k_ref, c_ref, g_ref, sp_own, sp_got, sp_fwd, rt_fwd,
     box1, val1, box2, val2,
     q_part, m_part, work, bq, bm,
     a_part, n_part, cbox, ybuf, ysum, ztot, zbox,
@@ -531,29 +512,64 @@
     sq, sm, rq, rm,
     cs2, cr2, ys2, yr2, zs2, zr2, dxs, dxr, dzs, dzr, qzs, qzr, qys, qyr, wsem, ggs, ggr,
 ):
-    loads = [pltpu.make_async_copy(w_hbm, w_ref, wsem.at[0]), pltpu.make_async_copy(wo_hbm, wo_ref, wsem.at[1])]
+    pairs = (
+        (p_hbm, p_ref), (k_hbm, k_ref), (c_hbm, c_ref), (g_hbm, g_ref), (w_hbm, w_ref), (wo_hbm, wo_ref)
+    )
+    loads = [pltpu.make_async_copy(src, dst, wsem.at[i]) for i, (src, dst) in enumerate(pairs)]
     for c in loads:
         c.start()
     place = Place()
-    greet(place.peers())
+    peers = place.peers()
+    barrier = pltpu.get_barrier_semaphore()
+    for peer in peers:
+        pl.semaphore_signal(barrier, inc=1, device_id=peer, device_id_type=MESH)
     width = x_loc.shape[0]
     core, zh = place.core, place.zh
-    chain = Chain(place, sp_own, sp_got, sp_fwd, sps, spr)
-    chain.start()
-    chain.run()
-    spare = [[chain.slot(a, s) for s in range(SPARE)] for a in range(2)]
-    sums, squares = [], []
-    for j in range(SLOTS):
-        here = slice(j * KEEP, (j + 1) * KEEP)
+    share = Share(counts, place.dp)
+    patch = lax.broadcasted_iota(jnp.int32, (p_ref.shape[2], KEEP), 0)
+    for c in loads[:4]:
+        c.wait()
+
+    def lanes_of(i):
+        return slice(i * KEEP, (i + 1) * KEEP)
+
+    def kept(i):
+        pick = (patch == k_ref[i : i + 1, :]).astype(F32).astype(BF16)
+        return dot(p_ref[i], pick, 1, 0)
+
+    late = [(kept(i), c_ref[:, lanes_of(i)].astype(F32)) for i in range(SLOTS, 2 * SLOTS)]
+    for s in range(SPARE):
+        flags = [share.holds(s, i) for i in range(SLOTS, 2 * SLOTS)]
+        for a in range(2):
+            total = late[0][a] * flags[0]
+            for image, flag in zip(late[1:], flags[1:]):
+                total = total + image[a] * flag
+            sp_own[a, :, lanes_of(s)] = total.astype(BF16)
+    pl.semaphore_wait(barrier, len(peers))
+    chains = [
+        Chain(place, sp_own.at[a], sp_got.at[a], sp_fwd.at[a], sps.at[a], spr.at[a]) for a in range(2)
+    ]
+    for chain in chains:
+        chain.start()
+    first = [kept(j) for j in range(SLOTS)], [c_ref[:, lanes_of(j)].astype(F32) for j in range(SLOTS)]
+    keeps = [share.keeps(j) for j in range(SLOTS)]
+    works = [[share.works(j, s) for s in range(SPARE)] for j in range(SLOTS)]
+
+    def choose(a, loc):
+        chains[a].run()
+        spare = [chains[a].slot(s) for s in range(SPARE)]
         values = []
-        for a, loc in enumerate((x_loc, u_loc)):
-            v = first[a, :, here].astype(F32)
+        for j in range(SLOTS):
+            v = first[a][j] * keeps[j]
             for s in range(SPARE):
-                v = v + spare[a][s] * sel[j * SPARE + s : j * SPARE + s + 1, :]
-            loc[:, here] = v.astype(BF16)
+                v = v + spare[s] * works[j][s]
+            loc[:, lanes_of(j)] = v.astype(BF16)
             values.append(v)
-        sums.append(jnp.sum(values[0], axis=0, keepdims=True))
-        squares.append(jnp.sum(values[0] * values[0], axis=0, keepdims=True))
+        return values
+
+    values = choose(0, x_loc)
+    sums = [jnp.sum(v, axis=0, keepdims=True) for v in values]
+    squares = [jnp.sum(v * v, axis=0, keepdims=True) for v in values]
     me_row = lax.broadcasted_iota(jnp.int32, (16, KEEP), 0) == place.me
     gval[...] = jnp.zeros(gval.shape, F32)
     gval[:1, :width] = g_ref[...]
@@ -564,14 +580,15 @@
     small.start(jnp.concatenate(sums + squares + [own_gain], axis=0))
 
     def turn_weights():
-        for c in loads:
+        for c in loads[4:]:
             c.wait()
         for p in range(3):
             wt[p] = jnp.transpose(w_ref[p])
         wot[...] = jnp.transpose(wo_ref[...])
 
     stats = gather_rows(
-        place, (x_loc, u_loc), (x_all, u_all), small, zs1, ys1, fs1, cs1, r1, turn_weights
+        place, (x_loc, u_loc), (x_all, u_all), small, zs1, ys1, fs1, cs1, r1,
+        lambda: choose(1, u_loc), turn_weights,
     )
     gain_cols = jnp.transpose(
         jnp.concatenate([val1[3, 2 * SLOTS :], jnp.zeros((KEEP - 16, KEEP), F32)], axis=0)
@@ -726,45 +743,48 @@
     back = small.step()
     for r in (1, 3, 2):
         ring.forward(r)
-    for c in zcopies:
-        c.wait()
 
     mean_hat = back[:SLOTS] * (1.0 / D)
     mean_cross = back[SLOTS:] * (1.0 / D)
     gain_col = jnp.transpose(jnp.broadcast_to(gain_row, (KEEP, KEEP)))[:width, :1]
     acc = jnp.zeros((width, KEEP), F32)
-    for j in range(SLOTS):
-        here = slice(j * KEEP, (j + 1) * KEEP)
-        attn = ysum[0, zh, :, here] + zbox[0, :, here].astype(F32)
-        dn = ysum[1, zh, :, here] + zbox[1, :, here].astype(F32)
-        xv = x_loc[:, here].astype(F32)
-        centred = (xv - mean[j : j + 1]) * inv[j : j + 1]
-        acc = acc + dn * centred
-        d_in = u_loc[:, here].astype(F32) + inv[j : j + 1] * (
-            dn * gain_col - mean_hat[j : j + 1] - centred * mean_cross[j : j + 1]
-        )
-        out_own[0, :, here] = (xv + attn).astype(BF16)
-        out_own[1, :, here] = d_in.astype(BF16)
-    for s in range(SPARE):
-        for a in range(2):
-            value = jnp.zeros((width, KEEP), F32)
-            for j in range(SLOTS):
-                value = value + out_own[a, :, j * KEEP : (j + 1) * KEEP].astype(F32) * (
-                    sel[j * SPARE + s : j * SPARE + s + 1, :]
+    backs = [
+        Chain(place, out_buf.at[a], out_got.at[a], rt_fwd.at[a], rts.at[a], rtr.at[a]) for a in range(2)
+    ]
+    for a in range(2):
+        zcopies[a].wait()
+        results = []
+        for j in range(SLOTS):
+            here = lanes_of(j)
+            total = ysum[a, zh, :, here] + zbox[a, :, here].astype(F32)
+            xv = x_loc[:, here].astype(F32)
+            if a == 0:
+                result = xv + total
+            else:
+                centred = (xv - mean[j : j + 1]) * inv[j : j + 1]
+                acc = acc + total * centred
+                result = u_loc[:, here].astype(F32) + inv[j : j + 1] * (
+                    total * gain_col - mean_hat[j : j + 1] - centred * mean_cross[j : j + 1]
                 )
-            out_buf[a, :, s * KEEP : (s + 1) * KEEP] = value.astype(BF16)
+            out_own[a, :, here] = result.astype(BF16)
+            results.append(result)
+        for s in range(SPARE):
+            total = results[0] * works[0][s]
+            for j in range(1, SLOTS):
+                total = total + results[j] * works[j][s]
+            out_buf[a, :, lanes_of(s)] = total.astype(BF16)
+        backs[a].start()
     gain_row = jnp.sum(
         jnp.transpose(jnp.concatenate([acc, jnp.zeros((KEEP - width, KEEP), F32)], axis=0)),
         axis=0, keepdims=True,
     )
     gval[...] = jnp.broadcast_to(gain_row, gval.shape)
-    back_chain = Chain(place, out_buf, out_got, rt_fwd, rts, rtr)
-    back_chain.start()
     gains = []
     for k in range(3):
         c = remote(gval, gbox.at[k], ggs.at[k], ggr.at[k], {"dp": place.dps[k + 1]})
         c.start()
         gains.append(c)
+    backs[0].run()
     fetch.finish()
     quarter = quarters.shape[2]
     for a, arr in enumerate((normed, u_all)):
@@ -780,7 +800,7 @@
     for r in range(1, 4):
         total = total + dot(dh[r, 3 * part :], quarters[1, r], 1, 1)
     go_out[...] = total
-    back_chain.run()
+    backs[1].run()
     total = gval[...]
     for k, c in enumerate(gains):
         c.wait()
@@ -790,15 +810,26 @@
         c.wait_send()
 
 
-def post_kernel(n, counts, k_hbm, own_hbm, buf_hbm, got_hbm, out, dp_out, k_ref, own_ref, buf_ref, got_ref, sem):
-    load(((k_hbm, k_ref), (own_hbm, own_ref), (buf_hbm, buf_ref), (got_hbm, got_ref)), sem)
-    share = Share(counts, lax.axis_index("dp"))
+def post_kernel(
+    n, counts, k_hbm, own_hbm, buf_hbm, got_hbm, gg_hbm, gq_hbm, go_hbm,
+    out, dp_out, gain_out, gq_out, go_out, k_ref, own_ref, buf_ref, got_ref, gg_ref, sem, osem,
+):
+    through = [
+        pltpu.make_async_copy(src, dst, osem.at[i])
+        for i, (src, dst) in enumerate(((gq_hbm, gq_out), (go_hbm, go_out)))
+    ]
+    for c in through:
+        c.start()
+    load(
+        ((k_hbm, k_ref), (own_hbm, own_ref), (buf_hbm, buf_ref), (got_hbm, got_ref), (gg_hbm, gg_ref)), sem
+    )
+    dp = lax.axis_index("dp")
+    share = Share(counts, dp)
     patch = lax.broadcasted_iota(jnp.int32, (dp_out.shape[2], KEEP), 0)
     for i in range(n):
         lanes = slice(i * KEEP, (i + 1) * KEEP)
         if i < SLOTS:
-            flag = jnp.where(i < share.own, 1.0, 0.0)
-            res, d_in = (own_ref[a, :, lanes].astype(F32) * flag for a in range(2))
+            res, d_in = (own_ref[a, :, lanes].astype(F32) * share.keeps(i) for a in range(2))
         else:
             slot = clamp(share.spare_at + i - SLOTS, SPARE - 1)
             flag = jnp.where(i - SLOTS < share.extra, 1.0, 0.0)
@@ -806,8 +837,8 @@
             res, d_in = (
                 (
                     buf_ref[a, :, here].astype(F32)
-                    + got_ref[0, a, :, here].astype(F32)
-                    + got_ref[1, a, :, here].astype(F32)
+                    + got_ref[a, 0, :, here].astype(F32)
+                    + got_ref[a, 1, :, here].astype(F32)
                 )
                 * flag
                 for a in range(2)
@@ -815,6 +846,13 @@
         pick = (patch == k_ref[i : i + 1, :]).astype(F32).astype(BF16)
         out[:, lanes] = res.astype(BF16)
         dp_out[i] = dot(d_in.astype(BF16), pick, 1, 1).astype(BF16)
+    part = gain_out.shape[1]
+    for g in range(4):
+        @pl.when(dp == g)
+        def _():
+            gain_out[...] = gg_ref[:1, g * part : (g + 1) * part]
+    for c in through:
+        c.wait()
 
 
 def sharded(patches, keep_index, counts, gain, w_qkv, w_out, cotangent):
@@ -837,7 +875,8 @@
     scratch = [
         v((width, rows)), v((width, rows)), v((feats, rows)), v((feats, rows)), v((feats, rows)),
         v((3, heads, feats)), v((feats, heads)),
-        v((2, 2, width, spare)), v((2, 2, width, spare)), v((2, 2, width, spare)),
+        v((n, width, patch_count)), v((n, KEEP), jnp.int32), v((width, total_rows)), v((1, width), F32),
+        v((2, width, spare)), v((2, 2, width, spare)), v((2, 2, width, spare)), v((2, 2, width, spare)),
         v((8, small, KEEP), F32), v((4, small, KEEP), F32),
         v((8, 2 * SLOTS, KEEP), F32), v((4, 2 * SLOTS, KEEP), F32),
         v((heads3, rows)), v((heads, rows)),
@@ -849,26 +888,13 @@
         v((3, 8, KEEP), F32), v((8, KEEP), F32),
         DMA((8,)), DMA((8,)), DMA((8,)), DMA((8,)),
         DMA((2,)), DMA((2, 4)), DMA((2, 2)), DMA((2, 8)), DMA((2, 16)),
-        DMA((2, CHUNKS)), DMA((2, CHUNKS)), DMA((2, CHUNKS)), DMA((2, CHUNKS)),
+        DMA((2, 2, CHUNKS)), DMA((2, 2, CHUNKS)), DMA((2, 2, CHUNKS)), DMA((2, 2, CHUNKS)),
         DMA((6,)), DMA((6,)), DMA((6,)), DMA((6,)),
         DMA((2, 4, 2)), DMA((2, 4, 2)), DMA((2, 3)), DMA((2, 3)), DMA((2,)), DMA((2,)),
         DMA((4, 2, 3)), DMA((4, 2, 4)), DMA((4,)), DMA((4,)), DMA((2, 4)), DMA((2, 4)),
-        DMA((2, 8)), DMA((2, 8)), DMA((2,)), DMA((3,)), DMA((3,)),
+        DMA((2, 8)), DMA((2, 8)), DMA((6,)), DMA((3,)), DMA((3,)),
     ]
     shape = jax.ShapeDtypeStruct
-    first, spare_own, sel = pl.pallas_call(
-        prep_kernel,
-        out_shape=[
-            shape((2, width, rows), BF16), shape((2, width, spare), BF16),
-            shape((SLOTS * SPARE, KEEP), F32),
-        ],
-        in_specs=[SM] + [ANY] * 3,
-        out_specs=[VM] * 3,
-        scratch_shapes=[
-            v((n, width, patch_count)), v((n, KEEP), jnp.int32), v((width, total_rows)), DMA((3,))
-        ],
-        compiler_params=pltpu.CompilerParams(vmem_limit_bytes=58 * 1024 * 1024),
-    )(counts, jnp.transpose(patches, (0, 2, 1)), keep_index, cotangent.T)
     out_own, out_buf, out_got, gq, go, gg = pl.pallas_call(
         main_kernel,
         out_shape=[
@@ -877,30 +903,34 @@
             shape((3, quarter, heads), F32), shape((heads, quarter), F32),
             shape((8, KEEP), F32),
         ],
-        in_specs=[VM] * 4 + [ANY] * 2,
+        in_specs=[SM] + [ANY] * 6,
         out_specs=[VM] * 6,
         scratch_shapes=scratch,
         compiler_params=pltpu.CompilerParams(
             vmem_limit_bytes=58 * 1024 * 1024, collective_id=1, has_side_effects=True
         ),
     )(
-        first, spare_own, sel, gain_row, jnp.transpose(w_qkv, (1, 0, 2)), w_out,
-    )
-    outputs, d_patches = pl.pallas_call(
+        counts, jnp.transpose(patches, (0, 2, 1)), keep_index, cotangent.T, gain_row,
+        jnp.transpose(w_qkv, (1, 0, 2)), w_out,
+    )
+    part = width // 4
+    outputs, d_patches, grad_gain, gq, go = pl.pallas_call(
         partial(post_kernel, n),
-        out_shape=[shape((width, total_rows), BF16), shape((n, width, patch_count), BF16)],
-        in_specs=[SM] + [ANY] * 4,
-        out_specs=[VM] * 2,
+        out_shape=[
+            shape((width, total_rows), BF16), shape((n, width, patch_count), BF16), shape((1, part), F32),
+            shape(gq.shape, F32), shape(go.shape, F32),
+        ],
+        in_specs=[SM] + [ANY] * 7,
+        out_specs=[VM] * 3 + [ANY] * 2,
         scratch_shapes=[
             v((n, KEEP), jnp.int32), v((2, width, rows)), v((2, width, spare)), v((2, 2, width, spare)),
-            DMA((4,)),
+            v((8, KEEP), F32), DMA((5,)), DMA((2,)),
         ],
         compiler_params=pltpu.CompilerParams(vmem_limit_bytes=58 * 1024 * 1024),
-    )(counts, keep_index, out_own, out_buf, out_got)
-    part = width // 4
-    grad_gain = lax.dynamic_slice(gg[0], (lax.axis_index("dp") * part,), (part,))
+    )(counts, keep_index, out_own, out_buf, out_got, gg, gq, go)
     return (
-        outputs.T, jnp.transpose(d_patches, (0, 2, 1)), jnp.transpose(gq, (1, 0, 2)), go, grad_gain
+        outputs.T, jnp.transpose(d_patches, (0, 2, 1)), jnp.transpose(gq, (1, 0, 2)), go,
+        grad_gain.reshape(part),
     )
 
 

time: 144 us -> 191 us (1.33)
  Pallas kernels: 137 us -> 188 us
  local copies, waits for them, and re-layouts: 4.43 us -> 0 us
    pallas_call x1, Pallas kernels: 3.1 us -> 50.3 us  [sharded(): pl.pallas_call(partial(post_kernel, n), out_shape=[shape((width, total_ro...]
    pallas_call x1, Pallas kernels: 131 us -> 138 us  [sharded(): pl.pallas_call(main_kernel, out_shape=[shape((2, width, rows), BF16), sha...]
    unnamed x4 -> x0, local copies, waits for them, and re-layouts: 3.16 us -> none
    pallas_call x1 -> x0, Pallas kernels: 2.81 us -> none  [sharded(): pl.pallas_call(prep_kernel, out_shape=[shape((2, width, rows), BF16), sha...]
where the time goes in v4:
time: 191 us; the launch traced here: 189 us
  Pallas kernels  188 us (98%)
    pallas_call x1, Pallas kernels, sharded(): pl.pallas_call(main_kernel, out_shape=[shape((2, width, rows), BF16), sha...  138 us
    pallas_call x1, Pallas kernels, sharded(): pl.pallas_call(partial(post_kernel, n), out_shape=[shape((width, total_ro...  50.3 us

profile of v4, /device:TPU:0, one launch (start us, length us, event | category | flops | bytes accessed | tf_op | source)
XLA Modules:
  0.0 188.8 jit_solution(17193489793080573494)
XLA Ops:
  0.6 137.9 %shard_map.110 = (bf16[2,96,512]{2,1,0:T(8,128)(2,1)}, bf16[2,96,768]{2,1,0:T(8,128)(2,1)}, bf16[2,2,96,768]{3,2,1,0:T(8,128)(2,1)}, f32[3,384,256]{2,1,0:T(8,12...) custom-call(s32[4]{0:T(128)} %counts.3, bf16[8,96,256]{2,1,0:T(8,128)(2,1)} %bitcast.9, s32[8,128]{1,0:T(8,128)} %k_hbm.3, ...), custom_call_target="tpu_custom_call" | custom-call | tf_op jit(solution)/shard_map/pallas_call | solution.py:898
  138.6 50.3 %shard_map.111 = (bf16[96,1024]{1,0:T(8,128)(2,1)}, bf16[8,96,256]{2,1,0:T(8,128)(2,1)}, f32[1,24]{1,0:T(1,128)}, f32[3,384,256]{2,1,0:T(8,128)}, f32[256,384]{1,0:T(8,128)}) custom-call(s32[4]{0:T(128)} %counts.3, s32[8,128]{1,0:T(8,128)} %k_hbm.3, bf16[2,96,512]{2,1,0:T(8,128)(2,1)} %get-tuple-element.16.own_hbm, ...), custom_call_target="tpu_custom_call" | custom-call | tf_op jit(solution)/shard_map/pallas_call | solution.py:917

commit v5 on v4

v5 whole, which is shorter than its diff:
```python
import heapq
from functools import partial

import jax
import jax.numpy as jnp
from jax import lax
from jax.experimental import pallas as pl
from jax.experimental.pallas import tpu as pltpu
from jax.sharding import PartitionSpec as P

D = 6144
HD = 128
KEEP = 128
SLOTS = 4
SPARE = 6
CHUNKS = 3
EPSILON = 1e-06

F32 = jnp.float32
BF16 = jnp.bfloat16
MESH = pl.DeviceIdType.MESH
VM = pl.BlockSpec(memory_space=pltpu.VMEM)
SM = pl.BlockSpec(memory_space=pltpu.SMEM)
ANY = pl.BlockSpec(memory_space=pl.ANY)
DMA = pltpu.SemaphoreType.DMA


def dot(a, b, ca, cb):
    return lax.dot_general(a, b, (((ca,), (cb,)), ((), ())), preferred_element_type=F32)


def remote(src, dst, send, recv, where):
    return pltpu.make_async_remote_copy(
        src_ref=src, dst_ref=dst, send_sem=send, recv_sem=recv, device_id=where, device_id_type=MESH
    )


def clamp(value, top):
    return jnp.minimum(jnp.maximum(value, 0), top)


def greet(peers):
    barrier = pltpu.get_barrier_semaphore()
    for peer in peers:
        pl.semaphore_signal(barrier, inc=1, device_id=peer, device_id_type=MESH)
    pl.semaphore_wait(barrier, len(peers))


def span(start, size, step=None):
    return pl.ds(pl.multiple_of(start, step or size), size)


class Event:
    done = False


class Plan:
    def __init__(self):
        self.now, self.count, self.queue, self.parked = 0.0, 0, [], []

    def add(self, flow, delay=0.0):
        self.count += 1
        heapq.heappush(self.queue, (self.now + delay, self.count, flow))

    def run(self):
        while self.queue:
            at, _, flow = heapq.heappop(self.queue)
            self.now = max(self.now, at)
            want = next(flow, None)
            if isinstance(want, tuple):
                self.parked.append((want, flow))
            elif want is not None:
                self.add(flow, want)
            waiting, self.parked = self.parked, []
            for events, other in waiting:
                if all(e.done for e in events):
                    self.add(other)
                else:
                    self.parked.append((events, other))
        assert not self.parked


def load(pairs, sem):
    copies = [pltpu.make_async_copy(src, dst, sem.at[i]) for i, (src, dst) in enumerate(pairs)]
    for c in copies:
        c.start()
    for c in copies:
        c.wait()


class Place:
    def __init__(self):
        self.me = lax.axis_index("mrow")
        self.core = lax.rem(self.me, 2)
        self.y = lax.rem(lax.div(self.me, 2), 4)
        self.zh = lax.div(self.me, 8)
        self.x = lax.axis_index("mcol")
        self.dp = lax.axis_index("dp")
        self.sib = self.at(self.zh, 0, 1 - self.core)
        self.anti = self.at(1 - self.zh, 0, self.core)
        self.ys = [self.at(self.zh, d, self.core) for d in range(4)]
        self.xs = [lax.rem(self.x + d, 4) for d in range(4)]
        self.dps = [lax.rem(self.dp + d, 4) for d in range(4)]

    def at(self, zh, dy, core):
        return zh * 8 + lax.rem(self.y + dy, 4) * 2 + core

    def peers(self):
        rows = [self.sib, self.anti] + self.ys[1:]
        return (
            [{"mrow": r} for r in rows]
            + [{"mcol": c} for c in self.xs[1:]]
            + [{"dp": c} for c in self.dps[1:]]
        )


class Share:
    def __init__(self, counts, dp):
        c = [counts[g] for g in range(4)]
        keep = [jnp.minimum(v, SLOTS) for v in c]
        zero = jnp.int32(0)
        self.own = self.extra = self.spare_at = self.free = self.free_at = zero
        spare_at = free_at = zero
        for g in range(4):
            here = dp == g
            spare, free = c[g] - keep[g], SLOTS - keep[g]
            self.own = jnp.where(here, keep[g], self.own)
            self.extra = jnp.where(here, spare, self.extra)
            self.free = jnp.where(here, free, self.free)
            self.spare_at = jnp.where(here, spare_at, self.spare_at)
            self.free_at = jnp.where(here, free_at, self.free_at)
            spare_at, free_at = spare_at + spare, free_at + free

    def holds(self, slot, image):
        k = image - SLOTS
        return jnp.where((self.spare_at + k == slot) & (k < self.extra), 1.0, 0.0)

    def keeps(self, position):
        return jnp.where(position < self.own, 1.0, 0.0)

    def works(self, position, slot):
        k = position - self.own
        return jnp.where((k >= 0) & (self.free_at + k == slot), 1.0, 0.0)


class SmallSum:
    def __init__(self, place, val, box, send, recv, x_rows):
        self.place, self.val, self.box = place, val, box
        self.send, self.recv, self.x_rows = send, recv, x_rows
        self.live = []
        self.n = 0

    def push(self, peers, rows=None):
        self.live = []
        for where in peers:
            k = self.n
            self.n += 1
            stage = self.val.at[self.stage]
            box = self.box.at[k]
            if rows is not None:
                stage, box = stage.at[:rows], box.at[:rows]
            c = remote(stage, box, self.send.at[k], self.recv.at[k], where)
            c.start()
            self.live.append((k, c))

    def start(self, value):
        self.stage = 0
        self.val[0] = value
        self.push([{"mrow": self.place.sib}])

    def step(self):
        total = self.val[self.stage]
        rows = self.x_rows if self.stage == 3 else total.shape[0]
        total = total[:rows]
        for k, c in self.live:
            c.wait()
            total = total + self.box[k, :rows]
        self.stage += 1
        if self.stage < 4:
            self.val[self.stage] = total
        if self.stage == 1:
            self.push([{"mrow": r} for r in self.place.ys[1:]])
        elif self.stage == 2:
            self.push([{"mrow": self.place.anti}])
        elif self.stage == 3:
            self.push([{"mcol": c} for c in self.place.xs[1:]], self.x_rows)
        return total


class Chain:
    def __init__(self, place, own, got, fwd, send, recv):
        self.dp, self.own, self.got, self.fwd, self.send, self.recv = place.dp, own, got, fwd, send, recv
        self.near = [{"dp": place.dps[1]}, {"dp": place.dps[3]}]
        self.width = own.shape[1] // CHUNKS

    def lanes(self, ch):
        return pl.ds(ch * self.width, self.width)

    def copy(self, way, ch, first):
        src = self.own if first else self.fwd.at[way]
        return remote(
            src.at[:, self.lanes(ch)], self.got.at[way, :, self.lanes(ch)],
            self.send.at[way, ch], self.recv.at[way, ch], self.near[way],
        )

    def forward(self, way, ch):
        self.copy(way, ch, False).wait_recv()
        here = self.lanes(ch)
        self.fwd[way, :, here] = (
            self.got[way, :, here].astype(F32) + self.own[:, here].astype(F32)
        ).astype(BF16)
        self.copy(way, ch, False).start()

    def start(self):
        for dp, way in ((0, 0), (3, 1)):
            @pl.when(self.dp == dp)
            def _():
                for ch in range(CHUNKS):
                    self.copy(way, ch, True).start()
                self.got[way] = jnp.zeros(self.got.shape[1:], BF16)

    def flow(self):
        for way, ch, after in (
            (0, 0, 3.5), (0, 1, 1.0), (1, 0, 2.5), (0, 2, 0.0), (1, 1, 1.0), (1, 2, 1.0)
        ):
            yield after
            for dp, w in ((1, way), (2, 1 - way)):
                @pl.when(self.dp == dp)
                def _():
                    self.forward(w, ch)
        yield 3.5
        for dp, way in ((0, 1), (3, 0)):
            @pl.when(self.dp == dp)
            def _():
                for ch in range(CHUNKS):
                    self.copy(way, ch, False).wait_recv()

    def drain(self):
        for way, last in ((0, 3), (1, 0)):
            @pl.when(self.dp != last)
            def _():
                for ch in range(CHUNKS):
                    self.copy(way, ch, False).wait_send()

    def slot(self, s):
        here = slice(s * KEEP, (s + 1) * KEEP)
        return (
            self.own[:, here].astype(F32)
            + self.got[0, :, here].astype(F32)
            + self.got[1, :, here].astype(F32)
        )


def attend(q, k, v, do):
    def norm(t):
        c = t - jnp.mean(t, axis=0, keepdims=True)
        i = lax.rsqrt(jnp.mean(c * c, axis=0, keepdims=True) + EPSILON)
        return c * i, i

    def norm_back(d, y, i):
        return i * (
            d - jnp.mean(d, axis=0, keepdims=True) - y * jnp.mean(d * y, axis=0, keepdims=True)
        )

    def mm(a, b, ca, cb):
        return lax.dot_general(
            a, b, (((ca,), (cb,)), ((), ())), preferred_element_type=F32, precision=lax.Precision.HIGHEST
        )

    scale = HD ** (-0.5)
    qn, iq = norm(q)
    kn, ik = norm(k)
    w = jnp.exp(mm(kn, qn, 0, 0) * scale)
    w = w / jnp.sum(w, axis=0, keepdims=True)
    out = mm(v, w, 1, 0)
    dw = mm(v, do, 0, 0)
    ds = w * (dw - jnp.sum(w * dw, axis=0, keepdims=True)) * scale
    dv = mm(do, w, 1, 1)
    dq = norm_back(mm(kn, ds, 1, 0), qn, iq)
    dk = norm_back(mm(qn, ds, 1, 1), kn, ik)
    return out, dq, dk, dv


def gather_rows(place, loc, out, send, recv, sends):
    width, rows = loc.shape
    half = rows // 2
    me, sib, core = place.me, {"mrow": place.sib}, place.core
    right, left = {"mrow": place.ys[1]}, {"mrow": place.ys[3]}
    count = [0]

    def view(slot, part=None):
        block = out.at[span(slot * width, width)]
        return block if part is None else block.at[:, pl.ds(part * half, half)]

    def push(slot, where, part=None, src=None):
        k = count[0]
        count[0] += 1
        c = remote(
            view(slot, part) if src is None else src, view(slot, part),
            send.at[k], recv.at[slot, part or 0], where,
        )
        c.start()
        sends.append(c)

    def got(slot, part=None):
        remote(view(slot, part), view(slot, part), send.at[0], recv.at[slot, part or 0], sib).wait_recv()

    push(me, {"mrow": place.anti}, src=loc)
    push(me, right, src=loc)
    push(me, left, src=loc)
    push(me, sib, src=loc)
    out[span(me * width, width)] = loc[...]

    def ring(zh):
        before, after = place.at(zh, 3, core), place.at(zh, 1, core)
        got(before)
        push(before, right, 0)
        got(after)
        push(after, left, 1)
        push(before, sib)
        push(after, sib)

    def far(zh):
        slot = place.at(zh, 2, core)
        got(slot, 0)
        got(slot, 1)
        push(slot, sib)

    yield 4.0
    ring(place.zh)
    yield 3.5
    got(place.anti)
    push(place.anti, right)
    push(place.anti, left)
    push(place.anti, sib)
    yield 0.5
    far(place.zh)
    yield 4.0
    ring(1 - place.zh)
    yield 4.0
    far(1 - place.zh)
    yield 2.0
    for zh in range(2):
        for dy in range(4):
            got(place.at(zh, dy, 1 - core))


class ReduceX:
    def __init__(self, place, src, buf, fwd, send, recv):
        self.place, self.src, self.buf, self.fwd, self.send, self.recv = place, src, buf, fwd, send, recv
        self.half, self.width = buf.shape[1], buf.shape[2]

    def view(self, p, block):
        return self.src.at[pl.ds(p * self.half, self.half), span(block * self.width, self.width)]

    def push(self, src, slot, where, sends):
        c = remote(src, self.buf.at[slot], self.send.at[slot], self.recv.at[slot], where)
        c.start()
        sends.append(c)

    def got(self, slot):
        b = self.buf.at[slot]
        remote(b, b, self.send.at[slot], self.recv.at[slot], {"mcol": self.place.xs[1]}).wait_recv()

    def flow(self, sends):
        xs = self.place.xs
        right, left = {"mcol": xs[1]}, {"mcol": xs[3]}
        self.push(self.view(0, xs[2]), 0, right, sends)
        self.push(self.view(1, xs[2]), 1, left, sends)
        self.push(self.view(0, xs[3]), 2, left, sends)
        self.push(self.view(1, xs[1]), 3, right, sends)
        yield 4.0
        for p, (at, where) in enumerate(((xs[1], right), (xs[3], left))):
            self.got(p)
            self.fwd[p] = (self.buf[p].astype(F32) + self.view(p, at)[...].astype(F32)).astype(BF16)
            self.push(self.fwd.at[p], 4 + p, where, sends)
        yield 4.0
        for slot in range(2, 6):
            self.got(slot)

    def total(self, r0):
        p, r = divmod(r0, self.half)
        here = slice(r, r + HD)
        return (
            self.src[r0 : r0 + HD, span(self.place.x * self.width, self.width)].astype(F32)
            + self.buf[2 + p, here].astype(F32)
            + self.buf[4 + p, here].astype(F32)
        )


class RingX:
    def __init__(self, place, dh, slot, start, rows, send, recv):
        self.x, self.xs, self.view = place.x, place.xs, dh.at[slot, pl.ds(start, rows)]
        self.send, self.recv = send, recv
        self.right, self.left = {"mcol": place.xs[1]}, {"mcol": place.xs[3]}
        self.half, self.width = rows // 2, dh.shape[2] // 4

    def copy(self, p, block, k, where):
        view = self.view.at[pl.ds(p * self.half, self.half), span(block * self.width, self.width)]
        return remote(view, view, self.send.at[p, k], self.recv.at[p, block], where)

    def push(self, p, block, k, where, sends):
        c = self.copy(p, block, k, where)
        c.start()
        sends.append(c)

    def got(self, p, block):
        self.copy(p, block, 0, self.right).wait_recv()

    def flow(self, sends, pace):
        xs = self.xs
        for p in range(2):
            self.push(p, self.x, 0, self.right, sends)
            self.push(p, self.x, 1, self.left, sends)
        yield pace
        self.got(0, xs[3])
        self.push(0, xs[3], 2, self.right, sends)
        self.got(1, xs[1])
        self.push(1, xs[1], 2, self.left, sends)
        yield pace
        self.got(1, xs[3])
        self.got(0, xs[1])
        self.got(0, xs[2])
        self.got(1, xs[2])


class Quarter:
    def __init__(self, place, array, out, zsend, zrecv, send, recv, sends):
        self.place, self.array, self.out = place, array, out
        self.zsend, self.zrecv, self.send, self.recv, self.sends = zsend, zrecv, send, recv, sends
        self.share = out.shape[1] // 8
        self.n = 0

    def index(self, dy, core):
        return lax.rem(self.place.y + dy, 4) * 2 + core

    def view(self, index, part=None):
        rows = span(index * self.share, self.share)
        half = self.out.shape[2] // 2
        return self.out.at[1:4, rows] if part is None else self.out.at[1:4, rows, pl.ds(part * half, half)]

    def zcopy(self, r):
        dp, mine = self.place.dps[r], self.index(0, self.place.core)
        src = self.array.at[span(dp * self.out.shape[1] + mine * self.share, self.share)]
        dst = self.out.at[r, span(mine * self.share, self.share)]
        return remote(src, dst, self.zsend.at[r], self.zrecv.at[r], {"dp": dp})

    def copy(self, index, where, part, k):
        view = self.view(index, part)
        return remote(view, view, self.send.at[k], self.recv.at[index, part or 0], where)

    def push(self, index, where, part=None):
        c = self.copy(index, where, part, self.n)
        self.n += 1
        c.start()
        self.sends.append(c)

    def got(self, index, part=None):
        self.copy(index, {"mrow": self.place.sib}, part, 0).wait_recv()

    def flow(self):
        place, core = self.place, self.place.core
        right, left, sib = {"mrow": place.ys[1]}, {"mrow": place.ys[3]}, {"mrow": place.sib}
        for r in (1, 3, 2):
            self.zcopy(r).start()
        yield 9.0
        mine, before, after, far = (self.index(d, core) for d in (0, 3, 1, 2))
        for r in (1, 3, 2):
            self.zcopy(r).wait()
        for where in (right, left, sib):
            self.push(mine, where)
        yield 7.0
        self.got(before)
        self.push(before, right, 0)
        self.got(after)
        self.push(after, left, 1)
        self.push(before, sib)
        self.push(after, sib)
        yield 6.0
        self.got(far, 0)
        self.got(far, 1)
        self.push(far, sib)
        yield 6.0
        for dy in range(4):
            self.got(self.index(dy, 1 - core))


class ReduceRows:
    def __init__(self, place, array, cbox, ybuf, ysum, ztot, zbox, csem, ysem, zsem, sends):
        self.place, self.array, self.cbox, self.ybuf = place, array, cbox, ybuf
        self.ysum, self.ztot, self.zbox = ysum, ztot, zbox
        self.csem, self.ysem, self.zsem, self.sends = csem, ysem, zsem, sends
        self.width, self.rows = ztot.shape

    def target(self, z, d, c):
        return self.array.at[span(self.place.at(z, d, c) * self.width, self.width)]

    def core_copy(self, d, z):
        return remote(
            self.target(z, d, 1 - self.place.core), self.cbox.at[d, z],
            self.csem[0].at[d, z], self.csem[1].at[d, z], {"mrow": self.place.sib},
        )

    def add(self, d, srcs, lanes=slice(None)):
        for z in range(2):
            @pl.loop(0, self.width // 16)
            def _(i):
                r = span(i * 16, 16)
                total = self.cbox[d, z, r, lanes].astype(F32)
                for s in srcs:
                    total = total + s[z][r, lanes].astype(F32)
                self.cbox[d, z, r, lanes] = total.astype(BF16)

    def core_sum(self, d):
        for z in range(2):
            self.core_copy(d, z).wait_recv()
        self.add(d, [[self.target(z, d, self.place.core) for z in range(2)]])

    def ypush(self, d, slot, lanes, k, where):
        c = remote(
            self.cbox.at[d, :, :, lanes], self.ybuf.at[slot, :, :, lanes],
            self.ysem[0].at[k], self.ysem[1].at[k], where,
        )
        c.start()
        self.sends.append(c)

    def ygot(self, slot, lanes, k):
        b = self.ybuf.at[slot, :, :, lanes]
        remote(b, b, self.ysem[0].at[k], self.ysem[1].at[k], {"mrow": self.place.sib}).wait_recv()

    def flow(self):
        place = self.place
        right, left = {"mrow": place.ys[1]}, {"mrow": place.ys[3]}
        lo, hi = pl.ds(0, self.rows // 2), pl.ds(self.rows // 2, self.rows // 2)
        for d in (2, 1, 3, 0):
            for z in range(2):
                c = self.core_copy(d, z)
                c.start()
                self.sends.append(c)
        yield 2.5
        self.core_sum(2)
        self.ypush(2, 0, lo, 0, right)
        self.ypush(2, 1, hi, 1, left)
        self.core_sum(1)
        self.ypush(1, 2, hi, 3, right)
        self.core_sum(3)
        self.ypush(3, 3, lo, 4, left)
        self.core_sum(0)
        yield 3.0
        self.ygot(0, lo, 0)
        self.add(1, [[self.ybuf.at[0, z] for z in range(2)]], lo)
        self.ypush(1, 2, lo, 2, right)
        self.ygot(1, hi, 1)
        self.add(3, [[self.ybuf.at[1, z] for z in range(2)]], hi)
        self.ypush(3, 3, hi, 5, left)
        yield 4.0
        for slot, lanes, k in ((2, hi, 3), (3, lo, 4), (2, lo, 2), (3, hi, 5)):
            self.ygot(slot, lanes, k)

        @pl.loop(0, self.width // 16)
        def _(i):
            r = span(i * 16, 16)
            for z in range(2):
                self.ysum[z, r] = (
                    self.cbox[0, z, r].astype(F32)
                    + self.ybuf[2, z, r].astype(F32)
                    + self.ybuf[3, z, r].astype(F32)
                )
            self.ztot[r] = self.ysum[1 - place.zh, r].astype(BF16)

        c = remote(self.ztot, self.zbox, self.zsem[0], self.zsem[1], {"mrow": place.anti})
        c.start()
        self.sends.append(c)
        yield 8.0
        c.wait_recv()

    def result(self, lanes):
        return self.ysum[self.place.zh, :, lanes] + self.zbox[:, lanes].astype(F32)


def main_kernel(
    counts, p_hbm, k_hbm, c_hbm, g_hbm, w_hbm, wo_hbm,
    out_own, out_buf, out_got, gq_out, go_out, gain_out,
    x_loc, u_loc, x_all, u_all, normed, wt, wot,
    p_ref, k_ref, c_ref, g_ref, sp_own, sp_got, sp_fwd, rt_fwd,
    box1, val1, box2, val2,
    q_part, m_part, bq, bm, fq, fm,
    a_part, n_part, cbox, ybuf, ysum, ztot, zbox,
    dh, quarters, w_ref, wo_ref, gbox, gval,
    s1s, s1r, s2s, s2r, g1s, g1r,
    sps, spr, rts, rtr,
    sq, sm, rq, rm,
    cs2, cr2, ys2, yr2, zs2, zr2, dxs, dxr, dzs, dzr, qzs, qzr, qys, qyr, wsem, ggs, ggr,
):
    pairs = (
        (p_hbm, p_ref), (k_hbm, k_ref), (c_hbm, c_ref), (g_hbm, g_ref), (w_hbm, w_ref), (wo_hbm, wo_ref)
    )
    loads = [pltpu.make_async_copy(src, dst, wsem.at[i]) for i, (src, dst) in enumerate(pairs)]
    for c in loads:
        c.start()
    place = Place()
    peers = place.peers()
    barrier = pltpu.get_barrier_semaphore()
    for peer in peers:
        pl.semaphore_signal(barrier, inc=1, device_id=peer, device_id_type=MESH)
    width = x_loc.shape[0]
    core, zh = place.core, place.zh
    share = Share(counts, place.dp)
    patch = lax.broadcasted_iota(jnp.int32, (p_ref.shape[2], KEEP), 0)
    for c in loads[:4]:
        c.wait()

    def lanes_of(i):
        return slice(i * KEEP, (i + 1) * KEEP)

    def kept(i):
        pick = (patch == k_ref[i : i + 1, :]).astype(F32).astype(BF16)
        return dot(p_ref[i], pick, 1, 0)

    late = [(kept(i), c_ref[:, lanes_of(i)].astype(F32)) for i in range(SLOTS, 2 * SLOTS)]
    for s in range(SPARE):
        flags = [share.holds(s, i) for i in range(SLOTS, 2 * SLOTS)]
        for a in range(2):
            total = late[0][a] * flags[0]
            for image, flag in zip(late[1:], flags[1:]):
                total = total + image[a] * flag
            sp_own[a, :, lanes_of(s)] = total.astype(BF16)
    pl.semaphore_wait(barrier, len(peers))
    chains = [
        Chain(place, sp_own.at[a], sp_got.at[a], sp_fwd.at[a], sps.at[a], spr.at[a]) for a in range(2)
    ]
    plan = Plan()
    sends = []
    stats_in, q_in, u_in, m_in, heads_in, grads_in, back_in = (Event() for _ in range(7))
    far_in = [Event() for _ in range(5)]
    part = w_ref.shape[2]
    gval[...] = jnp.zeros(gval.shape, F32)
    gval[:1, :width] = g_ref[...]
    gain_row = gval[:1]
    gain_col = jnp.transpose(jnp.broadcast_to(gain_row, (KEEP, KEEP)))[:width, :1]
    keeps = [share.keeps(j) for j in range(SLOTS)]
    works = [[share.works(j, s) for s in range(SPARE)] for j in range(SLOTS)]
    known = {}

    def choose(a, loc, firsts):
        spare = [chains[a].slot(s) for s in range(SPARE)]
        values = []
        for j in range(SLOTS):
            v = firsts[j] * keeps[j]
            for s in range(SPARE):
                v = v + spare[s] * works[j][s]
            loc[:, lanes_of(j)] = v.astype(BF16)
            values.append(v)
        return values

    def small_flow(small, name, event):
        for pace in (2.5, 3.0, 4.5, 3.0):
            yield pace
            known[name] = small.step()
        event.done = True

    def weights_flow():
        for c in loads[4:]:
            c.wait()
        for p in range(3):
            wt[p] = jnp.transpose(w_ref[p])
        wot[...] = jnp.transpose(wo_ref[...])
        yield 0.0

    def rows_flow():
        chains[0].start()
        firsts = [kept(j) for j in range(SLOTS)]
        yield from chains[0].flow()
        values = choose(0, x_loc, firsts)
        me_row = lax.broadcasted_iota(jnp.int32, (16, KEEP), 0) == place.me
        small = SmallSum(place, val1, box1, s1s, s1r, 2 * SLOTS)
        small.start(
            jnp.concatenate(
                [jnp.sum(v, axis=0, keepdims=True) for v in values]
                + [jnp.sum(v * v, axis=0, keepdims=True) for v in values]
                + [jnp.where(me_row, gain_row, 0.0)],
                axis=0,
            )
        )
        plan.add(small_flow(small, "stats", stats_in), 2.5)
        gather = gather_rows(place, x_loc, x_all, g1s.at[0], g1r.at[0], sends)
        pace = next(gather)
        plan.add(weights_flow())
        yield pace
        yield from gather
        yield (stats_in,)
        known["gain_cols"] = gain_cols = jnp.transpose(
            jnp.concatenate([val1[3, 2 * SLOTS :], jnp.zeros((KEEP - 16, KEEP), F32)], axis=0)
        )
        stats = known["stats"]
        known["mean"] = mean = stats[:SLOTS] * (1.0 / D)
        known["inv"] = inv = lax.rsqrt(stats[SLOTS:] * (1.0 / D) - mean * mean + EPSILON)
        for b in range(16):
            rb = slice(b * width, (b + 1) * width)
            col = gain_cols[:width, b : b + 1]
            for j in range(SLOTS):
                here = lanes_of(j)
                centred = (x_all[rb, here].astype(F32) - mean[j : j + 1]) * inv[j : j + 1]
                normed[rb, here] = (centred * col).astype(BF16)
        for p in range(3):
            q_part[p * part : (p + 1) * part] = dot(wt[p], normed[...], 1, 0).astype(BF16)
        yield from q_sum.flow(sends)
        q_in.done = True

    def cotangent_flow():
        chains[1].start()
        firsts = [c_ref[:, lanes_of(j)].astype(F32) for j in range(SLOTS)]
        yield from chains[1].flow()
        choose(1, u_loc, firsts)
        yield from gather_rows(place, u_loc, u_all, g1s.at[1], g1r.at[1], sends)
        u_in.done = True
        m_part[...] = dot(wo_ref[...], u_all[...], 1, 0).astype(BF16)
        yield from m_sum.flow(sends)
        m_in.done = True

    def quarter_flow(a, array):
        yield (u_in, q_in)
        yield from Quarter(
            place, array, quarters.at[a], qzs.at[a], qzr.at[a], qys.at[a], qyr.at[a], sends
        ).flow()
        far_in[3 + a].done = True

    q_sum = ReduceX(place, q_part, bq, fq, sq, rq)
    m_sum = ReduceX(place, m_part, bm, fm, sm, rm)

    def ring_flow(n, slot, start, rows, event, pace):
        yield from RingX(place, dh, slot, start, rows, dxs.at[n], dxr.at[n]).flow(sends, pace)
        event.done = True

    def far_flow(n, r, copy, pace):
        yield pace
        copy.wait_recv()
        yield from ring_flow(1 + r, r, 0, dh.shape[1], far_in[n], 8.0)

    def attend_flow():
        yield (q_in, m_in)
        here = span(place.x * KEEP, KEEP)
        for h in range(part // HD):
            q, k, v, do = [q_sum.total((p * (part // HD) + h) * HD) for p in range(3)] + [m_sum.total(h * HD)]
            out, dq, dk, dv = attend(q, k, v, do)
            for p, value in enumerate((dq, dk, dv, out)):
                r0 = p * part + h * HD
                dh[0, r0 : r0 + HD, here] = value.astype(BF16)
        plan.add(ring_flow(0, 0, 3 * part, part, heads_in, 3.0))
        plan.add(ring_flow(1, 0, 0, 3 * part, grads_in, 4.5))
        copies = [
            remote(dh.at[0, :, here], dh.at[r, :, here], dzs.at[r], dzr.at[r], {"dp": place.dps[r]})
            for r in range(1, 4)
        ]
        yield 0.0
        for n, r in enumerate((1, 3, 2)):
            copies[r - 1].start()
            sends.append(copies[r - 1])
            plan.add(far_flow(n, r, copies[r - 1], (14.0, 16.0, 18.0)[n]))

    feats = normed.shape[0]
    block = 2 * width
    sums = [
        ReduceRows(
            place, array, cbox.at[a], ybuf.at[a], ysum.at[a], ztot.at[a], zbox.at[a],
            (cs2.at[a], cr2.at[a]), (ys2.at[a], yr2.at[a]), (zs2.at[a], zr2.at[a]), sends,
        )
        for a, array in enumerate((a_part, n_part))
    ]
    backs = [
        Chain(place, out_buf.at[a], out_got.at[a], rt_fwd.at[a], rts.at[a], rtr.at[a]) for a in range(2)
    ]

    def give_back(a, results):
        for s in range(SPARE):
            total = results[0] * works[0][s]
            for j in range(1, SLOTS):
                total = total + results[j] * works[j][s]
            out_buf[a, :, lanes_of(s)] = total.astype(BF16)
        backs[a].start()

    def forward_flow():
        yield (heads_in,)
        for b in range(feats // block):
            rb = slice(b * block, (b + 1) * block)
            a_part[rb] = dot(wot[rb], dh[0, 3 * part :], 1, 0).astype(BF16)
        yield from sums[0].flow()
        results = []
        for j in range(SLOTS):
            result = x_loc[:, lanes_of(j)].astype(F32) + sums[0].result(lanes_of(j))
            out_own[0, :, lanes_of(j)] = result.astype(BF16)
            results.append(result)
        give_back(0, results)
        yield from backs[0].flow()

    def backward_flow():
        yield (grads_in,)
        mean, inv, gain_cols = known["mean"], known["inv"], known["gain_cols"]
        hat = [jnp.zeros((8, KEEP), F32) for _ in range(SLOTS)]
        cross = [jnp.zeros((8, KEEP), F32) for _ in range(SLOTS)]
        for b in range(feats // block):
            rb = slice(b * block, (b + 1) * block)
            dn = dot(w_ref[0, rb], dh[0, :part], 1, 0)
            for p in (1, 2):
                dn = dn + dot(w_ref[p, rb], dh[0, p * part : (p + 1) * part], 1, 0)
            n_part[rb] = dn.astype(BF16)
            for i in range(2):
                col = gain_cols[:width, 2 * b + i : 2 * b + i + 1]
                ri = slice(i * width, (i + 1) * width)
                ra = slice((2 * b + i) * width, (2 * b + i + 1) * width)
                for j in range(SLOTS):
                    here = lanes_of(j)
                    d_hat = dn[ri, here] * col
                    centred = (x_all[ra, here].astype(F32) - mean[j : j + 1]) * inv[j : j + 1]
                    hat[j] = hat[j] + jnp.sum(d_hat.reshape(-1, 8, KEEP), axis=0)
                    cross[j] = cross[j] + jnp.sum((d_hat * centred).reshape(-1, 8, KEEP), axis=0)
        small = SmallSum(place, val2, box2, s2s, s2r, 2 * SLOTS)
        small.start(jnp.concatenate([jnp.sum(t, axis=0, keepdims=True) for t in hat + cross], axis=0))
        plan.add(small_flow(small, "back", back_in), 2.5)
        yield from sums[1].flow()
        yield (back_in,)
        back = known["back"]
        mean_hat = back[:SLOTS] * (1.0 / D)
        mean_cross = back[SLOTS:] * (1.0 / D)
        acc = jnp.zeros((width, KEEP), F32)
        results = []
        for j in range(SLOTS):
            here = lanes_of(j)
            total = sums[1].result(here)
            centred = (x_loc[:, here].astype(F32) - mean[j : j + 1]) * inv[j : j + 1]
            acc = acc + total * centred
            result = u_loc[:, here].astype(F32) + inv[j : j + 1] * (
                total * gain_col - mean_hat[j : j + 1] - centred * mean_cross[j : j + 1]
            )
            out_own[1, :, here] = result.astype(BF16)
            results.append(result)
        give_back(1, results)
        row = jnp.sum(
            jnp.transpose(jnp.concatenate([acc, jnp.zeros((KEEP - width, KEEP), F32)], axis=0)),
            axis=0, keepdims=True,
        )
        gval[...] = jnp.broadcast_to(row, gval.shape)
        gains = []
        for k in range(3):
            c = remote(gval, gbox.at[k], ggs.at[k], ggr.at[k], {"dp": place.dps[k + 1]})
            c.start()
            gains.append(c)
        yield from backs[1].flow()
        total = gval[...]
        for k, c in enumerate(gains):
            c.wait()
            total = total + gbox[k]
        gain_out[...] = total

    def weight_gradient_flow():
        yield tuple(far_in) + (heads_in, grads_in)
        quarter = quarters.shape[2]
        for a, arr in enumerate((normed, u_all)):
            quarters[a, 0] = arr[span(place.dp * quarter, quarter)]
        for p in range(3):
            total = dot(quarters[0, 0], dh[0, p * part : (p + 1) * part], 1, 1)
            for r in range(1, 4):
                total = total + dot(quarters[0, r], dh[r, p * part : (p + 1) * part], 1, 1)
            gq_out[p] = total
        total = dot(dh[0, 3 * part :], quarters[1, 0], 1, 1)
        for r in range(1, 4):
            total = total + dot(dh[r, 3 * part :], quarters[1, r], 1, 1)
        go_out[...] = total

    plan.add(rows_flow())
    plan.add(cotangent_flow(), 3.0)
    for a, array in enumerate((normed, u_all)):
        plan.add(quarter_flow(a, array))
    plan.add(attend_flow())
    plan.add(forward_flow())
    plan.add(backward_flow())
    plan.add(weight_gradient_flow())
    plan.run()
    for c in sends:
        c.wait_send()
    for chain in chains + backs:
        chain.drain()


def post_kernel(
    n, counts, k_hbm, own_hbm, buf_hbm, got_hbm, gg_hbm, gq_hbm, go_hbm,
    out, dp_out, gain_out, gq_out, go_out, k_ref, own_ref, buf_ref, got_ref, gg_ref, sem, osem,
):
    through = [
        pltpu.make_async_copy(src, dst, osem.at[i])
        for i, (src, dst) in enumerate(((gq_hbm, gq_out), (go_hbm, go_out)))
    ]
    for c in through:
        c.start()
    load(
        ((k_hbm, k_ref), (own_hbm, own_ref), (buf_hbm, buf_ref), (got_hbm, got_ref), (gg_hbm, gg_ref)), sem
    )
    dp = lax.axis_index("dp")
    share = Share(counts, dp)
    patch = lax.broadcasted_iota(jnp.int32, (dp_out.shape[2], KEEP), 0)
    for i in range(n):
        lanes = slice(i * KEEP, (i + 1) * KEEP)
        if i < SLOTS:
            res, d_in = (own_ref[a, :, lanes].astype(F32) * share.keeps(i) for a in range(2))
        else:
            slot = clamp(share.spare_at + i - SLOTS, SPARE - 1)
            flag = jnp.where(i - SLOTS < share.extra, 1.0, 0.0)
            here = span(slot * KEEP, KEEP)
            res, d_in = (
                (
                    buf_ref[a, :, here].astype(F32)
                    + got_ref[a, 0, :, here].astype(F32)
                    + got_ref[a, 1, :, here].astype(F32)
                )
                * flag
                for a in range(2)
            )
        pick = (patch == k_ref[i : i + 1, :]).astype(F32).astype(BF16)
        out[:, lanes] = res.astype(BF16)
        dp_out[i] = dot(d_in.astype(BF16), pick, 1, 1).astype(BF16)
    part = gain_out.shape[1]
    for g in range(4):
        @pl.when(dp == g)
        def _():
            gain_out[...] = gg_ref[:1, g * part : (g + 1) * part]
    for c in through:
        c.wait()


def sharded(patches, keep_index, counts, gain, w_qkv, w_out, cotangent):
    n, patch_count, width = patches.shape
    total_rows = n * KEEP
    rows = SLOTS * KEEP
    feats = w_qkv.shape[0]
    heads = w_out.shape[0]
    heads3 = 3 * heads
    quarter = feats // 4
    gain_row = gain[None]
    spare = SPARE * KEEP
    small = 2 * SLOTS + 16
    blk = (2, width, rows)

    def v(shape, dtype=BF16):
        return pltpu.VMEM(shape, dtype)

    scratch = [
        v((width, rows)), v((width, rows)), v((feats, rows)), v((feats, rows)), v((feats, rows)),
        v((3, heads, feats)), v((feats, heads)),
        v((n, width, patch_count)), v((n, KEEP), jnp.int32), v((width, total_rows)), v((1, width), F32),
        v((2, width, spare)), v((2, 2, width, spare)), v((2, 2, width, spare)), v((2, 2, width, spare)),
        v((8, small, KEEP), F32), v((4, small, KEEP), F32),
        v((8, 2 * SLOTS, KEEP), F32), v((4, 2 * SLOTS, KEEP), F32),
        v((heads3, rows)), v((heads, rows)),
        v((6, heads3 // 2, KEEP)), v((6, heads // 2, KEEP)), v((2, heads3 // 2, KEEP)), v((2, heads // 2, KEEP)),
        v((feats, rows)), v((feats, rows)), v((2, 4) + blk), v((2, 4) + blk),
        v((2,) + blk, F32), v((2, width, rows)), v((2, width, rows)),
        v((4, heads3 + heads, rows)), v((2, 4, quarter, rows)), v((3, feats, heads)), v((heads, feats)),
        v((3, 8, KEEP), F32), v((8, KEEP), F32),
        DMA((8,)), DMA((8,)), DMA((8,)), DMA((8,)),
        DMA((2, 20)), DMA((2, 16, 2)),
        DMA((2, 2, CHUNKS)), DMA((2, 2, CHUNKS)), DMA((2, 2, CHUNKS)), DMA((2, 2, CHUNKS)),
        DMA((6,)), DMA((6,)), DMA((6,)), DMA((6,)),
        DMA((2, 4, 2)), DMA((2, 4, 2)), DMA((2, 6)), DMA((2, 6)), DMA((2,)), DMA((2,)),
        DMA((5, 2, 3)), DMA((5, 2, 4)), DMA((4,)), DMA((4,)), DMA((2, 4)), DMA((2, 4)),
        DMA((2, 8)), DMA((2, 8, 2)), DMA((6,)), DMA((3,)), DMA((3,)),
    ]
    shape = jax.ShapeDtypeStruct
    out_own, out_buf, out_got, gq, go, gg = pl.pallas_call(
        main_kernel,
        out_shape=[
            shape((2, width, rows), BF16), shape((2, width, spare), BF16),
            shape((2, 2, width, spare), BF16),
            shape((3, quarter, heads), F32), shape((heads, quarter), F32),
            shape((8, KEEP), F32),
        ],
        in_specs=[SM] + [ANY] * 6,
        out_specs=[VM] * 6,
        scratch_shapes=scratch,
        compiler_params=pltpu.CompilerParams(
            vmem_limit_bytes=58 * 1024 * 1024, collective_id=1, has_side_effects=True
        ),
    )(
        counts, jnp.transpose(patches, (0, 2, 1)), keep_index, cotangent.T, gain_row,
        jnp.transpose(w_qkv, (1, 0, 2)), w_out,
    )
    part = width // 4
    outputs, d_patches, grad_gain, gq, go = pl.pallas_call(
        partial(post_kernel, n),
        out_shape=[
            shape((width, total_rows), BF16), shape((n, width, patch_count), BF16), shape((1, part), F32),
            shape(gq.shape, F32), shape(go.shape, F32),
        ],
        in_specs=[SM] + [ANY] * 7,
        out_specs=[VM] * 5,
        scratch_shapes=[
            v((n, KEEP), jnp.int32), v((2, width, rows)), v((2, width, spare)), v((2, 2, width, spare)),
            v((8, KEEP), F32), DMA((5,)), DMA((2,)),
        ],
        compiler_params=pltpu.CompilerParams(vmem_limit_bytes=58 * 1024 * 1024),
    )(counts, keep_index, out_own, out_buf, out_got, gg, gq, go)
    return (
        outputs.T, jnp.transpose(d_patches, (0, 2, 1)), jnp.transpose(gq, (1, 0, 2)), go,
        grad_gain.reshape(part),
    )


def solution(mesh):
    placed = (
        P("dp", None, ("mcol", "mrow")),
        P("dp", None),
        P(),
        P(("mcol", "mrow")),
        P("mcol", None, "mrow"),
        P("mrow", "mcol"),
        P("dp", ("mcol", "mrow")),
    )
    return jax.shard_map(
        sharded,
        mesh=mesh,
        in_specs=placed,
        out_specs=(
            P("dp", ("mcol", "mrow")),
            P("dp", None, ("mcol", "mrow")),
            P(("mcol", "dp"), None, "mrow"),
            P("mrow", ("mcol", "dp")),
            P(("mcol", "mrow", "dp")),
        ),
        check_vma=False,
    )
```

time: 191 us -> 125 us (0.65)
  Pallas kernels: 188 us -> 123 us
    pallas_call x1, Pallas kernels: 50.3 us -> 4.08 us  [sharded(): pl.pallas_call(partial(post_kernel, n), out_shape=[shape((width, total_ro...]
    pallas_call x1, Pallas kernels: 138 us -> 119 us  [sharded(): pl.pallas_call(main_kernel, out_shape=[shape((2, width, rows), BF16), sha...]
where the time goes in v5:
time: 125 us; the launch traced here: 124 us
  Pallas kernels  123 us (98%)
    pallas_call x1, Pallas kernels, sharded(): pl.pallas_call(main_kernel, out_shape=[shape((2, width, rows), BF16), sha...  119 us
    pallas_call x1, Pallas kernels, sharded(): pl.pallas_call(partial(post_kernel, n), out_shape=[shape((width, total_ro...  4.08 us

profile of v5, /device:TPU:0, one launch (start us, length us, event | category | flops | bytes accessed | tf_op | source)
XLA Modules:
  0.0 123.6 jit_solution(2309635369868929208)
XLA Ops:
  0.6 118.8 %shard_map.110 = (bf16[2,96,512]{2,1,0:T(8,128)(2,1)}, bf16[2,96,768]{2,1,0:T(8,128)(2,1)}, bf16[2,2,96,768]{3,2,1,0:T(8,128)(2,1)}, f32[3,384,256]{2,1,0:T(8,12...) custom-call(s32[4]{0:T(128)} %counts.3, bf16[8,96,256]{2,1,0:T(8,128)(2,1)} %bitcast.9, s32[8,128]{1,0:T(8,128)} %k_hbm.3, ...), custom_call_target="tpu_custom_call" | custom-call | tf_op jit(solution)/shard_map/pallas_call | solution.py:968
  119.5 4.1 %shard_map.111 = (bf16[96,1024]{1,0:T(8,128)(2,1)}, bf16[8,96,256]{2,1,0:T(8,128)(2,1)}, f32[1,24]{1,0:T(1,128)}, f32[3,384,256]{2,1,0:T(8,128)}, f32[256,384]{1,0:T(8,128)}) custom-call(s32[4]{0:T(128)} %counts.3, s32[8,128]{1,0:T(8,128)} %k_hbm.3, bf16[2,96,512]{2,1,0:T(8,128)(2,1)} %get-tuple-element.16.own_hbm, ...), custom_call_target="tpu_custom_call" | custom-call | tf_op jit(solution)/shard_map/pallas_call | solution.py:987

commit v6 on v5

--- a/solution.py
+++ b/solution.py
@@ -13,7 +13,8 @@
 KEEP = 128
 SLOTS = 4
 SPARE = 6
-CHUNKS = 3
+CHUNKS = 2
+DIRECT = (True, False)
 EPSILON = 1e-06
 
 F32 = jnp.float32
@@ -221,7 +222,7 @@
 
     def flow(self):
         for way, ch, after in (
-            (0, 0, 3.5), (0, 1, 1.0), (1, 0, 2.5), (0, 2, 0.0), (1, 1, 1.0), (1, 2, 1.0)
+            (0, 0, 3.5), (0, 1, 1.0), (1, 0, 2.5), (1, 1, 1.5)
         ):
             yield after
             for dp, w in ((1, way), (2, 1 - way)):
@@ -281,11 +282,11 @@
     return out, dq, dk, dv
 
 
-def gather_rows(place, loc, out, send, recv, sends):
+def gather_rows(place, loc, out, send, recv, sends, direct):
     width, rows = loc.shape
     half = rows // 2
     me, sib, core = place.me, {"mrow": place.sib}, place.core
-    right, left = {"mrow": place.ys[1]}, {"mrow": place.ys[3]}
+    right, left, across = ({"mrow": place.ys[d]} for d in (1, 3, 2))
     count = [0]
 
     def view(slot, part=None):
@@ -308,22 +309,29 @@
     push(me, {"mrow": place.anti}, src=loc)
     push(me, right, src=loc)
     push(me, left, src=loc)
+    if direct:
+        push(me, across, src=loc)
     push(me, sib, src=loc)
     out[span(me * width, width)] = loc[...]
 
     def ring(zh):
         before, after = place.at(zh, 3, core), place.at(zh, 1, core)
         got(before)
-        push(before, right, 0)
+        if not direct:
+            push(before, right, 0)
         got(after)
-        push(after, left, 1)
+        if not direct:
+            push(after, left, 1)
         push(before, sib)
         push(after, sib)
 
     def far(zh):
         slot = place.at(zh, 2, core)
-        got(slot, 0)
-        got(slot, 1)
+        if direct:
+            got(slot)
+        else:
+            got(slot, 0)
+            got(slot, 1)
         push(slot, sib)
 
     yield 4.0
@@ -332,12 +340,14 @@
     got(place.anti)
     push(place.anti, right)
     push(place.anti, left)
+    if direct:
+        push(place.anti, across)
     push(place.anti, sib)
     yield 0.5
     far(place.zh)
     yield 4.0
     ring(1 - place.zh)
-    yield 4.0
+    yield 1.5 if direct else 4.0
     far(1 - place.zh)
     yield 2.0
     for zh in range(2):
@@ -632,6 +642,7 @@
     plan = Plan()
     sends = []
     stats_in, q_in, u_in, m_in, heads_in, grads_in, back_in = (Event() for _ in range(7))
+    normed_in = Event()
     far_in = [Event() for _ in range(5)]
     part = w_ref.shape[2]
     gval[...] = jnp.zeros(gval.shape, F32)
@@ -683,7 +694,7 @@
             )
         )
         plan.add(small_flow(small, "stats", stats_in), 2.5)
-        gather = gather_rows(place, x_loc, x_all, g1s.at[0], g1r.at[0], sends)
+        gather = gather_rows(place, x_loc, x_all, g1s.at[0], g1r.at[0], sends, DIRECT[0])
         pace = next(gather)
         plan.add(weights_flow())
         yield pace
@@ -702,6 +713,7 @@
                 here = lanes_of(j)
                 centred = (x_all[rb, here].astype(F32) - mean[j : j + 1]) * inv[j : j + 1]
                 normed[rb, here] = (centred * col).astype(BF16)
+        normed_in.done = True
         for p in range(3):
             q_part[p * part : (p + 1) * part] = dot(wt[p], normed[...], 1, 0).astype(BF16)
         yield from q_sum.flow(sends)
@@ -712,14 +724,14 @@
         firsts = [c_ref[:, lanes_of(j)].astype(F32) for j in range(SLOTS)]
         yield from chains[1].flow()
         choose(1, u_loc, firsts)
-        yield from gather_rows(place, u_loc, u_all, g1s.at[1], g1r.at[1], sends)
+        yield from gather_rows(place, u_loc, u_all, g1s.at[1], g1r.at[1], sends, DIRECT[1])
         u_in.done = True
         m_part[...] = dot(wo_ref[...], u_all[...], 1, 0).astype(BF16)
         yield from m_sum.flow(sends)
         m_in.done = True
 
     def quarter_flow(a, array):
-        yield (u_in, q_in)
+        yield ((normed_in, u_in)[a],)
         yield from Quarter(
             place, array, quarters.at[a], qzs.at[a], qzr.at[a], qys.at[a], qyr.at[a], sends
         ).flow()

time: 125 us -> 117 us (0.936)
  Pallas kernels: 123 us -> 115 us
    pallas_call x1, Pallas kernels: 119 us -> 111 us  [sharded(): pl.pallas_call(main_kernel, out_shape=[shape((2, width, rows), BF16), sha...]
where the time goes in v6:
time: 117 us; the launch traced here: 116 us
  Pallas kernels  115 us (98%)
    pallas_call x1, Pallas kernels, sharded(): pl.pallas_call(main_kernel, out_shape=[shape((2, width, rows), BF16), sha...  111 us
    pallas_call x1, Pallas kernels, sharded(): pl.pallas_call(partial(post_kernel, n), out_shape=[shape((width, total_ro...  4.08 us

profile of v6, /device:TPU:0, one launch (start us, length us, event | category | flops | bytes accessed | tf_op | source)
XLA Modules:
  0.0 115.9 jit_solution(14307266459718780289)
XLA Ops:
  0.6 111.2 %shard_map.110 = (bf16[2,96,512]{2,1,0:T(8,128)(2,1)}, bf16[2,96,768]{2,1,0:T(8,128)(2,1)}, bf16[2,2,96,768]{3,2,1,0:T(8,128)(2,1)}, f32[3,384,256]{2,1,0:T(8,12...) custom-call(s32[4]{0:T(128)} %counts.3, bf16[8,96,256]{2,1,0:T(8,128)(2,1)} %bitcast.9, s32[8,128]{1,0:T(8,128)} %k_hbm.3, ...), custom_call_target="tpu_custom_call" | custom-call | tf_op jit(solution)/shard_map/pallas_call | solution.py:980
  111.8 4.1 %shard_map.111 = (bf16[96,1024]{1,0:T(8,128)(2,1)}, bf16[8,96,256]{2,1,0:T(8,128)(2,1)}, f32[1,24]{1,0:T(1,128)}, f32[3,384,256]{2,1,0:T(8,128)}, f32[256,384]{1,0:T(8,128)}) custom-call(s32[4]{0:T(128)} %counts.3, s32[8,128]{1,0:T(8,128)} %k_hbm.3, bf16[2,96,512]{2,1,0:T(8,128)(2,1)} %get-tuple-element.16.own_hbm, ...), custom_call_target="tpu_custom_call" | custom-call | tf_op jit(solution)/shard_map/pallas_call | solution.py:999

commit v7 on v6

--- a/solution.py
+++ b/solution.py
@@ -14,7 +14,7 @@
 SLOTS = 4
 SPARE = 6
 CHUNKS = 2
-DIRECT = (True, False)
+DIRECT = (True, True)
 EPSILON = 1e-06
 
 F32 = jnp.float32
@@ -207,9 +207,7 @@
     def forward(self, way, ch):
         self.copy(way, ch, False).wait_recv()
         here = self.lanes(ch)
-        self.fwd[way, :, here] = (
-            self.got[way, :, here].astype(F32) + self.own[:, here].astype(F32)
-        ).astype(BF16)
+        self.fwd[way, :, here] = self.got[way, :, here] + self.own[:, here]
         self.copy(way, ch, False).start()
 
     def start(self):
@@ -382,7 +380,7 @@
         yield 4.0
         for p, (at, where) in enumerate(((xs[1], right), (xs[3], left))):
             self.got(p)
-            self.fwd[p] = (self.buf[p].astype(F32) + self.view(p, at)[...].astype(F32)).astype(BF16)
+            self.fwd[p] = self.buf[p] + self.view(p, at)[...]
             self.push(self.fwd.at[p], 4 + p, where, sends)
         yield 4.0
         for slot in range(2, 6):
@@ -513,13 +511,10 @@
 
     def add(self, d, srcs, lanes=slice(None)):
         for z in range(2):
-            @pl.loop(0, self.width // 16)
-            def _(i):
-                r = span(i * 16, 16)
-                total = self.cbox[d, z, r, lanes].astype(F32)
-                for s in srcs:
-                    total = total + s[z][r, lanes].astype(F32)
-                self.cbox[d, z, r, lanes] = total.astype(BF16)
+            total = self.cbox[d, z, :, lanes]
+            for s in srcs:
+                total = total + s[z][:, lanes]
+            self.cbox[d, z, :, lanes] = total
 
     def core_sum(self, d):
         for z in range(2):
@@ -567,16 +562,11 @@
         for slot, lanes, k in ((2, hi, 3), (3, lo, 4), (2, lo, 2), (3, hi, 5)):
             self.ygot(slot, lanes, k)
 
-        @pl.loop(0, self.width // 16)
-        def _(i):
-            r = span(i * 16, 16)
-            for z in range(2):
-                self.ysum[z, r] = (
-                    self.cbox[0, z, r].astype(F32)
-                    + self.ybuf[2, z, r].astype(F32)
-                    + self.ybuf[3, z, r].astype(F32)
-                )
-            self.ztot[r] = self.ysum[1 - place.zh, r].astype(BF16)
+        for z in range(2):
+            self.ysum[z] = (
+                self.cbox[0, z].astype(F32) + self.ybuf[2, z].astype(F32) + self.ybuf[3, z].astype(F32)
+            )
+        self.ztot[...] = self.ysum[1 - place.zh].astype(BF16)
 
         c = remote(self.ztot, self.zbox, self.zsem[0], self.zsem[1], {"mrow": place.anti})
         c.start()
@@ -590,9 +580,9 @@
 
 def main_kernel(
     counts, p_hbm, k_hbm, c_hbm, g_hbm, w_hbm, wo_hbm,
-    out_own, out_buf, out_got, gq_out, go_out, gain_out,
+    out_own, out_sum, gq_out, go_out, gain_out,
     x_loc, u_loc, x_all, u_all, normed, wt, wot,
-    p_ref, k_ref, c_ref, g_ref, sp_own, sp_got, sp_fwd, rt_fwd,
+    p_ref, k_ref, c_ref, g_ref, sp_own, sp_got, sp_fwd, out_buf, out_got, rt_fwd,
     box1, val1, box2, val2,
     q_part, m_part, bq, bm, fq, fm,
     a_part, n_part, cbox, ybuf, ysum, ztot, zbox,
@@ -747,7 +737,7 @@
     def far_flow(n, r, copy, pace):
         yield pace
         copy.wait_recv()
-        yield from ring_flow(1 + r, r, 0, dh.shape[1], far_in[n], 8.0)
+        yield from ring_flow(1 + r, r, 0, dh.shape[1], far_in[n], 10.0)
 
     def attend_flow():
         yield (q_in, m_in)
@@ -804,6 +794,7 @@
             results.append(result)
         give_back(0, results)
         yield from backs[0].flow()
+        out_sum[0] = out_buf[0] + out_got[0, 0] + out_got[0, 1]
 
     def backward_flow():
         yield (grads_in,)
@@ -858,6 +849,7 @@
             c.start()
             gains.append(c)
         yield from backs[1].flow()
+        out_sum[1] = out_buf[1] + out_got[1, 0] + out_got[1, 1]
         total = gval[...]
         for k, c in enumerate(gains):
             c.wait()
@@ -895,8 +887,8 @@
 
 
 def post_kernel(
-    n, counts, k_hbm, own_hbm, buf_hbm, got_hbm, gg_hbm, gq_hbm, go_hbm,
-    out, dp_out, gain_out, gq_out, go_out, k_ref, own_ref, buf_ref, got_ref, gg_ref, sem, osem,
+    n, counts, k_hbm, own_hbm, sum_hbm, gg_hbm, gq_hbm, go_hbm,
+    out, dp_out, gain_out, gq_out, go_out, k_ref, own_ref, sum_ref, gg_ref, sem, osem,
 ):
     through = [
         pltpu.make_async_copy(src, dst, osem.at[i])
@@ -905,7 +897,7 @@
     for c in through:
         c.start()
     load(
-        ((k_hbm, k_ref), (own_hbm, own_ref), (buf_hbm, buf_ref), (got_hbm, got_ref), (gg_hbm, gg_ref)), sem
+        ((k_hbm, k_ref), (own_hbm, own_ref), (sum_hbm, sum_ref), (gg_hbm, gg_ref)), sem
     )
     dp = lax.axis_index("dp")
     share = Share(counts, dp)
@@ -918,15 +910,7 @@
             slot = clamp(share.spare_at + i - SLOTS, SPARE - 1)
             flag = jnp.where(i - SLOTS < share.extra, 1.0, 0.0)
             here = span(slot * KEEP, KEEP)
-            res, d_in = (
-                (
-                    buf_ref[a, :, here].astype(F32)
-                    + got_ref[a, 0, :, here].astype(F32)
-                    + got_ref[a, 1, :, here].astype(F32)
-                )
-                * flag
-                for a in range(2)
-            )
+            res, d_in = (sum_ref[a, :, here].astype(F32) * flag for a in range(2))
         pick = (patch == k_ref[i : i + 1, :]).astype(F32).astype(BF16)
         out[:, lanes] = res.astype(BF16)
         dp_out[i] = dot(d_in.astype(BF16), pick, 1, 1).astype(BF16)
@@ -959,7 +943,8 @@
         v((width, rows)), v((width, rows)), v((feats, rows)), v((feats, rows)), v((feats, rows)),
         v((3, heads, feats)), v((feats, heads)),
         v((n, width, patch_count)), v((n, KEEP), jnp.int32), v((width, total_rows)), v((1, width), F32),
-        v((2, width, spare)), v((2, 2, width, spare)), v((2, 2, width, spare)), v((2, 2, width, spare)),
+        v((2, width, spare)), v((2, 2, width, spare)), v((2, 2, width, spare)),
+        v((2, width, spare)), v((2, 2, width, spare)), v((2, 2, width, spare)),
         v((8, small, KEEP), F32), v((4, small, KEEP), F32),
         v((8, 2 * SLOTS, KEEP), F32), v((4, 2 * SLOTS, KEEP), F32),
         v((heads3, rows)), v((heads, rows)),
@@ -977,16 +962,15 @@
         DMA((2, 8)), DMA((2, 8, 2)), DMA((6,)), DMA((3,)), DMA((3,)),
     ]
     shape = jax.ShapeDtypeStruct
-    out_own, out_buf, out_got, gq, go, gg = pl.pallas_call(
+    out_own, out_sum, gq, go, gg = pl.pallas_call(
         main_kernel,
         out_shape=[
             shape((2, width, rows), BF16), shape((2, width, spare), BF16),
-            shape((2, 2, width, spare), BF16),
             shape((3, quarter, heads), F32), shape((heads, quarter), F32),
             shape((8, KEEP), F32),
         ],
         in_specs=[SM] + [ANY] * 6,
-        out_specs=[VM] * 6,
+        out_specs=[VM] * 5,
         scratch_shapes=scratch,
         compiler_params=pltpu.CompilerParams(
             vmem_limit_bytes=58 * 1024 * 1024, collective_id=1, has_side_effects=True
@@ -1002,14 +986,14 @@
             shape((width, total_rows), BF16), shape((n, width, patch_count), BF16), shape((1, part), F32),
             shape(gq.shape, F32), shape(go.shape, F32),
         ],
-        in_specs=[SM] + [ANY] * 7,
+        in_specs=[SM] + [ANY] * 6,
         out_specs=[VM] * 5,
         scratch_shapes=[
-            v((n, KEEP), jnp.int32), v((2, width, rows)), v((2, width, spare)), v((2, 2, width, spare)),
-            v((8, KEEP), F32), DMA((5,)), DMA((2,)),
+            v((n, KEEP), jnp.int32), v((2, width, rows)), v((2, width, spare)), v((8, KEEP), F32),
+            DMA((4,)), DMA((2,)),
         ],
         compiler_params=pltpu.CompilerParams(vmem_limit_bytes=58 * 1024 * 1024),
-    )(counts, keep_index, out_own, out_buf, out_got, gg, gq, go)
+    )(counts, keep_index, out_own, out_sum, gg, gq, go)
     return (
         outputs.T, jnp.transpose(d_patches, (0, 2, 1)), jnp.transpose(gq, (1, 0, 2)), go,
         grad_gain.reshape(part),

time: 117 us -> 115 us (0.983)
  Pallas kernels: 115 us -> 113 us
    pallas_call x1, Pallas kernels: 111 us -> 109 us  [sharded(): pl.pallas_call(main_kernel, out_shape=[shape((2, width, rows), BF16), sha...]
where the time goes in v7:
time: 115 us; the launch traced here: 114 us
  Pallas kernels  113 us (98%)
    pallas_call x1, Pallas kernels, sharded(): pl.pallas_call(main_kernel, out_shape=[shape((2, width, rows), BF16), sha...  109 us
    pallas_call x1, Pallas kernels, sharded(): pl.pallas_call(partial(post_kernel, n), out_shape=[shape((width, total_ro...  3.84 us

profile of v7, /device:TPU:0, one launch (start us, length us, event | category | flops | bytes accessed | tf_op | source)
XLA Modules:
  0.0 113.5 jit_solution(5340557845709415823)
XLA Ops:
  0.6 108.9 %shard_map.110 = (bf16[2,96,512]{2,1,0:T(8,128)(2,1)}, bf16[2,96,768]{2,1,0:T(8,128)(2,1)}, f32[3,384,256]{2,1,0:T(8,128)}, f32[256,384]{1,0:T(8,128)}, f32[8,128]{1,0:T(8,128)}) custom-call(s32[4]{0:T(128)} %counts.3, bf16[8,96,256]{2,1,0:T(8,128)(2,1)} %bitcast.9, s32[8,128]{1,0:T(8,128)} %k_hbm.3, bf16[96,1024]{1,0:T(8,128)(2,1)} %bitcast.10, ...), custom_call_target="tpu_custom_call" | custom-call | tf_op jit(solution)/shard_map/pallas_call | solution.py:965
  109.5 3.8 %shard_map.111 = (bf16[96,1024]{1,0:T(8,128)(2,1)}, bf16[8,96,256]{2,1,0:T(8,128)(2,1)}, f32[1,24]{1,0:T(1,128)}, f32[3,384,256]{2,1,0:T(8,128)}, f32[256,384]{1,0:T(8,128)}) custom-call(s32[4]{0:T(128)} %counts.3, s32[8,128]{1,0:T(8,128)} %k_hbm.3, bf16[2,96,512]{2,1,0:T(8,128)(2,1)} %get-tuple-element.15.own_hbm, ...), custom_call_target="tpu_custom_call" | custom-call | tf_op jit(solution)/shard_map/pallas_call | solution.py:983

commit v8 on v7

--- a/solution.py
+++ b/solution.py
@@ -758,7 +758,7 @@
         for n, r in enumerate((1, 3, 2)):
             copies[r - 1].start()
             sends.append(copies[r - 1])
-            plan.add(far_flow(n, r, copies[r - 1], (14.0, 16.0, 18.0)[n]))
+            plan.add(far_flow(n, r, copies[r - 1], (13.0, 15.0, 17.0)[n]))
 
     feats = normed.shape[0]
     block = 2 * width

time: 115 us -> 115 us (level)
  no operation moved by 1% of the time
where the time goes in v8:
time: 115 us; the launch traced here: 113 us
  Pallas kernels  113 us (98%)
    pallas_call x1, Pallas kernels, sharded(): pl.pallas_call(main_kernel, out_shape=[shape((2, width, rows), BF16), sha...  109 us
    pallas_call x1, Pallas kernels, sharded(): pl.pallas_call(partial(post_kernel, n), out_shape=[shape((width, total_ro...  3.84 us

profile of v8, /device:TPU:0, one launch (start us, length us, event | category | flops | bytes accessed | tf_op | source)
XLA Modules:
  0.0 113.4 jit_solution(14434076653441359470)
XLA Ops:
  0.6 108.8 %shard_map.110 = (bf16[2,96,512]{2,1,0:T(8,128)(2,1)}, bf16[2,96,768]{2,1,0:T(8,128)(2,1)}, f32[3,384,256]{2,1,0:T(8,128)}, f32[256,384]{1,0:T(8,128)}, f32[8,128]{1,0:T(8,128)}) custom-call(s32[4]{0:T(128)} %counts.3, bf16[8,96,256]{2,1,0:T(8,128)(2,1)} %bitcast.9, s32[8,128]{1,0:T(8,128)} %k_hbm.3, bf16[96,1024]{1,0:T(8,128)(2,1)} %bitcast.10, ...), custom_call_target="tpu_custom_call" | custom-call | tf_op jit(solution)/shard_map/pallas_call | solution.py:965
  109.4 3.8 %shard_map.111 = (bf16[96,1024]{1,0:T(8,128)(2,1)}, bf16[8,96,256]{2,1,0:T(8,128)(2,1)}, f32[1,24]{1,0:T(1,128)}, f32[3,384,256]{2,1,0:T(8,128)}, f32[256,384]{1,0:T(8,128)}) custom-call(s32[4]{0:T(128)} %counts.3, s32[8,128]{1,0:T(8,128)} %k_hbm.3, bf16[2,96,512]{2,1,0:T(8,128)(2,1)} %get-tuple-element.15.own_hbm, ...), custom_call_target="tpu_custom_call" | custom-call | tf_op jit(solution)/shard_map/pallas_call | solution.py:983
